TPU v7x, 32 devices: a whole 2x2x4 slice. The times are simulated.
32 devices in a mesh: dp: 4 (over y, x), vocab: 8 (over z, core).
Axes of the slice: x: 2, y: 2, z: 4, core: 2. Of those that a mesh axis runs over, the one named last changes fastest.
Arguments:
- master_tiles: float32 [2816, 64, 64], P(('dp', 'vocab')), may hold values from -0.25 to 0.25
- mom1_tiles: float32 [2816, 64, 64], P(('dp', 'vocab')), may hold values from -5.722046e-06 to 5.722046e-06
- mom2_tiles: float32 [2816, 64, 64], P(('dp', 'vocab')), may hold values from 3.7079958e-13 to 5.9327933e-12
- stat_left: float32 [2816, 64, 64], P(('dp', 'vocab')), as said below
- stat_right: float32 [2816, 64, 64], P(('dp', 'vocab')), as said below
- basis_left: float32 [2816, 64, 64], P(('dp', 'vocab')), as said below
- basis_right: float32 [2816, 64, 64], P(('dp', 'vocab')), as said below
- table_master: float32 [32768, 512], P('vocab')
- table_mom1: float32 [32768, 512], P('vocab'), may hold values from -5.722046e-06 to 5.722046e-06
- table_mom2: float32 [32768, 512], P('vocab'), may hold values from 3.7079958e-13 to 5.9327933e-12
- gains: float32 [11, 512], replicated, may hold values from 0.5 to 1.5
- gain_mom1: float32 [11, 512], replicated, may hold values from -2.2888184e-05 to 2.2888184e-05
- gain_mom2: float32 [11, 512], replicated, may hold values from 5.9327933e-12 to 9.5348465e-11
- source_ids: int32 [2, 32, 1024], P(None, ('dp', 'vocab')), may hold values from 0 to 32767
- target_ids: int32 [2, 32, 256], P(None, ('dp', 'vocab')), may hold values from 0 to 32767
- source_len: int32 [2, 32], P(None, ('dp', 'vocab')), may hold values from 1 to 1024, as said below
- target_len: int32 [2, 32], P(None, ('dp', 'vocab')), may hold values from 1 to 256, as said below
- loss_place: int32 [2, 32, 16], P(None, ('dp', 'vocab')), may hold values from 0 to 255
- exit_layer: int32 [2, 32, 16], P(None, ('dp', 'vocab')), may hold values from 0 to 1
- slot_list: int32 [2816], replicated, may hold values from 0 to 2815, each once
Outputs:
- loss_sum: float32 [], replicated
- loss_count: float32 [], replicated
- grad_norm: float32 [], replicated
- master_new: float32 [2816, 64, 64], P(('dp', 'vocab'))
- master_low: bfloat16 [2816, 64, 64], P(('dp', 'vocab'))
- mom1_new: float32 [2816, 64, 64], P(('dp', 'vocab'))
- mom2_new: float32 [2816, 64, 64], P(('dp', 'vocab'))
- stat_left_new: float32 [2816, 64, 64], P(('dp', 'vocab'))
- stat_right_new: float32 [2816, 64, 64], P(('dp', 'vocab'))
- basis_left_new: float32 [2816, 64, 64], P(('dp', 'vocab'))
- basis_right_new: float32 [2816, 64, 64], P(('dp', 'vocab'))
- table_new: float32 [32768, 512], P('vocab')
- table_low: bfloat16 [32768, 512], P('vocab')
- table_mom1_new: float32 [32768, 512], P('vocab')
- table_mom2_new: float32 [32768, 512], P('vocab')
- gains_new: float32 [11, 512], replicated
- gain_mom1_new: float32 [11, 512], replicated
- gain_mom2_new: float32 [11, 512], replicated
Inputs may be any that keep to these rules, and one draw needn't show every extreme that they name: `stat_left`: each block is symmetric positive definite. `stat_right`: each block is symmetric positive definite. `basis_left`: each block is orthogonal. `basis_right`: each block is orthogonal. `source_len`: some sequence has source length 1024. `target_len`: some sequence has target length 256.
All inputs are finite; a program needn't handle non-finite values.
Results may differ from a plain program's by a relative error of at most 0.0056.
Values may be sent and summed in bfloat16 or wider, within the bound.
No kernel may reach another device: no remote copies, remote signals or barrier semaphores. Data moves between devices by JAX's collectives and lax.ppermute only.
A program may use at most 768 MiB of HBM per device.

v0:
```python
import math

import jax
import jax.numpy as jnp
from jax import lax
from jax.sharding import PartitionSpec as P

D = 512
HEADS = 8
HEAD_DIM = 64
FF = 2048
ENC = 1
DEC = 2
MICRO = 2
LOSS_POS = 16
PB = 64
STEP = 10
MATS = 11
GAINS = 11


HIGHEST = lax.Precision.HIGHEST
NORM_EPS = 1e-06
CLIP_AT = 0.02
RATE_MATRIX = 0.1
RATE_VECTOR = 0.8
BETA_FIRST = 0.9
BETA_SECOND = 0.95
BETA_STAT = 0.95
ADAM_EPS = 1e-08
DECAY = 0.01


def rms_norm(stream, gain_row):
    return (
        stream * lax.rsqrt(jnp.mean(stream * stream, axis=-1, keepdims=True) + NORM_EPS) * gain_row
    )


def waves(length, columns):
    place_at = jnp.arange(length).astype(jnp.float32)[:, None]
    rate_at = jnp.exp(
        jnp.arange(columns // 2).astype(jnp.float32) * (-2.0 * math.log(10000.0) / columns)
    )
    angle = place_at * rate_at[None, :]
    return jnp.concatenate([jnp.sin(angle), jnp.cos(angle)], axis=1)


def linear(left_op, right_op):
    return jnp.dot(left_op, right_op, preferred_element_type=jnp.float32)


def linear_tr(left_op, right_op):
    return lax.dot_general(
        left_op, right_op, (((1,), (1,)), ((), ())), preferred_element_type=jnp.float32
    )


def outer_sum(left_op, right_op):
    return lax.dot_general(
        left_op, right_op, (((0,), (0,)), ((), ())), preferred_element_type=jnp.float32
    )


def split_heads(matrix):
    return matrix.reshape(matrix.shape[0], HEADS, HEAD_DIM)


def accumulate(store, index_at, value):
    store[index_at] = value if store[index_at] is None else store[index_at] + value


def block_scores(piece_q, key_heads, valid_len, causal, start_at):
    block_rows, key_count = (piece_q.shape[0], key_heads.shape[0])
    scores = jnp.einsum(
        "qhd,khd->hqk", piece_q, key_heads, preferred_element_type=jnp.float32
    ) * HEAD_DIM ** (-0.5)
    key_at = jnp.arange(key_count)
    allowed = jnp.broadcast_to(key_at[None, :] < valid_len, (block_rows, key_count))
    if causal:
        allowed = allowed & (key_at[None, :] <= start_at + jnp.arange(block_rows)[:, None])
    return jnp.where(allowed[None], scores, -1000000000.0)


def attend_forward(query_in, keys_in, values_in, valid_len, causal):
    row_count = query_in.shape[0]
    block_rows = min(512, row_count)
    key_heads, value_heads = (split_heads(keys_in), split_heads(values_in))
    outputs, stats_kept = ([], [])
    for start_at in range(0, row_count, block_rows):
        scores = block_scores(
            split_heads(query_in[start_at : start_at + block_rows]),
            key_heads,
            valid_len,
            causal,
            start_at,
        )
        summit = jnp.max(scores, axis=-1, keepdims=True)
        expo_val = jnp.exp(scores - summit)
        totals = jnp.sum(expo_val, axis=-1, keepdims=True)
        probs_low = (expo_val / totals).astype(jnp.bfloat16)
        mixed_out = jnp.einsum(
            "hqk,khd->qhd", probs_low, value_heads, preferred_element_type=jnp.float32
        )
        outputs.append(mixed_out.reshape(block_rows, -1))
        stats_kept.append(summit + jnp.log(totals))
    return (jnp.concatenate(outputs, 0).astype(jnp.bfloat16), stats_kept)


def attend_backward(query_in, keys_in, values_in, valid_len, causal, stats_kept, grad_out):
    row_count = query_in.shape[0]
    block_rows = min(512, row_count)
    key_heads, value_heads = (split_heads(keys_in), split_heads(values_in))
    grad_keys = jnp.zeros(key_heads.shape, jnp.float32)
    grad_values = jnp.zeros(value_heads.shape, jnp.float32)
    grad_query = []
    for block_no, start_at in enumerate(range(0, row_count, block_rows)):
        piece_q = split_heads(query_in[start_at : start_at + block_rows])
        upstream = split_heads(grad_out[start_at : start_at + block_rows])
        probs_f = jnp.exp(
            block_scores(piece_q, key_heads, valid_len, causal, start_at) - stats_kept[block_no]
        )
        grad_probs = jnp.einsum(
            "qhd,khd->hqk", upstream, value_heads, preferred_element_type=jnp.float32
        )
        inner_sum = jnp.sum(probs_f * grad_probs, axis=-1, keepdims=True)
        grad_scores = (probs_f * (grad_probs - inner_sum)).astype(jnp.bfloat16)
        grad_query.append(
            (
                jnp.einsum(
                    "hqk,khd->qhd", grad_scores, key_heads, preferred_element_type=jnp.float32
                )
                * HEAD_DIM ** (-0.5)
            ).reshape(block_rows, -1)
        )
        grad_keys = grad_keys + jnp.einsum(
            "hqk,qhd->khd", grad_scores, piece_q, preferred_element_type=jnp.float32
        ) * HEAD_DIM ** (-0.5)
        grad_values = grad_values + jnp.einsum(
            "hqk,qhd->khd",
            probs_f.astype(jnp.bfloat16),
            upstream,
            preferred_element_type=jnp.float32,
        )
    key_count = keys_in.shape[0]
    return (
        jnp.concatenate(grad_query, 0),
        grad_keys.reshape(key_count, -1),
        grad_values.reshape(key_count, -1),
    )


def norm_backward(stream, gain_row, grad_normed):
    _, pull_back = jax.vjp(rms_norm, stream, gain_row)
    return pull_back(grad_normed)


def self_forward(stream, gain_row, weight, valid_len, causal):
    normed = rms_norm(stream, gain_row).astype(jnp.bfloat16)
    joint_qkv = linear(normed, weight[:, : 3 * D]).astype(jnp.bfloat16)
    mixed_out, stats_kept = attend_forward(
        joint_qkv[:, :D], joint_qkv[:, D : 2 * D], joint_qkv[:, 2 * D :], valid_len, causal
    )
    return (
        stream + linear(mixed_out, weight[:, 3 * D :]),
        (stream, normed, joint_qkv, mixed_out, stats_kept),
    )


def self_backward(grad_stream, kept_block, gain_row, weight, valid_len, causal):
    stream, normed, joint_qkv, mixed_out, stats_kept = kept_block
    grad_low = grad_stream.astype(jnp.bfloat16)
    grad_out_w = outer_sum(mixed_out, grad_low)
    grad_mixed = linear_tr(grad_low, weight[:, 3 * D :]).astype(jnp.bfloat16)
    grad_q, grad_k, grad_v = attend_backward(
        joint_qkv[:, :D],
        joint_qkv[:, D : 2 * D],
        joint_qkv[:, 2 * D :],
        valid_len,
        causal,
        stats_kept,
        grad_mixed,
    )
    grad_joint = jnp.concatenate([grad_q, grad_k, grad_v], 1).astype(jnp.bfloat16)
    grad_x, grad_gain = norm_backward(stream, gain_row, linear_tr(grad_joint, weight[:, : 3 * D]))
    return (
        grad_stream + grad_x,
        grad_gain,
        jnp.concatenate([outer_sum(normed, grad_joint), grad_out_w], 1),
    )


def cross_forward(stream, gain_row, weight, memory, valid_len):
    normed = rms_norm(stream, gain_row).astype(jnp.bfloat16)
    query_in = linear(normed, weight[:, :D]).astype(jnp.bfloat16)
    pair_kv = linear(memory, weight[:, D : 3 * D]).astype(jnp.bfloat16)
    mixed_out, stats_kept = attend_forward(
        query_in, pair_kv[:, :D], pair_kv[:, D:], valid_len, False
    )
    return (
        stream + linear(mixed_out, weight[:, 3 * D :]),
        (stream, normed, query_in, pair_kv, mixed_out, stats_kept),
    )


def cross_backward(grad_stream, kept_block, gain_row, weight, memory, valid_len):
    stream, normed, query_in, pair_kv, mixed_out, stats_kept = kept_block
    grad_low = grad_stream.astype(jnp.bfloat16)
    grad_out_w = outer_sum(mixed_out, grad_low)
    grad_mixed = linear_tr(grad_low, weight[:, 3 * D :]).astype(jnp.bfloat16)
    grad_q, grad_k, grad_v = attend_backward(
        query_in, pair_kv[:, :D], pair_kv[:, D:], valid_len, False, stats_kept, grad_mixed
    )
    grad_query = grad_q.astype(jnp.bfloat16)
    grad_pair = jnp.concatenate([grad_k, grad_v], 1).astype(jnp.bfloat16)
    grad_weight = jnp.concatenate(
        [outer_sum(normed, grad_query), outer_sum(memory, grad_pair), grad_out_w], 1
    )
    grad_x, grad_gain = norm_backward(stream, gain_row, linear_tr(grad_query, weight[:, :D]))
    return (
        grad_stream + grad_x,
        grad_gain,
        grad_weight,
        linear_tr(grad_pair, weight[:, D : 3 * D]),
    )


def gelu_tanh(hidden):
    return jax.nn.gelu(hidden, approximate=True)


def ffn_forward(stream, gain_row, w_in, w_out):
    normed = rms_norm(stream, gain_row).astype(jnp.bfloat16)
    hidden = linear(normed, w_in)
    active = gelu_tanh(hidden).astype(jnp.bfloat16)
    return (stream + linear_tr(active, w_out), (stream, normed, hidden, active))


def ffn_backward(grad_stream, kept_block, gain_row, w_in, w_out):
    stream, normed, hidden, active = kept_block
    grad_low = grad_stream.astype(jnp.bfloat16)
    grad_out_w = outer_sum(grad_low, active)
    _, pull_back = jax.vjp(gelu_tanh, hidden)
    grad_hidden = pull_back(linear(grad_low, w_out))[0].astype(jnp.bfloat16)
    grad_x, grad_gain = norm_backward(stream, gain_row, linear_tr(grad_hidden, w_in))
    return (grad_stream + grad_x, grad_gain, outer_sum(normed, grad_hidden), grad_out_w)


def embed(table_full, token_ids):
    return table_full[token_ids].astype(jnp.float32) * math.sqrt(D) + waves(token_ids.shape[0], D)


def forward_sequence(
    weights, gain_set, table_full, source, target, source_len, target_len, place_at
):
    stream = embed(table_full, source)
    layer_no = 0
    stream, kept_self = self_forward(
        stream, gain_set[2 * layer_no], weights[layer_no], source_len, False
    )
    stream, kept_ffn = ffn_forward(
        stream,
        gain_set[2 * layer_no + 1],
        weights[ENC + 2 * DEC + layer_no],
        weights[2 * ENC + 3 * DEC + layer_no],
    )
    enc_kept = [(kept_self, kept_ffn)]
    memory = rms_norm(stream, gain_set[2 * ENC]).astype(jnp.bfloat16)
    shifted = jnp.concatenate([jnp.zeros((1,), jnp.int32), target[:-1]])
    decoded = embed(table_full, shifted)
    dec_kept, exit_in, exit_rows = ([], [], [])
    for layer_no in range(DEC):
        base_at = 2 * ENC + 1 + 3 * layer_no
        decoded, kept_self = self_forward(
            decoded, gain_set[base_at], weights[ENC + layer_no], target_len, True
        )
        decoded, kept_cross = cross_forward(
            decoded, gain_set[base_at + 1], weights[ENC + DEC + layer_no], memory, source_len
        )
        decoded, kept_ffn = ffn_forward(
            decoded,
            gain_set[base_at + 2],
            weights[2 * ENC + 2 * DEC + layer_no],
            weights[3 * ENC + 3 * DEC + layer_no],
        )
        dec_kept.append((kept_self, kept_cross, kept_ffn))
        picked_rows = decoded[place_at]
        exit_in.append(picked_rows)
        exit_rows.append(
            rms_norm(picked_rows, gain_set[2 * ENC + 1 + 3 * DEC + layer_no]).astype(jnp.bfloat16)
        )
    return (
        (
            source,
            shifted,
            source_len,
            target_len,
            place_at,
            enc_kept,
            stream,
            memory,
            dec_kept,
            exit_in,
        ),
        exit_rows,
    )


def backward_sequence(
    weights, gain_set, kept_seq, exit_grads, grad_table, matrix_store, gain_store
):
    (
        source,
        shifted,
        source_len,
        target_len,
        place_at,
        enc_kept,
        stream,
        memory,
        dec_kept,
        exit_in,
    ) = kept_seq
    grad_decoded = jnp.zeros((shifted.shape[0], D), jnp.float32)
    grad_memory = jnp.zeros(memory.shape, jnp.float32)
    for layer_no in reversed(range(DEC)):
        base_at = 2 * ENC + 1 + 3 * layer_no
        exit_at = 2 * ENC + 1 + 3 * DEC + layer_no
        grad_rows, grad_gain = norm_backward(
            exit_in[layer_no], gain_set[exit_at], exit_grads[layer_no]
        )
        accumulate(gain_store, exit_at, grad_gain)
        grad_decoded = grad_decoded.at[place_at].add(grad_rows)
        kept_self, kept_cross, kept_ffn = dec_kept[layer_no]
        in_at, out_at = (2 * ENC + 2 * DEC + layer_no, 3 * ENC + 3 * DEC + layer_no)
        grad_decoded, grad_gain, grad_in, grad_out = ffn_backward(
            grad_decoded, kept_ffn, gain_set[base_at + 2], weights[in_at], weights[out_at]
        )
        accumulate(gain_store, base_at + 2, grad_gain)
        accumulate(matrix_store, in_at, grad_in)
        accumulate(matrix_store, out_at, grad_out)
        grad_decoded, grad_gain, grad_weight, grad_mem = cross_backward(
            grad_decoded,
            kept_cross,
            gain_set[base_at + 1],
            weights[ENC + DEC + layer_no],
            memory,
            source_len,
        )
        accumulate(gain_store, base_at + 1, grad_gain)
        accumulate(matrix_store, ENC + DEC + layer_no, grad_weight)
        grad_memory = grad_memory + grad_mem
        grad_decoded, grad_gain, grad_weight = self_backward(
            grad_decoded, kept_self, gain_set[base_at], weights[ENC + layer_no], target_len, True
        )
        accumulate(gain_store, base_at, grad_gain)
        accumulate(matrix_store, ENC + layer_no, grad_weight)
    grad_table = grad_table.at[shifted].add(grad_decoded * math.sqrt(D))
    grad_stream, grad_gain = norm_backward(stream, gain_set[2 * ENC], grad_memory)
    accumulate(gain_store, 2 * ENC, grad_gain)
    for layer_no in reversed(range(ENC)):
        kept_self, kept_ffn = enc_kept[layer_no]
        in_at, out_at = (ENC + 2 * DEC + layer_no, 2 * ENC + 3 * DEC + layer_no)
        grad_stream, grad_gain, grad_in, grad_out = ffn_backward(
            grad_stream, kept_ffn, gain_set[2 * layer_no + 1], weights[in_at], weights[out_at]
        )
        accumulate(gain_store, 2 * layer_no + 1, grad_gain)
        accumulate(matrix_store, in_at, grad_in)
        accumulate(matrix_store, out_at, grad_out)
        grad_stream, grad_gain, grad_weight = self_backward(
            grad_stream, kept_self, gain_set[2 * layer_no], weights[layer_no], source_len, False
        )
        accumulate(gain_store, 2 * layer_no, grad_gain)
        accumulate(matrix_store, layer_no, grad_weight)
    return grad_table.at[source].add(grad_stream * math.sqrt(D))


def local_stats(logits, summit_local, picked_local):
    return (summit_local, jnp.sum(jnp.exp(logits - summit_local[:, :, None]), axis=2), picked_local)


def exit_head(row_set, labels, valid_rows, table_part, first_row, fraction, count_all, reducer):
    logits = jnp.einsum("erd,vd->erv", row_set, table_part, preferred_element_type=jnp.float32)
    hit_mask = labels[:, None] - first_row == jnp.arange(table_part.shape[0])[None, :]
    picked_local = jnp.sum(jnp.where(hit_mask[None], logits, 0.0), axis=2)
    summit, total_sum, picked = reducer(logits, jnp.max(logits, axis=2), picked_local)
    spread = summit + jnp.log(total_sum)
    weight_rows = fraction[:, None] * valid_rows[None, :].astype(jnp.float32)
    probs_f = jnp.exp(logits - spread[:, :, None])
    grad_logits = (
        weight_rows[:, :, None] / count_all * (probs_f - hit_mask[None].astype(jnp.float32))
    ).astype(jnp.bfloat16)
    return (grad_logits, weight_rows * (spread - picked))


def untile(tiles):
    split = tiles.reshape(MATS, D // PB, FF // PB, PB, PB)
    return split.transpose(0, 1, 3, 2, 4).reshape(MATS, D, FF)


def tile_up(matrices):
    split = matrices.reshape(MATS, D // PB, PB, FF // PB, PB)
    return split.transpose(0, 1, 3, 2, 4).reshape(-1, PB, PB)


def turn_in(left_basis, tiles, right_basis):
    half = jnp.einsum("tki,tkl->til", left_basis, tiles, precision=HIGHEST)
    return jnp.einsum("til,tlj->tij", half, right_basis, precision=HIGHEST)


def turn_out(left_basis, tiles, right_basis):
    half = jnp.einsum("tik,tkl->til", left_basis, tiles, precision=HIGHEST)
    return jnp.einsum("til,tjl->tij", half, right_basis, precision=HIGHEST)


def solve_lower(lower_tri, right_side):
    return jax.scipy.linalg.solve_triangular(lower_tri, right_side, lower=True)


def renew_basis(statistic, basis):
    moved = jnp.einsum("tij,tjk->tik", statistic, basis, precision=HIGHEST)
    gram = jnp.einsum("tki,tkj->tij", moved, moved, precision=HIGHEST)
    lower_tri = jnp.linalg.cholesky(gram)
    solved = jax.vmap(solve_lower)(lower_tri, jnp.swapaxes(moved, 1, 2))
    return jnp.swapaxes(solved, 1, 2)


def soap_update(
    master, grad_tiles, first_mom, second_mom, left_stat, right_stat, left_basis, right_basis
):
    first_new = BETA_FIRST * first_mom + (1 - BETA_FIRST) * grad_tiles
    grad_turned = turn_in(left_basis, grad_tiles, right_basis)
    first_turned = turn_in(left_basis, first_new, right_basis)
    second_new = BETA_SECOND * second_mom + (1 - BETA_SECOND) * grad_turned * grad_turned
    direction = (
        first_turned
        / (1 - BETA_FIRST**STEP)
        / (jnp.sqrt(second_new / (1 - BETA_SECOND**STEP)) + ADAM_EPS)
    )
    master_new = master - RATE_MATRIX * (
        turn_out(left_basis, direction, right_basis) + DECAY * master
    )
    left_new = BETA_STAT * left_stat + (1 - BETA_STAT) * jnp.einsum(
        "tik,tjk->tij", grad_tiles, grad_tiles, precision=HIGHEST
    )
    right_new = BETA_STAT * right_stat + (1 - BETA_STAT) * jnp.einsum(
        "tki,tkj->tij", grad_tiles, grad_tiles, precision=HIGHEST
    )
    return (
        master_new,
        first_new,
        second_new,
        left_new,
        right_new,
        renew_basis(left_new, left_basis),
        renew_basis(right_new, right_basis),
    )


def adamw_update(master, grad_now, first_mom, second_mom, rate, decay_by):
    first_new = BETA_FIRST * first_mom + (1 - BETA_FIRST) * grad_now
    second_new = BETA_SECOND * second_mom + (1 - BETA_SECOND) * grad_now * grad_now
    direction = (
        first_new
        / (1 - BETA_FIRST**STEP)
        / (jnp.sqrt(second_new / (1 - BETA_SECOND**STEP)) + ADAM_EPS)
    )
    return (master - rate * (direction + decay_by * master), first_new, second_new)


def per_device(
    master_tiles,
    mom1_tiles,
    mom2_tiles,
    stat_left,
    stat_right,
    basis_left,
    basis_right,
    table_master,
    table_mom1,
    table_mom2,
    gains,
    gain_mom1,
    gain_mom2,
    source_ids,
    target_ids,
    source_len,
    target_len,
    loss_place,
    exit_layer,
    slot_list,
):
    counted = loss_place < target_len[:, :, None]
    local_counts = jnp.stack(
        [jnp.sum(counted.astype(jnp.float32))]
        + [
            jnp.sum((counted & (exit_layer >= layer_no)).astype(jnp.float32))
            for layer_no in range(DEC)
        ]
    )
    global_counts = lax.psum(local_counts, ("dp", "vocab"))
    count_all = global_counts[0]
    fraction = global_counts[1:] / jnp.sum(global_counts[1:])
    every_tile = lax.all_gather(
        master_tiles.astype(jnp.bfloat16), ("dp", "vocab"), axis=0, tiled=True
    )
    weights = untile(jnp.zeros_like(every_tile).at[slot_list].set(every_tile))
    table_used = table_master.astype(jnp.bfloat16)
    table_full = lax.all_gather(table_used, "vocab", axis=0, tiled=True)
    matrix_store = [None] * MATS
    gain_store = [None] * GAINS
    grad_table = jnp.zeros(table_full.shape, jnp.float32)
    loss_part = jnp.zeros((), jnp.float32)
    for micro_no in range(MICRO):
        rows_all = [[] for layer_no in range(DEC)]
        seq_no = 0
        kept_seq, exit_rows = forward_sequence(
            weights,
            gains,
            table_full,
            source_ids[micro_no, seq_no],
            target_ids[micro_no, seq_no],
            source_len[micro_no, seq_no],
            target_len[micro_no, seq_no],
            loss_place[micro_no, seq_no],
        )
        kept_all = [kept_seq]
        for layer_no in range(DEC):
            rows_all[layer_no].append(exit_rows[layer_no])
        rows_send = jnp.stack([jnp.concatenate(rows_all[layer_no], 0) for layer_no in range(DEC)])
        labels = target_ids[micro_no, 0][loss_place[micro_no, 0]]
        valid_rows = counted[micro_no].reshape(-1).astype(jnp.int32)
        grad_logits, row_loss = exit_head(
            rows_send, labels, valid_rows, table_full, 0, fraction, count_all, local_stats
        )
        grad_exit = jnp.einsum(
            "erv,vd->erd", grad_logits, table_full, preferred_element_type=jnp.float32
        )
        grad_table = grad_table + jnp.einsum(
            "erv,erd->vd", grad_logits, rows_send, preferred_element_type=jnp.float32
        )
        loss_part = loss_part + jnp.sum(row_loss)
        seq_no = 0
        exit_grads = [
            grad_exit[layer_no, seq_no * LOSS_POS : (seq_no + 1) * LOSS_POS]
            for layer_no in range(DEC)
        ]
        grad_table = backward_sequence(
            weights, gains, kept_all[seq_no], exit_grads, grad_table, matrix_store, gain_store
        )
    reduced = lax.psum_scatter(grad_table, "vocab", scatter_dimension=0, tiled=True)
    table_grad = lax.psum(reduced, "dp")
    tiles_grad = tile_up(jnp.stack(matrix_store))[slot_list]
    owned_grad = lax.psum_scatter(tiles_grad, ("dp", "vocab"), scatter_dimension=0, tiled=True)
    squares = jnp.sum(owned_grad * owned_grad) + jnp.sum(table_grad * table_grad) / lax.axis_size(
        "dp"
    )
    gain_total, square_total, loss_sum = lax.psum(
        (jnp.stack(gain_store), squares, loss_part), ("dp", "vocab")
    )
    grad_norm = jnp.sqrt(square_total + jnp.sum(gain_total * gain_total))
    factor = jnp.minimum(1.0, CLIP_AT / grad_norm)
    master_new, mom1_new, mom2_new, left_new, right_new, bleft_new, bright_new = soap_update(
        master_tiles,
        owned_grad * factor,
        mom1_tiles,
        mom2_tiles,
        stat_left,
        stat_right,
        basis_left,
        basis_right,
    )
    table_new, table_m, table_v = adamw_update(
        table_master, table_grad * factor, table_mom1, table_mom2, RATE_MATRIX, DECAY
    )
    gains_new, gains_m, gains_v = adamw_update(
        gains, gain_total * factor, gain_mom1, gain_mom2, RATE_VECTOR, 0.0
    )
    return (
        loss_sum,
        count_all,
        grad_norm,
        master_new,
        master_new.astype(jnp.bfloat16),
        mom1_new,
        mom2_new,
        left_new,
        right_new,
        bleft_new,
        bright_new,
        table_new,
        table_new.astype(jnp.bfloat16),
        table_m,
        table_v,
        gains_new,
        gains_m,
        gains_v,
    )


def solution(mesh):
    placed = (
        P(("dp", "vocab"), None, None),
        P(("dp", "vocab"), None, None),
        P(("dp", "vocab"), None, None),
        P(("dp", "vocab"), None, None),
        P(("dp", "vocab"), None, None),
        P(("dp", "vocab"), None, None),
        P(("dp", "vocab"), None, None),
        P("vocab", None),
        P("vocab", None),
        P("vocab", None),
        P(),
        P(),
        P(),
        P(None, ("dp", "vocab"), None),
        P(None, ("dp", "vocab"), None),
        P(None, ("dp", "vocab")),
        P(None, ("dp", "vocab")),
        P(None, ("dp", "vocab"), None),
        P(None, ("dp", "vocab"), None),
        P(),
    )
    return jax.shard_map(
        per_device,
        mesh=mesh,
        in_specs=placed,
        out_specs=(
            P(),
            P(),
            P(),
            P(("dp", "vocab"), None, None),
            P(("dp", "vocab"), None, None),
            P(("dp", "vocab"), None, None),
            P(("dp", "vocab"), None, None),
            P(("dp", "vocab"), None, None),
            P(("dp", "vocab"), None, None),
            P(("dp", "vocab"), None, None),
            P(("dp", "vocab"), None, None),
            P("vocab", None),
            P("vocab", None),
            P("vocab", None),
            P("vocab", None),
            P(),
            P(),
            P(),
        ),
        check_vma=False,
    )
```

profile of v0, /device:TPU:0, one launch (start us, length us, event | category | flops | bytes accessed | tf_op | source)
XLA Modules:
  0.0 5138.4 jit_solution(14176953991094298439)
XLA Ops:
  21.3 44.1 psum.35
  88.2 182.9 %all-gather.5.cloned.1.call-done = bf16[2816,64,64]{2,1,0:T(8,128)(2,1)} async-done(((bf16[88,64,64]{2,1,0:T(8,128)(2,1)}), bf16[2816,64,64]{2,1,0:T(8,128)(2,1)}) %all-gather.5.cloned.1.call-update) | async-done | bytes 23068688 | tf_op jit(solution)/shard_map/all_gather | solution.py:504
  271.1 20.1 broadcast_in_dim.198
  291.3 364.0 %scatter_fusion = bf16[2816,64,64]{2,1,0:T(8,128)(2,1)} fusion(bf16[2816,64,64]{2,1,0:T(8,128)(2,1)} %broadcast_in_dim.198, s32[2816]{0:T(1024)S(1)} %compare_select_fusion, bf16[2816,64,64]{2,1,0:T(8,128)(2,1)} %all-gather.5.cloned.1.call-done), kind=kCustom, calls=%fused_computation.11 | custom fusion | bytes 69217280 | tf_op jit(solution)/shard_map/scatter | solution.py:507
  655.2 46.4 copy.630
  701.6 30.4 fusion.460
  806.4 12.1 gather_fusion.1
  1086.7 15.7 fusion.488
  1104.5 17.3 fusion.487
  1130.9 14.3 fusion.2
  1145.3 13.6 fusion
  1387.2 14.3 multiply_reduce_fusion.2
  1445.4 14.4 multiply_reduce_fusion
  1463.8 25.3 fusion.356
  1489.2 12.6 multiply_convert_fusion.2
  1519.3 12.2 multiply_convert_fusion
  1567.4 46.5 bitcast_add_fusion
  1618.2 31.3 scatter_fusion.1
  1649.6 121.3 %scatter_fusion.2 = f32[32768,512]{1,0:T(8,128)} fusion(f32[32768,512]{1,0:T(8,128)} %scatter_fusion.1, s32[1024]{0:T(1024)S(1)} %bitcast.917, f32[1024,512]{1,0:T(8,128)S(1)} %copy-done.151), kind=kCustom, calls=%fused_computation.17 | custom fusion | flops 524288 | bytes 6295552 | tf_op jit(solution)/shard_map/scatter-add | solution.py:375
  1770.8 31.4 scatter_fusion.3
  1802.2 121.3 %scatter_fusion.4 = f32[32768,512]{1,0:T(8,128)} fusion(f32[32768,512]{1,0:T(8,128)} %scatter_fusion.3, s32[1024]{0:T(1024)S(1)} %bitcast.915, f32[1024,512]{1,0:T(8,128)S(1)} %copy-done.152), kind=kCustom, calls=%fused_computation.19 | custom fusion | flops 524288 | bytes 6295552 | tf_op jit(solution)/shard_map/scatter-add | solution.py:375
  2167.3 12.3 copy_dynamic-update-slice_fusion.3
  2203.8 66.4 %gather_fusion.10 = f32[2816,64,64]{2,1,0:T(8,128)} fusion(f32[2816,64,64]{2,1,0:T(8,128)} %bitcast.216, s32[3072]{0:T(1024)S(1)} %copy-done.429), kind=kCustom, calls=%fused_computation.10 | custom fusion | bytes 92285952 | tf_op jit(solution)/shard_map/gather | solution.py:553
  2270.3 290.9 %reduce-scatter.5.cloned.1.call-done = f32[4096,512]{1,0:T(8,128)} async-done(((f32[32768,512]{1,0:T(8,128)}), f32[4096,512]{1,0:T(8,128)}) %reduce-scatter.5.cloned.1.call-update) | async-done | bytes 8388624 | tf_op jit(solution)/shard_map/reduce_scatter | solution.py:551
  2588.9 943.8 %reduce-scatter.3.cloned.1.call-done = f32[88,64,64]{2,1,0:T(8,128)} async-done(((f32[2816,64,64]{2,1,0:T(8,128)}), f32[88,64,64]{2,1,0:T(8,128)}) %reduce-scatter.3.cloned.1.call-update) | async-done | bytes 1441808 | tf_op jit(solution)/shard_map/reduce_scatter | solution.py:554
  3535.9 169.3 %all-reduce.3.cloned.1.call-done = f32[4096,512]{1,0:T(8,128)} async-done(((f32[4096,512]{1,0:T(8,128)}), f32[4096,512]{1,0:T(8,128)}) %all-reduce.3.cloned.1.call-update) | async-done | bytes 8388624 | tf_op jit(solution)/shard_map/psum | solution.py:552
  3717.3 40.4 all-reduce
  3809.1 517.6 %custom-call.8 = f32[88,64,64]{2,1,0:T(8,128)} custom-call(f32[88,64,64]{2,1,0:T(8,128)} %fusion.81), custom_call_target="Cholesky" | custom-call | tf_op jit(solution)/shard_map/jit(cholesky)/cholesky | solution.py:423
  4364.4 517.6 %custom-call.10 = f32[88,64,64]{2,1,0:T(8,128)} custom-call(f32[88,64,64]{2,1,0:T(8,128)} %fusion.78), custom_call_target="Cholesky" | custom-call | tf_op jit(solution)/shard_map/jit(cholesky)/cholesky | solution.py:423
  4892.1 68.6 %custom-call.11 = f32[88,1,64,64]{0,2,3,1:T(8,128)} custom-call(f32[88,1,64,64]{0,3,2,1:T(8,128)} %get-tuple-element.230), custom_call_target="InvertDiagBlocksLowerTriangular" | custom-call | tf_op jit(solution)/shard_map/vmap(jit(_solve_triangular))/triangular_solve | solution.py:417
  4978.8 68.4 %custom-call.9 = f32[88,1,64,64]{0,2,3,1:T(8,128)} custom-call(f32[88,1,64,64]{0,3,2,1:T(8,128)} %get-tuple-element.231), custom_call_target="InvertDiagBlocksLowerTriangular" | custom-call | tf_op jit(solution)/shard_map/vmap(jit(_solve_triangular))/triangular_solve | solution.py:417
  5106.7 23.8 fusion.458
  (1798 shorter events, 1200.5 us)
Async XLA Ops:
  7.2 263.9 %all-gather.5.cloned.1.call-start = ((), (), s32[]{:S(2)}) async-start(), calls=%async_computation.3 | async-start | bytes 47579136 | tf_op jit(solution)/shard_map/all_gather | solution.py:504
  11.9 794.5 %all-gather.3.cloned.1.call-start = ((), (), s32[]{:S(2)}) async-start(), calls=%async_computation.2 | async-start | bytes 37748736 | tf_op jit(solution)/shard_map/all_gather | solution.py:509
  17.9 48.2 copy-start.531
  17.9 51.5 %copy-start.560 = (s32[2,1]{0,1:T(1,128)S(1)}, s32[2,1]{0,1:T(1,128)}, u32[]{:S(2)}) copy-start(s32[2,1]{0,1:T(1,128)} %param.38) | copy-start | bytes 28
  17.9 57.7 %copy-start.530 = (s32[2,1,1024]{2,1,0:T(1,128)S(1)}, s32[2,1,1024]{2,1,0:T(1,128)}, u32[]{:S(2)}) copy-start(s32[2,1,1024]{2,1,0:T(1,128)} %param.36) | copy-start | bytes 24580
  17.9 57.7 %copy-start.490 = (s32[2816]{0:T(1024)S(1)}, s32[2816]{0:T(1024)}, u32[]{:S(2)}) copy-start(s32[2816]{0:T(1024)} %param.42) | copy-start | bytes 33796
  17.9 57.7 %copy-start.389 = (f32[11,512]{1,0:T(8,128)S(1)}, f32[11,512]{1,0:T(8,128)}, u32[]{:S(2)}) copy-start(f32[11,512]{1,0:T(8,128)} %param.33) | copy-start | bytes 67588
  18.0 2543.2 %reduce-scatter.5.cloned.1.call-start = ((), (), s32[]{:S(2)}) async-start(), calls=%async_computation.5 | async-start | bytes 75497472 | tf_op jit(solution)/shard_map/reduce_scatter | solution.py:551
  70.6 786.3 %copy-start.379 = (pred[1024]{0:T(1024)(128)(4,1)}, pred[1024]{0:T(1024)(128)(4,1)S(1)}, u32[]{:S(2)}) copy-start(pred[1024]{0:T(1024)(128)(4,1)S(1)} %iota_compare_fusion.5) | copy-start | bytes 3076
  75.7 215.6 %copy-start.374 = (s32[2816]{0:T(1024)}, s32[2816]{0:T(1024)S(1)}, u32[]{:S(2)}) copy-start(s32[2816]{0:T(1024)S(1)} %compare_select_fusion) | copy-start | bytes 33796
  76.3 764.2 %copy-start.515 = (f32[1,512]{1,0:T(1,128)}, f32[1,512]{1,0:T(1,128)S(1)}, u32[]{:S(2)}) copy-start(f32[1,512]{1,0:T(1,128)S(1)} %get-tuple-element.227) | copy-start | bytes 6148
  835.5 106.3 %copy-start.60 = (f32[1024,512]{0,1:T(8,128)}, f32[1024,512]{0,1:T(8,128)S(1)}, u32[]{:S(2)}) copy-start(f32[1024,512]{0,1:T(8,128)S(1)} %get-tuple-element.164) | copy-start | bytes 6291460
  898.8 53.1 %copy-start.442 = (f32[1024]{0:T(1024)}, f32[1024]{0:T(1024)S(1)}, u32[]{:S(2)}) copy-start(f32[1024]{0:T(1024)S(1)} %fusion.374) | copy-start | bytes 12292
  972.8 28.3 copy-start.493
  972.8 38.3 copy-start.105
  999.7 29.5 copy-start.546
  1035.0 179.0 %copy-start.75 = (f32[256,512]{1,0:T(8,128)}, f32[256,512]{1,0:T(8,128)S(1)}, u32[]{:S(2)}) copy-start(f32[256,512]{1,0:T(8,128)S(1)} %get-tuple-element.349) | copy-start | bytes 1572868
  1063.1 151.0 %copy-start.77 = (f32[256,512]{1,0:T(8,128)}, f32[256,512]{1,0:T(8,128)S(1)}, u32[]{:S(2)}) copy-start(f32[256,512]{1,0:T(8,128)S(1)} %get-tuple-element.331) | copy-start | bytes 1572868
  1254.0 26.5 copy-start.144
  1353.6 59.3 %copy-start.38 = (f32[1024,512]{0,1:T(8,128)}, f32[1024,512]{0,1:T(8,128)S(1)}, u32[]{:S(2)}) copy-start(f32[1024,512]{0,1:T(8,128)S(1)} %get-tuple-element.252) | copy-start | bytes 6291460
  1387.2 28.2 slice-start
  1387.2 28.2 slice-start.1
  1387.2 28.2 slice-start.2
  1489.2 26.2 slice-start.16
  1618.2 31.4 copy-start.151
  1618.2 31.4 copy-start.441
  1649.5 121.3 %copy-start.512 = (s32[256,1]{0,1:T(1,128)S(1)}, s32[256,1]{0,1:T(1,128)}, u32[]{:S(2)}) copy-start(s32[256,1]{0,1:T(1,128)} %copy-done.511) | copy-start | bytes 3076
  1770.8 31.4 copy-start.152
  1770.8 31.4 copy-start.439
  1923.5 1609.2 %reduce-scatter.3.cloned.1.call-start = ((), (), s32[]{:S(2)}) async-start(), calls=%async_computation.4 | async-start | bytes 95158272 | tf_op jit(solution)/shard_map/reduce_scatter | solution.py:554
  2270.2 1434.9 %all-reduce.3.cloned.1.call-start = ((), (), s32[]{:S(2)}) async-start(), calls=%async_computation.6 | async-start | bytes 16777216 | tf_op jit(solution)/shard_map/psum | solution.py:552
  3711.3 48.4 copy-start.12
  (618 other events, 3000.9 us)
Sparse Core Ops, SparseCore 0:
  12.0 259.0 all-gather.4
  273.3 286.7 all-gather.2
  1923.6 637.5 reduce-scatter.4
  2563.5 969.1 reduce-scatter.2
  3536.5 168.6 all-reduce.2
where the time goes:
time: 5170 us; the launch traced here: 5140 us
  other arithmetic  1710 us (33%)
  waiting for transfers between devices  1590 us (31%)
  local copies, waits for them, and re-layouts  1050 us (20%)
  matrix products  681 us (13%)
  blocking collectives  84.6 us (2%)
    another operation x6, other arithmetic, renew_basis(): lower_tri = jnp.linalg.cholesky(gram)  1040 us
    reduce_scatter x1, waiting for transfers between devices, per_device(): lax.psum_scatter(tiles_grad, ('dp', 'vocab'), scatter_dimension=0, tiled=...  944 us
    scatter x1, local copies, waits for them, and re-layouts, per_device(): weights = untile(jnp.zeros_like(every_tile).at[slot_list].set(every_tile))  364 us
    reduce_scatter x1, waiting for transfers between devices, per_device(): lax.psum_scatter(grad_table, 'vocab', scatter_dimension=0, tiled=True)  291 us
    scatter-add x2, other arithmetic, backward_sequence(): return grad_table.at[source].add(grad_stream * math.sqrt(D))  243 us
    unnamed x1315, local copies, waits for them, and re-layouts  221 us
    all_gather x1, waiting for transfers between devices, per_device(): lax.all_gather(master_tiles.astype(jnp.bfloat16), ('dp', 'vocab'), axis=0...  183 us
    psum x1, waiting for transfers between devices, per_device(): table_grad = lax.psum(reduced, 'dp')  169 us
  transfers between devices with their start and end apart: 5, of which 4 were waited for; matrix products, arithmetic and copies ran while one was open for 18% of the time, Pallas kernels for 0%

commit v1 on v0

--- a/solution.py
+++ b/solution.py
@@ -3,6 +3,8 @@
 import jax
 import jax.numpy as jnp
 from jax import lax
+from jax.experimental import pallas as pl
+from jax.experimental.pallas import tpu as pltpu
 from jax.sharding import PartitionSpec as P
 
 D = 512
@@ -66,10 +68,6 @@
     return matrix.reshape(matrix.shape[0], HEADS, HEAD_DIM)
 
 
-def accumulate(store, index_at, value):
-    store[index_at] = value if store[index_at] is None else store[index_at] + value
-
-
 def block_scores(piece_q, key_heads, valid_len, causal, start_at):
     block_rows, key_count = (piece_q.shape[0], key_heads.shape[0])
     scores = jnp.einsum(
@@ -155,10 +153,45 @@
     return pull_back(grad_normed)
 
 
+def by_sequence(matrix):
+    return jnp.split(matrix, MICRO, axis=0)
+
+
+def attend_all(query_in, keys_in, values_in, valid_len, causal):
+    outs, stats = ([], [])
+    for seq_no, (piece_q, piece_k, piece_v) in enumerate(
+        zip(by_sequence(query_in), by_sequence(keys_in), by_sequence(values_in))
+    ):
+        out, kept = attend_forward(piece_q, piece_k, piece_v, valid_len[seq_no], causal)
+        outs.append(out)
+        stats.append(kept)
+    return (jnp.concatenate(outs, 0), stats)
+
+
+def attend_all_backward(query_in, keys_in, values_in, valid_len, causal, stats, mixed_out, grad_out):
+    parts = []
+    for seq_no, pieces in enumerate(
+        zip(
+            by_sequence(query_in), by_sequence(keys_in), by_sequence(values_in),
+            by_sequence(grad_out),
+        )
+    ):
+        piece_q, piece_k, piece_v, upstream = pieces
+        parts.append(
+            attend_backward(
+                piece_q, piece_k, piece_v, valid_len[seq_no], causal, stats[seq_no], upstream
+            )
+        )
+    return tuple(
+        jnp.concatenate([part[item] for part in parts], 0).astype(jnp.bfloat16)
+        for item in range(3)
+    )
+
+
 def self_forward(stream, gain_row, weight, valid_len, causal):
     normed = rms_norm(stream, gain_row).astype(jnp.bfloat16)
     joint_qkv = linear(normed, weight[:, : 3 * D]).astype(jnp.bfloat16)
-    mixed_out, stats_kept = attend_forward(
+    mixed_out, stats_kept = attend_all(
         joint_qkv[:, :D], joint_qkv[:, D : 2 * D], joint_qkv[:, 2 * D :], valid_len, causal
     )
     return (
@@ -172,21 +205,22 @@
     grad_low = grad_stream.astype(jnp.bfloat16)
     grad_out_w = outer_sum(mixed_out, grad_low)
     grad_mixed = linear_tr(grad_low, weight[:, 3 * D :]).astype(jnp.bfloat16)
-    grad_q, grad_k, grad_v = attend_backward(
+    grad_q, grad_k, grad_v = attend_all_backward(
         joint_qkv[:, :D],
         joint_qkv[:, D : 2 * D],
         joint_qkv[:, 2 * D :],
         valid_len,
         causal,
         stats_kept,
+        mixed_out,
         grad_mixed,
     )
-    grad_joint = jnp.concatenate([grad_q, grad_k, grad_v], 1).astype(jnp.bfloat16)
+    grad_joint = jnp.concatenate([grad_q, grad_k, grad_v], 1)
     grad_x, grad_gain = norm_backward(stream, gain_row, linear_tr(grad_joint, weight[:, : 3 * D]))
     return (
         grad_stream + grad_x,
         grad_gain,
-        jnp.concatenate([outer_sum(normed, grad_joint), grad_out_w], 1),
+        jnp.concatenate([outer_sum(normed, grad_joint), grad_out_w], 1).astype(jnp.bfloat16),
     )
 
 
@@ -194,9 +228,7 @@
     normed = rms_norm(stream, gain_row).astype(jnp.bfloat16)
     query_in = linear(normed, weight[:, :D]).astype(jnp.bfloat16)
     pair_kv = linear(memory, weight[:, D : 3 * D]).astype(jnp.bfloat16)
-    mixed_out, stats_kept = attend_forward(
-        query_in, pair_kv[:, :D], pair_kv[:, D:], valid_len, False
-    )
+    mixed_out, stats_kept = attend_all(query_in, pair_kv[:, :D], pair_kv[:, D:], valid_len, False)
     return (
         stream + linear(mixed_out, weight[:, 3 * D :]),
         (stream, normed, query_in, pair_kv, mixed_out, stats_kept),
@@ -208,14 +240,13 @@
     grad_low = grad_stream.astype(jnp.bfloat16)
     grad_out_w = outer_sum(mixed_out, grad_low)
     grad_mixed = linear_tr(grad_low, weight[:, 3 * D :]).astype(jnp.bfloat16)
-    grad_q, grad_k, grad_v = attend_backward(
-        query_in, pair_kv[:, :D], pair_kv[:, D:], valid_len, False, stats_kept, grad_mixed
-    )
-    grad_query = grad_q.astype(jnp.bfloat16)
-    grad_pair = jnp.concatenate([grad_k, grad_v], 1).astype(jnp.bfloat16)
+    grad_query, grad_k, grad_v = attend_all_backward(
+        query_in, pair_kv[:, :D], pair_kv[:, D:], valid_len, False, stats_kept, mixed_out, grad_mixed
+    )
+    grad_pair = jnp.concatenate([grad_k, grad_v], 1)
     grad_weight = jnp.concatenate(
         [outer_sum(normed, grad_query), outer_sum(memory, grad_pair), grad_out_w], 1
-    )
+    ).astype(jnp.bfloat16)
     grad_x, grad_gain = norm_backward(stream, gain_row, linear_tr(grad_query, weight[:, :D]))
     return (
         grad_stream + grad_x,
@@ -239,35 +270,34 @@
 def ffn_backward(grad_stream, kept_block, gain_row, w_in, w_out):
     stream, normed, hidden, active = kept_block
     grad_low = grad_stream.astype(jnp.bfloat16)
-    grad_out_w = outer_sum(grad_low, active)
+    grad_out_w = outer_sum(grad_low, active).astype(jnp.bfloat16)
     _, pull_back = jax.vjp(gelu_tanh, hidden)
     grad_hidden = pull_back(linear(grad_low, w_out))[0].astype(jnp.bfloat16)
     grad_x, grad_gain = norm_backward(stream, gain_row, linear_tr(grad_hidden, w_in))
-    return (grad_stream + grad_x, grad_gain, outer_sum(normed, grad_hidden), grad_out_w)
-
-
-def embed(table_full, token_ids):
-    return table_full[token_ids].astype(jnp.float32) * math.sqrt(D) + waves(token_ids.shape[0], D)
-
-
-def forward_sequence(
-    weights, gain_set, table_full, source, target, source_len, target_len, place_at
-):
-    stream = embed(table_full, source)
-    layer_no = 0
-    stream, kept_self = self_forward(
-        stream, gain_set[2 * layer_no], weights[layer_no], source_len, False
-    )
-    stream, kept_ffn = ffn_forward(
-        stream,
-        gain_set[2 * layer_no + 1],
-        weights[ENC + 2 * DEC + layer_no],
-        weights[2 * ENC + 3 * DEC + layer_no],
-    )
-    enc_kept = [(kept_self, kept_ffn)]
+    return (
+        grad_stream + grad_x,
+        grad_gain,
+        outer_sum(normed, grad_hidden).astype(jnp.bfloat16),
+        grad_out_w,
+    )
+
+
+def forward_all(weights, gain_set, source_rows, target_rows, source_len, target_len, place_rows):
+    stream = source_rows
+    enc_kept = []
+    for layer_no in range(ENC):
+        stream, kept_self = self_forward(
+            stream, gain_set[2 * layer_no], weights[layer_no], source_len, False
+        )
+        stream, kept_ffn = ffn_forward(
+            stream,
+            gain_set[2 * layer_no + 1],
+            weights[ENC + 2 * DEC + layer_no],
+            weights[2 * ENC + 3 * DEC + layer_no],
+        )
+        enc_kept.append((kept_self, kept_ffn))
     memory = rms_norm(stream, gain_set[2 * ENC]).astype(jnp.bfloat16)
-    shifted = jnp.concatenate([jnp.zeros((1,), jnp.int32), target[:-1]])
-    decoded = embed(table_full, shifted)
+    decoded = target_rows
     dec_kept, exit_in, exit_rows = ([], [], [])
     for layer_no in range(DEC):
         base_at = 2 * ENC + 1 + 3 * layer_no
@@ -284,123 +314,300 @@
             weights[3 * ENC + 3 * DEC + layer_no],
         )
         dec_kept.append((kept_self, kept_cross, kept_ffn))
-        picked_rows = decoded[place_at]
+        picked_rows = decoded[place_rows]
         exit_in.append(picked_rows)
         exit_rows.append(
             rms_norm(picked_rows, gain_set[2 * ENC + 1 + 3 * DEC + layer_no]).astype(jnp.bfloat16)
         )
-    return (
-        (
-            source,
-            shifted,
-            source_len,
-            target_len,
-            place_at,
-            enc_kept,
-            stream,
-            memory,
-            dec_kept,
-            exit_in,
-        ),
-        exit_rows,
-    )
-
-
-def backward_sequence(
-    weights, gain_set, kept_seq, exit_grads, grad_table, matrix_store, gain_store
-):
-    (
-        source,
-        shifted,
-        source_len,
-        target_len,
-        place_at,
-        enc_kept,
-        stream,
-        memory,
-        dec_kept,
-        exit_in,
-    ) = kept_seq
-    grad_decoded = jnp.zeros((shifted.shape[0], D), jnp.float32)
+    kept = (source_len, target_len, place_rows, enc_kept, stream, memory, dec_kept, exit_in)
+    return (kept, jnp.concatenate(exit_rows, 0))
+
+
+def backward_all(weights, gain_set, kept, exit_grads, matrix_store, gain_store):
+    source_len, target_len, place_rows, enc_kept, stream, memory, dec_kept, exit_in = kept
+    exit_each = jnp.split(exit_grads, DEC, axis=0)
+    grad_decoded = jnp.zeros(dec_kept[0][0][0].shape, jnp.float32)
     grad_memory = jnp.zeros(memory.shape, jnp.float32)
     for layer_no in reversed(range(DEC)):
         base_at = 2 * ENC + 1 + 3 * layer_no
         exit_at = 2 * ENC + 1 + 3 * DEC + layer_no
-        grad_rows, grad_gain = norm_backward(
-            exit_in[layer_no], gain_set[exit_at], exit_grads[layer_no]
-        )
-        accumulate(gain_store, exit_at, grad_gain)
-        grad_decoded = grad_decoded.at[place_at].add(grad_rows)
+        grad_rows, gain_store[exit_at] = norm_backward(
+            exit_in[layer_no], gain_set[exit_at], exit_each[layer_no]
+        )
+        grad_decoded = grad_decoded.at[place_rows].add(grad_rows)
         kept_self, kept_cross, kept_ffn = dec_kept[layer_no]
         in_at, out_at = (2 * ENC + 2 * DEC + layer_no, 3 * ENC + 3 * DEC + layer_no)
-        grad_decoded, grad_gain, grad_in, grad_out = ffn_backward(
-            grad_decoded, kept_ffn, gain_set[base_at + 2], weights[in_at], weights[out_at]
-        )
-        accumulate(gain_store, base_at + 2, grad_gain)
-        accumulate(matrix_store, in_at, grad_in)
-        accumulate(matrix_store, out_at, grad_out)
-        grad_decoded, grad_gain, grad_weight, grad_mem = cross_backward(
-            grad_decoded,
-            kept_cross,
-            gain_set[base_at + 1],
-            weights[ENC + DEC + layer_no],
-            memory,
-            source_len,
-        )
-        accumulate(gain_store, base_at + 1, grad_gain)
-        accumulate(matrix_store, ENC + DEC + layer_no, grad_weight)
+        grad_decoded, gain_store[base_at + 2], matrix_store[in_at], matrix_store[out_at] = (
+            ffn_backward(
+                grad_decoded, kept_ffn, gain_set[base_at + 2], weights[in_at], weights[out_at]
+            )
+        )
+        cross_at = ENC + DEC + layer_no
+        grad_decoded, gain_store[base_at + 1], matrix_store[cross_at], grad_mem = cross_backward(
+            grad_decoded, kept_cross, gain_set[base_at + 1], weights[cross_at], memory, source_len
+        )
         grad_memory = grad_memory + grad_mem
-        grad_decoded, grad_gain, grad_weight = self_backward(
+        grad_decoded, gain_store[base_at], matrix_store[ENC + layer_no] = self_backward(
             grad_decoded, kept_self, gain_set[base_at], weights[ENC + layer_no], target_len, True
         )
-        accumulate(gain_store, base_at, grad_gain)
-        accumulate(matrix_store, ENC + layer_no, grad_weight)
-    grad_table = grad_table.at[shifted].add(grad_decoded * math.sqrt(D))
-    grad_stream, grad_gain = norm_backward(stream, gain_set[2 * ENC], grad_memory)
-    accumulate(gain_store, 2 * ENC, grad_gain)
+    grad_stream, gain_store[2 * ENC] = norm_backward(stream, gain_set[2 * ENC], grad_memory)
     for layer_no in reversed(range(ENC)):
         kept_self, kept_ffn = enc_kept[layer_no]
         in_at, out_at = (ENC + 2 * DEC + layer_no, 2 * ENC + 3 * DEC + layer_no)
-        grad_stream, grad_gain, grad_in, grad_out = ffn_backward(
-            grad_stream, kept_ffn, gain_set[2 * layer_no + 1], weights[in_at], weights[out_at]
-        )
-        accumulate(gain_store, 2 * layer_no + 1, grad_gain)
-        accumulate(matrix_store, in_at, grad_in)
-        accumulate(matrix_store, out_at, grad_out)
-        grad_stream, grad_gain, grad_weight = self_backward(
+        grad_stream, gain_store[2 * layer_no + 1], matrix_store[in_at], matrix_store[out_at] = (
+            ffn_backward(
+                grad_stream, kept_ffn, gain_set[2 * layer_no + 1], weights[in_at], weights[out_at]
+            )
+        )
+        grad_stream, gain_store[2 * layer_no], matrix_store[layer_no] = self_backward(
             grad_stream, kept_self, gain_set[2 * layer_no], weights[layer_no], source_len, False
         )
-        accumulate(gain_store, 2 * layer_no, grad_gain)
-        accumulate(matrix_store, layer_no, grad_weight)
-    return grad_table.at[source].add(grad_stream * math.sqrt(D))
-
-
-def local_stats(logits, summit_local, picked_local):
-    return (summit_local, jnp.sum(jnp.exp(logits - summit_local[:, :, None]), axis=2), picked_local)
-
-
-def exit_head(row_set, labels, valid_rows, table_part, first_row, fraction, count_all, reducer):
-    logits = jnp.einsum("erd,vd->erv", row_set, table_part, preferred_element_type=jnp.float32)
-    hit_mask = labels[:, None] - first_row == jnp.arange(table_part.shape[0])[None, :]
-    picked_local = jnp.sum(jnp.where(hit_mask[None], logits, 0.0), axis=2)
-    summit, total_sum, picked = reducer(logits, jnp.max(logits, axis=2), picked_local)
-    spread = summit + jnp.log(total_sum)
-    weight_rows = fraction[:, None] * valid_rows[None, :].astype(jnp.float32)
-    probs_f = jnp.exp(logits - spread[:, :, None])
-    grad_logits = (
-        weight_rows[:, :, None] / count_all * (probs_f - hit_mask[None].astype(jnp.float32))
-    ).astype(jnp.bfloat16)
-    return (grad_logits, weight_rows * (spread - picked))
-
-
-def untile(tiles):
-    split = tiles.reshape(MATS, D // PB, FF // PB, PB, PB)
-    return split.transpose(0, 1, 3, 2, 4).reshape(MATS, D, FF)
-
-
-def tile_up(matrices):
-    split = matrices.reshape(MATS, D // PB, PB, FF // PB, PB)
-    return split.transpose(0, 1, 3, 2, 4).reshape(-1, PB, PB)
+    return (grad_stream, grad_decoded)
+
+
+def fold_blocks(tiles):
+    return jnp.concatenate([tiles[:, : PB // 2], tiles[:, PB // 2 :]], axis=2)
+
+
+def unfold_blocks(folded):
+    return jnp.concatenate([folded[:, :, :PB], folded[:, :, PB:]], axis=1)
+
+
+def swap_halves(value):
+    return jnp.concatenate([value[:, PB:], value[:, :PB]], axis=1)
+
+
+def lay_matrices(folded_all, slot_of):
+    half = PB // 2
+    row_blocks, pairs = (D // PB, FF // (2 * PB))
+
+    def kernel(slot_ref, folded_ref, out_ref):
+        first = pl.program_id(0) * row_blocks * 2 * pairs + pl.program_id(1) * 2 * pairs
+        left_half = lax.broadcasted_iota(jnp.int32, (half, 2 * PB), 1) < PB
+        for pair_no in range(pairs):
+            even = folded_ref[slot_ref[first + 2 * pair_no]].astype(jnp.float32)
+            odd = folded_ref[slot_ref[first + 2 * pair_no + 1]].astype(jnp.float32)
+            even_turned = pltpu.roll(even, PB, 1)
+            odd_turned = pltpu.roll(odd, PB, 1)
+            columns = slice(2 * PB * pair_no, 2 * PB * (pair_no + 1))
+            out_ref[0, :half, columns] = jnp.where(left_half, even, odd_turned).astype(jnp.bfloat16)
+            out_ref[0, half:, columns] = jnp.where(left_half, even_turned, odd).astype(jnp.bfloat16)
+
+    return pl.pallas_call(
+        kernel,
+        out_shape=jax.ShapeDtypeStruct((MATS, D, FF), jnp.bfloat16),
+        grid_spec=pltpu.PrefetchScalarGridSpec(
+            num_scalar_prefetch=1,
+            grid=(MATS, row_blocks),
+            in_specs=[pl.BlockSpec(memory_space=pltpu.VMEM)],
+            out_specs=pl.BlockSpec((1, PB, FF), lambda mat_no, row_no, slots: (mat_no, row_no, 0)),
+        ),
+        compiler_params=pltpu.CompilerParams(vmem_limit_bytes=40 * 2**20),
+    )(slot_of, folded_all)
+
+
+def fold_gradients(matrices, slot_of):
+    half = PB // 2
+    row_blocks, pairs = (D // PB, FF // (2 * PB))
+    count = MATS * row_blocks * 2 * pairs
+
+    def kernel(slot_ref, *refs):
+        sources, out_ref, held, arrived = (refs[:MATS], refs[MATS], refs[MATS + 1], refs[MATS + 2])
+        left_half = lax.broadcasted_iota(jnp.int32, (half, 2 * PB), 1) < PB
+
+        def fetch(mat_no):
+            return pltpu.make_async_copy(
+                sources[mat_no], held.at[mat_no % 2], arrived.at[mat_no % 2]
+            )
+
+        fetch(0).start()
+        for mat_no in range(MATS):
+            if mat_no + 1 < MATS:
+                fetch(mat_no + 1).start()
+            fetch(mat_no).wait()
+
+            def one_row(row_no, carry, mat_no=mat_no):
+                first = (mat_no * row_blocks + row_no) * 2 * pairs
+                row_at = pl.multiple_of(row_no * PB, PB)
+                for pair_no in range(pairs):
+                    columns = slice(2 * PB * pair_no, 2 * PB * (pair_no + 1))
+                    upper = held[mat_no % 2, pl.ds(row_at, half), columns].astype(jnp.float32)
+                    lower = held[mat_no % 2, pl.ds(row_at + half, half), columns].astype(jnp.float32)
+                    even = jnp.where(left_half, upper, pltpu.roll(lower, PB, 1))
+                    odd = jnp.where(left_half, pltpu.roll(upper, PB, 1), lower)
+                    out_ref[slot_ref[first + 2 * pair_no]] = even.astype(jnp.bfloat16)
+                    out_ref[slot_ref[first + 2 * pair_no + 1]] = odd.astype(jnp.bfloat16)
+                return carry
+
+            lax.fori_loop(0, row_blocks, one_row, 0)
+
+    return pl.pallas_call(
+        kernel,
+        out_shape=jax.ShapeDtypeStruct((count, half, 2 * PB), jnp.bfloat16),
+        grid_spec=pltpu.PrefetchScalarGridSpec(
+            num_scalar_prefetch=1,
+            grid=(1,),
+            in_specs=[pl.BlockSpec(memory_space=pl.ANY)] * MATS,
+            out_specs=pl.BlockSpec(memory_space=pltpu.VMEM),
+            scratch_shapes=[
+                pltpu.VMEM((2, D, FF), jnp.bfloat16),
+                pltpu.SemaphoreType.DMA((2,)),
+            ],
+        ),
+        compiler_params=pltpu.CompilerParams(vmem_limit_bytes=40 * 2**20),
+    )(slot_of, *matrices)
+
+
+def take_rows(source, index_at, kind):
+    count, width, block = (index_at.shape[0], source.shape[1], 128)
+    whole = -(-count // block) * block
+    index_at = jnp.pad(index_at, (0, whole - count))
+
+    def kernel(index_ref, source_ref, out_ref, held_ref):
+        first = pl.program_id(0) * block
+
+        def copy_eight(group, carry):
+            base = pl.multiple_of(group * 8, 8)
+            for row_no in range(8):
+                held_ref[pl.ds(base + row_no, 1), :] = source_ref[
+                    pl.ds(index_ref[first + base + row_no], 1), :
+                ]
+            return carry
+
+        lax.fori_loop(0, block // 8, copy_eight, 0)
+        out_ref[...] = held_ref[...].astype(kind)
+
+    taken = pl.pallas_call(
+        kernel,
+        out_shape=jax.ShapeDtypeStruct((whole, width), kind),
+        grid_spec=pltpu.PrefetchScalarGridSpec(
+            num_scalar_prefetch=1,
+            grid=(whole // block,),
+            in_specs=[pl.BlockSpec(memory_space=pltpu.VMEM)],
+            out_specs=pl.BlockSpec((block, width), lambda step, index: (step, 0)),
+            scratch_shapes=[pltpu.VMEM((block, width), jnp.float32)],
+        ),
+        compiler_params=pltpu.CompilerParams(vmem_limit_bytes=40 * 2**20),
+    )(index_at, source)
+    return taken[:count]
+
+
+def add_rows(rows, index_at, total):
+    count, width, block = (rows.shape[0], rows.shape[1], 512)
+    whole = -(-count // block) * block
+    index_at = jnp.pad(index_at, (0, whole - count), constant_values=-1)[None, :]
+    rows = jnp.pad(rows, ((0, whole - count), (0, 0)))
+    height = total.shape[0]
+
+    def kernel(index_ref, rows_ref, total_ref, out_ref):
+        @pl.when(pl.program_id(0) == 0)
+        def _():
+            out_ref[...] = total_ref[...]
+
+        hits = lax.broadcasted_iota(jnp.int32, (height, block), 0) == index_ref[...]
+        out_ref[...] += jnp.dot(
+            hits.astype(jnp.float32).astype(jnp.bfloat16),
+            rows_ref[...],
+            preferred_element_type=jnp.float32,
+        )
+
+    return pl.pallas_call(
+        kernel,
+        out_shape=jax.ShapeDtypeStruct(total.shape, jnp.float32),
+        grid=(whole // block,),
+        in_specs=[
+            pl.BlockSpec((1, block), lambda step: (0, step)),
+            pl.BlockSpec((block, width), lambda step: (step, 0)),
+            pl.BlockSpec((height, width), lambda step: (0, 0)),
+        ],
+        out_specs=pl.BlockSpec((height, width), lambda step: (0, 0)),
+        compiler_params=pltpu.CompilerParams(vmem_limit_bytes=40 * 2**20),
+    )(index_at, rows, total)
+
+
+def count_before(mask):
+    size, width = (mask.shape[-1], 128)
+    parts = mask.reshape(*mask.shape[:-1], size // width, width).astype(jnp.bfloat16)
+    earlier = (jnp.arange(width)[:, None] < jnp.arange(width)[None, :]).astype(jnp.bfloat16)
+    inside = jnp.einsum("...pw,wk->...pk", parts, earlier, preferred_element_type=jnp.float32)
+    totals = jnp.sum(parts.astype(jnp.float32), axis=-1)
+    ahead = jnp.cumsum(totals, axis=-1) - totals
+    return (inside + ahead[..., None]).reshape(mask.shape).astype(jnp.int32)
+
+
+def room(count, peers):
+    mean = count / peers
+    return min(count, -(-int(mean + 5.0 * math.sqrt(mean)) // 16) * 16)
+
+
+def listed(mask, rank, values, size, empty):
+    spot = jnp.arange(size)[:, None]
+    chosen = mask[..., None, :] & (rank[..., None, :] == spot)
+    return jnp.sum(jnp.where(chosen, values[..., None, :] - empty, 0), axis=-1) + empty
+
+
+def rounds_needed(owner_all, peers, size):
+    held = jnp.sum((owner_all[:, None, :] == jnp.arange(peers)[:, None]).astype(jnp.int32), axis=2)
+    return (jnp.max(held) + size - 1) // size
+
+
+def fetch_rows(table_part, tokens_all, peers_here, peer_me):
+    peers, rows_each = (peers_here.shape[0], table_part.shape[0])
+    count = tokens_all.shape[1]
+    size = room(count, peers)
+    asked = peers_here // rows_each == peer_me
+    asked_rank = count_before(asked)
+    own_tokens = lax.dynamic_index_in_dim(peers_here, peer_me, 0, keepdims=False)
+    own_owner = own_tokens // rows_each
+    own_mask = own_owner[None, :] == jnp.arange(peers)[:, None]
+    own_rank = jnp.sum(jnp.where(own_mask, count_before(own_mask), 0), axis=0)
+
+    def one_round(round_no):
+        wanted = listed(
+            asked, asked_rank - round_no * size, peers_here - peer_me * rows_each, size, 0
+        )
+        rows = take_rows(table_part, wanted.reshape(-1), jnp.bfloat16)
+        arrived = lax.all_to_all(rows, "vocab", 0, 0, tiled=True)
+        rank_now = own_rank - round_no * size
+        now = (rank_now >= 0) & (rank_now < size)
+        found = take_rows(
+            arrived.astype(jnp.float32), jnp.where(now, own_owner * size + rank_now, 0), jnp.float32
+        )
+        return (now, found)
+
+    def again(round_no, rows):
+        now, found = one_round(round_no)
+        return jnp.where(now[:, None], found, rows)
+
+    rounds = rounds_needed(tokens_all // rows_each, peers, size)
+    return lax.fori_loop(1, rounds, again, one_round(0)[1])
+
+
+def return_rows(grad_rows, tokens_all, rows_each, dp_size, total):
+    peers, count = tokens_all.shape
+    along = peers // dp_size
+    quarter = rows_each // dp_size
+    me = lax.axis_index("dp") * along + lax.axis_index("vocab")
+    size = room(count, peers)
+    owner_all = (tokens_all % rows_each) // quarter * along + tokens_all // rows_each
+    arriving = owner_all == me
+    arriving_rank = count_before(arriving)
+    own_owner = lax.dynamic_index_in_dim(owner_all, me, 0, keepdims=False)
+    leaving = own_owner[None, :] == jnp.arange(peers)[:, None]
+    leaving_rank = count_before(leaving)
+    place = jnp.broadcast_to(jnp.arange(count)[None, :], leaving.shape)
+
+    def one_round(round_no, so_far):
+        chosen = listed(leaving, leaving_rank - round_no * size, place, size, 0)
+        rows = take_rows(grad_rows, chosen.reshape(-1), jnp.bfloat16)
+        arrived = lax.all_to_all(rows, ("dp", "vocab"), 0, 0, tiled=True)
+        where = listed(
+            arriving, arriving_rank - round_no * size, tokens_all % quarter, size, -1
+        )
+        return add_rows(arrived, where.reshape(-1), so_far)
+
+    rounds = rounds_needed(owner_all, peers, size)
+    return lax.fori_loop(1, rounds, one_round, one_round(0, total))
 
 
 def turn_in(left_basis, tiles, right_basis):
@@ -413,16 +620,56 @@
     return jnp.einsum("til,tjl->tij", half, right_basis, precision=HIGHEST)
 
 
-def solve_lower(lower_tri, right_side):
-    return jax.scipy.linalg.solve_triangular(lower_tri, right_side, lower=True)
-
-
-def renew_basis(statistic, basis):
-    moved = jnp.einsum("tij,tjk->tik", statistic, basis, precision=HIGHEST)
-    gram = jnp.einsum("tki,tkj->tij", moved, moved, precision=HIGHEST)
-    lower_tri = jnp.linalg.cholesky(gram)
-    solved = jax.vmap(solve_lower)(lower_tri, jnp.swapaxes(moved, 1, 2))
-    return jnp.swapaxes(solved, 1, 2)
+def orthonormal(columns):
+    lanes, group = (128, 4)
+
+    def kernel(in_ref, out_ref):
+        out_ref[...] = in_ref[...]
+
+        def one_column(column_no, carry):
+            pivot = out_ref[column_no]
+            pivot = pivot / jnp.sqrt(jnp.sum(pivot * pivot, axis=0, keepdims=True))
+            out_ref[column_no] = pivot
+
+            def one_group(group_no, inner):
+                first = group_no * group
+                held = [out_ref[first + item] for item in range(group)]
+                for item in range(group):
+                    share = jnp.sum(pivot * held[item], axis=0, keepdims=True)
+                    share = jnp.where(first + item > column_no, share, 0.0)
+                    held[item] = held[item] - share * pivot
+                for item in range(group):
+                    out_ref[first + item] = held[item]
+                return inner
+
+            return lax.fori_loop((column_no + 1) // group, PB // group, one_group, carry)
+
+        lax.fori_loop(0, PB, one_column, 0)
+
+    spec = pl.BlockSpec((PB, PB, lanes), lambda step: (0, 0, step))
+    return pl.pallas_call(
+        kernel,
+        out_shape=jax.ShapeDtypeStruct(columns.shape, jnp.float32),
+        grid=(columns.shape[2] // lanes,),
+        in_specs=[spec],
+        out_specs=spec,
+        compiler_params=pltpu.CompilerParams(vmem_limit_bytes=40 * 2**20),
+    )(columns)
+
+
+def renew_bases(left_stat, right_stat, left_basis, right_basis):
+    moved = jnp.concatenate(
+        [
+            jnp.einsum("tij,tjk->tik", left_stat, left_basis, precision=HIGHEST),
+            jnp.einsum("tij,tjk->tik", right_stat, right_basis, precision=HIGHEST),
+        ],
+        0,
+    )
+    count = moved.shape[0]
+    whole = -(-count // 128) * 128
+    columns = jnp.pad(jnp.transpose(moved, (2, 1, 0)), ((0, 0), (0, 0), (0, whole - count)))
+    renewed = jnp.transpose(orthonormal(columns)[:, :, :count], (2, 1, 0))
+    return (renewed[: count // 2], renewed[count // 2 :])
 
 
 def soap_update(
@@ -452,8 +699,7 @@
         second_new,
         left_new,
         right_new,
-        renew_basis(left_new, left_basis),
-        renew_basis(right_new, right_basis),
+        *renew_bases(left_new, right_new, left_basis, right_basis),
     )
 
 
@@ -490,76 +736,130 @@
     exit_layer,
     slot_list,
 ):
-    counted = loss_place < target_len[:, :, None]
-    local_counts = jnp.stack(
-        [jnp.sum(counted.astype(jnp.float32))]
-        + [
-            jnp.sum((counted & (exit_layer >= layer_no)).astype(jnp.float32))
-            for layer_no in range(DEC)
-        ]
-    )
-    global_counts = lax.psum(local_counts, ("dp", "vocab"))
-    count_all = global_counts[0]
-    fraction = global_counts[1:] / jnp.sum(global_counts[1:])
+    dp_size, along = (lax.axis_size("dp"), lax.axis_size("vocab"))
+    dp_me, peer_me = (lax.axis_index("dp"), lax.axis_index("vocab"))
+    devices = dp_size * along
+    rows_each = table_master.shape[0]
+    quarter = rows_each // dp_size
+    source_len, target_len = (source_len[:, 0], target_len[:, 0])
+
+    shifted = jnp.pad(target_ids[:, 0, :-1], ((0, 0), (1, 0)))
+    tokens = jnp.concatenate([source_ids.reshape(-1), shifted.reshape(-1)])
+    places = loss_place[:, 0]
+    counted = places < target_len[:, None]
+    reach = [
+        jnp.sum((counted & (exit_layer[:, 0] >= layer_no)).astype(jnp.int32))
+        for layer_no in range(DEC)
+    ]
+    labels = jnp.take_along_axis(target_ids[:, 0], places, axis=1).reshape(-1)
+    row_count = MICRO * LOSS_POS
+    own_facts = jnp.concatenate(
+        [tokens, labels, counted.reshape(-1).astype(jnp.int32), jnp.stack(reach)]
+    )
+    fact_count = own_facts.shape[0]
+    own_facts = jnp.pad(own_facts, (0, -fact_count % 128))
+    facts = lax.all_gather(own_facts, ("dp", "vocab"), axis=0, tiled=False)
+    tokens_all = facts[:, : tokens.shape[0]]
+    after = facts[:, tokens.shape[0] :]
+    labels_all = after[:, :row_count]
+    counted_all = after[:, row_count : 2 * row_count].astype(jnp.float32)
+    reach_all = jnp.sum(after[:, 2 * row_count : 2 * row_count + DEC].astype(jnp.float32), axis=0)
+    count_all = jnp.sum(counted_all)
+    fraction = reach_all / jnp.sum(reach_all)
+
     every_tile = lax.all_gather(
-        master_tiles.astype(jnp.bfloat16), ("dp", "vocab"), axis=0, tiled=True
-    )
-    weights = untile(jnp.zeros_like(every_tile).at[slot_list].set(every_tile))
-    table_used = table_master.astype(jnp.bfloat16)
-    table_full = lax.all_gather(table_used, "vocab", axis=0, tiled=True)
+        fold_blocks(master_tiles).astype(jnp.bfloat16), ("dp", "vocab"), axis=0, tiled=True
+    )
+    slot_at = jnp.arange(slot_list.shape[0])
+    slot_of = jnp.sum(
+        jnp.where(slot_list[None, :] == slot_at[:, None], slot_at[None, :], 0), axis=1
+    )
+    peers_here = lax.dynamic_slice_in_dim(tokens_all, dp_me * along, along, 0)
+    embedded = fetch_rows(table_master, tokens_all, peers_here, peer_me) * math.sqrt(D)
+    src_count, tgt_count = (source_ids.shape[2], target_ids.shape[2])
+    wave_set = waves(src_count, D)
+    source_rows = embedded[: MICRO * src_count] + jnp.tile(wave_set, (MICRO, 1))
+    target_rows = embedded[MICRO * src_count :] + jnp.tile(wave_set[:tgt_count], (MICRO, 1))
+    weights = lay_matrices(every_tile, slot_of)
+
+    place_rows = (places + jnp.arange(MICRO)[:, None] * tgt_count).reshape(-1)
+    kept, exit_rows = forward_all(
+        weights, gains, source_rows, target_rows, source_len, target_len, place_rows
+    )
+
+    table_low_part = table_master.astype(jnp.bfloat16)
+    exit_count = DEC * row_count
+    exit_all = lax.all_gather(exit_rows, ("dp", "vocab"), axis=0, tiled=True)
+    label_rows = jnp.tile(labels_all, (1, DEC)).reshape(-1)
+    weight_rows = (
+        jnp.repeat(fraction, row_count)[None, :] * jnp.tile(counted_all, (1, DEC))
+    ).reshape(-1)
+    group_rows = along * exit_count
+    group_at = dp_me * group_rows
+    exit_here = lax.dynamic_slice_in_dim(exit_all, group_at, group_rows, 0)
+    label_here = lax.dynamic_slice_in_dim(label_rows, group_at, group_rows, 0)
+    weight_here = lax.dynamic_slice_in_dim(weight_rows, group_at, group_rows, 0)
+    logits = linear_tr(exit_here, table_low_part)
+    hit_here = label_here[:, None] - peer_me * rows_each == jnp.arange(rows_each)[None, :]
+    summit = jnp.max(logits, axis=1)
+    spread_part = jnp.sum(jnp.exp(logits - summit[:, None]), axis=1)
+    picked_part = jnp.sum(jnp.where(hit_here, logits, 0.0), axis=1)
+    stats = lax.all_gather(
+        jnp.stack([summit, spread_part, picked_part]), ("dp", "vocab"), axis=0, tiled=False
+    ).reshape(dp_size, along, 3, group_rows)
+    summit_all = jnp.max(stats[:, :, 0], axis=1)
+    total_all = jnp.sum(stats[:, :, 1] * jnp.exp(stats[:, :, 0] - summit_all[:, None]), axis=1)
+    spread_all = summit_all + jnp.log(total_all)
+    picked_all = jnp.sum(stats[:, :, 2], axis=1)
+    loss_sum = jnp.sum(weight_rows * (spread_all - picked_all).reshape(-1))
+    spread_here = lax.dynamic_index_in_dim(spread_all, dp_me, 0, keepdims=False)
+
+    def logit_grads(logit_set, spread, weight_set, hits):
+        return (
+            (weight_set / count_all)[:, None]
+            * (jnp.exp(logit_set - spread[:, None]) - hits.astype(jnp.float32))
+        ).astype(jnp.bfloat16)
+
+    grads_here = logit_grads(logits, spread_here, weight_here, hit_here)
+    grad_parts = linear(grads_here, table_low_part).astype(jnp.bfloat16)
+    grad_parts = lax.all_to_all(grad_parts, "vocab", 0, 0, tiled=True)
+    exit_grads = jnp.sum(
+        grad_parts.reshape(along, exit_count, D).astype(jnp.float32), axis=0
+    )
+
     matrix_store = [None] * MATS
     gain_store = [None] * GAINS
-    grad_table = jnp.zeros(table_full.shape, jnp.float32)
-    loss_part = jnp.zeros((), jnp.float32)
-    for micro_no in range(MICRO):
-        rows_all = [[] for layer_no in range(DEC)]
-        seq_no = 0
-        kept_seq, exit_rows = forward_sequence(
-            weights,
-            gains,
-            table_full,
-            source_ids[micro_no, seq_no],
-            target_ids[micro_no, seq_no],
-            source_len[micro_no, seq_no],
-            target_len[micro_no, seq_no],
-            loss_place[micro_no, seq_no],
-        )
-        kept_all = [kept_seq]
-        for layer_no in range(DEC):
-            rows_all[layer_no].append(exit_rows[layer_no])
-        rows_send = jnp.stack([jnp.concatenate(rows_all[layer_no], 0) for layer_no in range(DEC)])
-        labels = target_ids[micro_no, 0][loss_place[micro_no, 0]]
-        valid_rows = counted[micro_no].reshape(-1).astype(jnp.int32)
-        grad_logits, row_loss = exit_head(
-            rows_send, labels, valid_rows, table_full, 0, fraction, count_all, local_stats
-        )
-        grad_exit = jnp.einsum(
-            "erv,vd->erd", grad_logits, table_full, preferred_element_type=jnp.float32
-        )
-        grad_table = grad_table + jnp.einsum(
-            "erv,erd->vd", grad_logits, rows_send, preferred_element_type=jnp.float32
-        )
-        loss_part = loss_part + jnp.sum(row_loss)
-        seq_no = 0
-        exit_grads = [
-            grad_exit[layer_no, seq_no * LOSS_POS : (seq_no + 1) * LOSS_POS]
-            for layer_no in range(DEC)
-        ]
-        grad_table = backward_sequence(
-            weights, gains, kept_all[seq_no], exit_grads, grad_table, matrix_store, gain_store
-        )
-    reduced = lax.psum_scatter(grad_table, "vocab", scatter_dimension=0, tiled=True)
-    table_grad = lax.psum(reduced, "dp")
-    tiles_grad = tile_up(jnp.stack(matrix_store))[slot_list]
-    owned_grad = lax.psum_scatter(tiles_grad, ("dp", "vocab"), scatter_dimension=0, tiled=True)
-    squares = jnp.sum(owned_grad * owned_grad) + jnp.sum(table_grad * table_grad) / lax.axis_size(
-        "dp"
-    )
-    gain_total, square_total, loss_sum = lax.psum(
-        (jnp.stack(gain_store), squares, loss_part), ("dp", "vocab")
-    )
+    grad_source, grad_target = backward_all(
+        weights, gains, kept, exit_grads, matrix_store, gain_store
+    )
+
+    first_row = peer_me * rows_each + dp_me * quarter
+    table_quarter = lax.dynamic_slice_in_dim(table_low_part, dp_me * quarter, quarter, 0)
+    hit_quarter = label_rows[:, None] - first_row == jnp.arange(quarter)[None, :]
+    grads_quarter = logit_grads(
+        linear_tr(exit_all, table_quarter), spread_all.reshape(-1), weight_rows, hit_quarter
+    )
+    grad_quarter = outer_sum(grads_quarter, exit_all)
+    grad_rows = jnp.concatenate([grad_source, grad_target], 0) * math.sqrt(D)
+    grad_quarter = return_rows(grad_rows, tokens_all, rows_each, dp_size, grad_quarter)
+
+    owned_grad = unfold_blocks(
+        lax.psum_scatter(
+            lax.psum_scatter(
+                fold_gradients(matrix_store, slot_of), "dp", scatter_dimension=0, tiled=True
+            ),
+            "vocab",
+            scatter_dimension=0,
+            tiled=True,
+        ).astype(jnp.float32)
+    )
+    squares = jnp.sum(owned_grad * owned_grad) + jnp.sum(grad_quarter * grad_quarter)
+    gain_total, square_total = lax.psum((jnp.stack(gain_store), squares), ("dp", "vocab"))
     grad_norm = jnp.sqrt(square_total + jnp.sum(gain_total * gain_total))
     factor = jnp.minimum(1.0, CLIP_AT / grad_norm)
+    table_grad = lax.all_gather(
+        grad_quarter.astype(jnp.bfloat16), "dp", axis=0, tiled=True
+    ).astype(jnp.float32)
     master_new, mom1_new, mom2_new, left_new, right_new, bleft_new, bright_new = soap_update(
         master_tiles,
         owned_grad * factor,

time: 5170 us -> 1660 us (0.32)
  other arithmetic: 1710 us -> 283 us
  waiting for transfers between devices: 1590 us -> 324 us
  local copies, waits for them, and re-layouts: 1050 us -> 169 us
  Pallas kernels: 0 us -> 170 us
  matrix products: 681 us -> 534 us
    another operation x11 -> x5, other arithmetic: 1180 us -> 1.01 us  [the longest x4 0.7 us: count_before(): ahead = jnp.cumsum(totals, axis=-1) - totals]
    reduce_scatter x2, waiting for transfers between devices: 1230 us -> 144 us  [the longest x1 90.2 us: per_device(): lax.psum_scatter(fold_gradients(matrix_store, slot_of), 'dp', scatter_dim...]
    scatter x1 -> x0, local copies, waits for them, and re-layouts: 364 us -> none  [per_device(): weights = untile(jnp.zeros_like(every_tile).at[slot_list].set(every_tile))]
    scatter-add x8 -> x2, other arithmetic: 313 us -> 3.52 us  [backward_all(): grad_decoded = grad_decoded.at[place_rows].add(grad_rows)]
    pallas_call x0 -> x7, Pallas kernels: none -> 170 us  [the longest x3 49.8 us: take_rows(): pl.pallas_call(kernel, out_shape=jax.ShapeDtypeStruct((whole, width), kin...]
    psum x1 -> x0, waiting for transfers between devices: 169 us -> none  [per_device(): table_grad = lax.psum(reduced, 'dp')]
    all_gather x2 -> x3, waiting for transfers between devices: 183 us -> 21 us  [the longest x1 21 us: per_device(): exit_all = lax.all_gather(exit_rows, ('dp', 'vocab'), axis=0, tiled=True)]
    all_to_all x0 -> x3, waiting for transfers between devices: none -> 159 us  [the longest x1 105 us: one_round(): arrived = lax.all_to_all(rows, 'vocab', 0, 0, tiled=True)]
  transfers between devices with their start and end apart: 5 -> 8, of which waited for: 4 -> 6; matrix products, arithmetic and copies ran while one was open for 18% -> 17% of each run, Pallas kernels for 0% -> 6%
where the time goes in v1:
time: 1660 us; the launch traced here: 1650 us
  matrix products  534 us (32%)
  waiting for transfers between devices  324 us (20%)
  other arithmetic  283 us (17%)
  Pallas kernels  170 us (10%)
  local copies, waits for them, and re-layouts  169 us (10%)
  blocking collectives  127 us (8%)
  between operations  24.8 us (1%)
    unnamed x872, local copies, waits for them, and re-layouts  112 us
    all_to_all x1, waiting for transfers between devices, one_round(): arrived = lax.all_to_all(rows, 'vocab', 0, 0, tiled=True)  105 us
    dot_general x19, matrix products, outer_sum(): lax.dot_general(left_op, right_op, (((0,), (0,)), ((), ())), preferred_el...  90.4 us
    reduce_scatter x1, waiting for transfers between devices, per_device(): lax.psum_scatter(fold_gradients(matrix_store, slot_of), 'dp', scatter_dim...  90.2 us
    dot_general x19, matrix products, linear(): return jnp.dot(left_op, right_op, preferred_element_type=jnp.float32)  73.5 us
    dot_general x19, matrix products, linear_tr(): lax.dot_general(left_op, right_op, (((1,), (1,)), ((), ())), preferred_el...  71.2 us
    dot_general x12, matrix products, attend_backward(): jnp.einsum('qhd,khd->hqk', upstream, value_heads, preferred_element_type=...  66.7 us
    convert_element_type x12, other arithmetic, attend_backward(): grad_scores = (probs_f * (grad_probs - inner_sum)).astype(jnp.bfloat16)  56.1 us
  transfers between devices with their start and end apart: 8, of which 6 were waited for; matrix products, arithmetic and copies ran while one was open for 17% of the time, Pallas kernels for 6%

profile of v1, /device:TPU:0, one launch (start us, length us, event | category | flops | bytes accessed | tf_op | source)
XLA Modules:
  0.0 1652.1 jit_solution(11897892570776795277)
XLA Ops:
  17.5 47.5 %all-gather.2 = s32[32,1,2688]{2,1,0:T(1,128)S(1)} all-gather(s32[1,1,2688]{2,1,0:T(1,128)S(1)} %reshape.1369), channel_id=2, replica_groups=mesh['dp'=4,'vocab'=8] {'dp','vocab'}, dimensions={0}, use_global_device_ids=true | all-gather | bytes 354816 | tf_op jit(solution)/shard_map/all_gather | solution.py:761
  76.9 19.4 %shard_map.331 = bf16[3328,512]{1,0:T(8,128)(2,1)} custom-call(s32[3328]{0:T(1024)S(1)} %reshape.1230.index_ref, f32[4096,512]{1,0:T(8,128)} %source_ref.1), custom_call_target="tpu_custom_call" | custom-call | tf_op jit(solution)/shard_map/pallas_call | solution.py:480
  124.9 104.7 %all-to-all-done.2 = bf16[8,416,512]{2,1,0:T(8,128)(2,1)S(1)} async-done(((bf16[8,416,512]{2,1,0:T(8,128)(2,1)}), bf16[8,416,512]{2,1,0:T(8,128)(2,1)S(1)}, u32[]{:S(2)}, u32[]{:S(2)}) %all-to-all-start.2) | async-done | bytes 3407904 | tf_op jit(solution)/shard_map/all_to_all | solution.py:570
  230.9 13.1 shard_map.332
  250.4 47.3 %shard_map.333 = bf16[11,512,2048]{2,1,0:T(8,128)(2,1)} custom-call(s32[2816]{0:T(1024)S(1)} %select_reduce_fusion.5.slot_ref, bf16[2816,32,128]{2,1,0:T(8,128)(2,1)} %all-gather.8.cloned.1.call-done.folded_ref), custom_call_target="tpu_custom_call" | custom-call | tf_op jit(solution)/shard_map/pallas_call | solution.py:396
  394.7 10.6 fusion.107
  405.3 10.2 multiply_reduce_fusion.14
  537.1 21.0 %all-gather.10.cloned.1.call-done = bf16[2048,512]{1,0:T(8,128)(2,1)} async-done(((bf16[64,512]{1,0:T(8,128)(2,1)}), bf16[2048,512]{1,0:T(8,128)(2,1)}) %all-gather.10.cloned.1.call-update) | async-done | bytes 2097168 | tf_op jit(solution)/shard_map/all_gather | solution.py:792
  565.8 40.4 %all-gather.3 = f32[32,3,512]{2,1,0:T(4,128)S(1)} all-gather(f32[1,3,512]{2,1,0:T(4,128)S(1)} %maximum_bitcast_fusion.1), channel_id=3, replica_groups=mesh['dp'=4,'vocab'=8] {'dp','vocab'}, dimensions={0}, use_global_device_ids=true | all-gather | bytes 202752 | tf_op jit(solution)/shard_map/all_gather | solution.py:807
  751.4 19.1 %fusion.19 = bf16[2048,2048]{1,0:T(8,128)(2,1)} fusion(f32[2048,2048]{1,0:T(8,128)} %fusion.107, bf16[11,512,2048]{2,1,0:T(8,128)(2,1)} %shard_map.333, f32[2048,512]{1,0:T(8,128)S(1)} %add_add_fusion.2), kind=kOutput, calls=%fused_computation.51 | convolution fusion | flops 4379901952 | bytes 31457280 | tf_op jit(solution)/shard_map/dot_general | solution.py:52
  800.4 10.0 fusion.33
  810.5 13.4 multiply_reduce_fusion.2
  823.9 9.5 multiply_reduce_fusion.1
  854.4 16.0 multiply_reduce_fusion.3
  915.1 18.0 %convolution_convert_fusion.16 = bf16[512,1024]{1,0:T(8,128)(2,1)} fusion(bf16[2048,512]{1,0:T(8,128)(2,1)S(1)} %copy-done.163, bf16[1024,512]{0,1:T(8,128)(2,1)S(1)} %bitcast.811, bf16[1024,512]{0,1:T(8,128)(2,1)S(1)} %bitcast.813, bf16[1024,512]{0,1:T(8,128)(2,1)S(1)} %bitcast.682, bf16[1024,512]{0,1:T(8,128)(2,1)S(1)} %bitcast.684), kind=kOutput, calls=%fused_computation.331 | convolution fusion | flops 2164785152 | bytes 7340032 | tf_op jit(solution)/shard_map/dot_general | solution.py:62
  935.9 18.4 %convolution_convert_fusion.15 = bf16[512,1024]{1,0:T(8,128)(2,1)} fusion(bf16[2048,512]{1,0:T(8,128)(2,1)S(1)} %copy-done.163, bf16[1024,512]{0,1:T(8,128)(2,1)S(1)} %bitcast.807, bf16[1024,512]{0,1:T(8,128)(2,1)S(1)} %bitcast.809, bf16[1024,512]{0,1:T(8,128)(2,1)S(1)} %bitcast.678, bf16[1024,512]{0,1:T(8,128)(2,1)S(1)} %bitcast.680), kind=kOutput, calls=%fused_computation.330 | convolution fusion | flops 2164785152 | bytes 7340032 | tf_op jit(solution)/shard_map/dot_general | solution.py:62
  966.7 11.3 convolution_convert_fusion.9.refs_8_
  1002.1 10.5 multiply_convert_fusion
  1020.6 11.8 multiply_convert_fusion.2
  1036.8 34.3 %maximum_maximum_fusion = bf16[2048,1536]{0,1:T(8,128)(2,1)S(1)} fusion(bf16[1024,512]{0,1:T(8,128)(2,1)S(1)} %bitcast.605, bf16[1024,512]{0,1:T(8,128)(2,1)S(1)} %bitcast.606, bf16[1024,512]{0,1:T(8,128)(2,1)S(1)} %bitcast.587, bf16[1024,512]{0,1:T(8,128)(2,1)S(1)} %bitcast.588, bf16[512,512]{0,1:T(8,128)(2,1)S(1)} %bitcast.657, ...), kind=kLoop, calls=%fused_computation.143 | loop fusion | flops 50331648 | bytes 12582912 | tf_op jit(solution)/shard_map/concatenate | solution.py:218
  1081.5 23.2 %shard_map.334 = bf16[2816,32,128]{2,1,0:T(8,128)(2,1)} custom-call(s32[2816]{0:T(1024)S(1)} %select_reduce_fusion.5.slot_ref, bf16[512,2048]{1,0:T(8,128)(2,1)S(1)} %pad_maximum_fusion.3.refs_0_, bf16[512,2048]{1,0:T(8,128)(2,1)S(1)} %pad_maximum_fusion.4.refs_1_, bf16[512,2048]{1,0:T(8,128)(2,1)S(1)} %pad_maximum_fusion.5.refs_2_, ...), custom_call_target="tpu_custom_call" | custom-call | tf_op jit(solution)/shard_map/pallas_call | solution.py:444
  1107.1 12.9 select_reduce_fusion.2
  1135.1 17.2 %shard_map.335 = bf16[4096,512]{1,0:T(8,128)(2,1)S(1)} custom-call(s32[4096]{0:T(1024)S(1)} %bitcast.539, f32[2560,512]{1,0:T(8,128)S(1)} %maximum_multiply_fusion.source_ref), custom_call_target="tpu_custom_call" | custom-call | tf_op jit(solution)/shard_map/pallas_call | solution.py:480
  1186.2 12.2 select_reduce_fusion.3
  1207.2 46.1 %all-to-all-done.4 = bf16[32,128,512]{2,1,0:T(8,128)(2,1)} async-done(((bf16[32,128,512]{2,1,0:T(8,128)(2,1)}), bf16[32,128,512]{2,1,0:T(8,128)(2,1)}, u32[]{:S(2)}, u32[]{:S(2)}) %all-to-all-start.4) | async-done | bytes 4194336 | tf_op jit(solution)/shard_map/all_to_all | solution.py:603
  1262.6 90.2 %reduce-scatter.3.cloned.1.call-done = bf16[704,32,128]{2,1,0:T(8,128)(2,1)} async-done(((bf16[2816,32,128]{2,1,0:T(8,128)(2,1)}), bf16[704,32,128]{2,1,0:T(8,128)(2,1)}) %reduce-scatter.3.cloned.1.call-update) | async-done | bytes 5767184 | tf_op jit(solution)/shard_map/reduce_scatter | solution.py:848
  1366.4 53.6 %reduce-scatter.5.cloned.1.call-done = bf16[88,32,128]{2,1,0:T(8,128)(2,1)} async-done(((bf16[704,32,128]{2,1,0:T(8,128)(2,1)}), bf16[88,32,128]{2,1,0:T(8,128)(2,1)}) %reduce-scatter.5.cloned.1.call-update) | async-done | bytes 720912 | tf_op jit(solution)/shard_map/reduce_scatter | solution.py:847
  1424.5 38.6 %all-reduce.3 = (f32[]{:T(128)}, f32[11,512]{1,0:T(8,128)S(1)}) all-reduce(f32[]{:T(128)S(6)} %add.726, f32[11,512]{1,0:T(8,128)S(1)} %stack.38), channel_id=1, replica_groups=mesh['dp'=4,'vocab'=8] {'dp','vocab'}, use_global_device_ids=true, to_apply=%region_101.102 | all-reduce | flops 5633 | bytes 45064 | tf_op jit(solution)/shard_map/psum | solution.py:857
  1520.0 10.2 multiply_add_fusion.2
  1534.2 10.0 multiply_add_fusion.1
  1573.7 40.5 %shard_map.337 = f32[64,64,256]{2,1,0:T(8,128)S(1)} custom-call(f32[64,64,256]{2,1,0:T(8,128)S(1)} %pad.14.in_ref), custom_call_target="tpu_custom_call" | custom-call | tf_op jit(solution)/shard_map/pallas_call | solution.py:650
  1621.1 23.1 %fusion.357 = (bf16[4096,512]{1,0:T(8,128)(2,1)}, f32[4096,512]{1,0:T(8,128)}, f32[4096,512]{1,0:T(8,128)}, f32[4096,512]{1,0:T(8,128)}) fusion(f32[4096,512]{1,0:T(8,128)} %get-tuple-element.906, f32[]{:T(128)S(6)} %min.3, bf16[4096,512]{1,0:T(8,128)(2,1)} %all-gather.12.cloned.1.call-done, f32[4096,512]{1,0:T(8,128)} %param.32, f32[4096,512]{1,0:T(8,128)} %param.33), kind=kLoop, calls=%fused_computation.748 | loop fusion | flops 37748736 | bytes 58720260 | tf_op jit(solution)/shard_map/convert_element_type | solution.py:892
  (1251 shorter events, 763.1 us)
Async XLA Ops:
  7.2 243.2 %all-gather.8.cloned.1.call-start = ((), (), s32[]{:S(2)}) async-start(), calls=%async_computation.7 | async-start | bytes 23789568 | tf_op jit(solution)/shard_map/all_gather | solution.py:770
  96.3 133.3 %all-to-all-start.2 = ((bf16[8,416,512]{2,1,0:T(8,128)(2,1)}), bf16[8,416,512]{2,1,0:T(8,128)(2,1)S(1)}, u32[]{:S(2)}, u32[]{:S(2)}) async-start(bf16[8,416,512]{2,1,0:T(8,128)(2,1)} %bitcast.11), calls=%async_computation.2 | async-start | bytes 6815744 | tf_op jit(solution)/shard_map/all_to_all | solution.py:570
  100.2 457.9 %all-gather.10.cloned.1.call-start = ((), (), s32[]{:S(2)}) async-start(), calls=%async_computation.8 | async-start | bytes 2162688 | tf_op jit(solution)/shard_map/all_gather | solution.py:792
  109.9 214.8 %copy-start.253 = (pred[1024]{0:T(1024)(128)(4,1)}, pred[1024]{0:T(1024)(128)(4,1)S(1)}, u32[]{:S(2)}) copy-start(pred[1024]{0:T(1024)(128)(4,1)S(1)} %iota_compare_fusion.19) | copy-start | bytes 3076
  247.7 64.4 %copy-start.72 = (f32[512,512]{1,0:T(8,128)}, f32[512,512]{1,0:T(8,128)S(1)}, u32[]{:S(2)}) copy-start(f32[512,512]{1,0:T(8,128)S(1)} %get-tuple-element.500) | copy-start | bytes 3145732
  250.3 47.4 %copy-start.269 = (f32[2048]{0:T(1024)}, f32[2048]{0:T(1024)S(1)}, u32[]{:S(2)}) copy-start(f32[2048]{0:T(1024)S(1)} %get-tuple-element.497) | copy-start | bytes 24580
  250.3 61.8 %copy-start.350 = (f32[512]{0:T(512)}, f32[512]{0:T(512)S(1)}, u32[]{:S(2)}) copy-start(f32[512]{0:T(512)S(1)} %fusion.298) | copy-start | bytes 6148
  250.3 54.6 %copy-start.290 = (f32[2048]{0:T(1024)}, f32[2048]{0:T(1024)S(1)}, u32[]{:S(2)}) copy-start(f32[2048]{0:T(1024)S(1)} %fusion.293) | copy-start | bytes 24580
  310.7 48.7 %copy-start.32 = (bf16[1024,512]{0,1:T(8,128)(2,1)}, bf16[1024,512]{0,1:T(8,128)(2,1)S(1)}, u32[]{:S(2)}) copy-start(bf16[1024,512]{0,1:T(8,128)(2,1)S(1)} %get-tuple-element.517) | copy-start | bytes 3145732
  341.6 49.6 %copy-start.391 = (bf16[8,64,512]{2,1,0:T(8,128)(2,1)}, bf16[8,64,512]{2,1,0:T(8,128)(2,1)S(1)}, u32[]{:S(2)}) copy-start(bf16[8,64,512]{2,1,0:T(8,128)(2,1)S(1)} %fusion.157) | copy-start | bytes 1572868
  356.7 34.6 %copy-start.393 = (bf16[8,64,512]{2,1,0:T(8,128)(2,1)}, bf16[8,64,512]{2,1,0:T(8,128)(2,1)S(1)}, u32[]{:S(2)}) copy-start(bf16[8,64,512]{2,1,0:T(8,128)(2,1)S(1)} %fusion.158) | copy-start | bytes 1572868
  394.0 21.4 %copy-start.308 = (f32[2048]{0:T(1024)}, f32[2048]{0:T(1024)S(1)}, u32[]{:S(2)}) copy-start(f32[2048]{0:T(1024)S(1)} %get-tuple-element.606) | copy-start | bytes 24580
  470.3 217.0 %copy-start.55 = (f32[512,512]{1,0:T(8,128)}, f32[512,512]{1,0:T(8,128)S(1)}, u32[]{:S(2)}) copy-start(f32[512,512]{1,0:T(8,128)S(1)} %get-tuple-element.625) | copy-start | bytes 3145732
  562.9 44.2 %copy-start.50 = (bf16[4096,512]{1,0:T(8,128)(2,1)S(1)}, bf16[4096,512]{1,0:T(8,128)(2,1)}, u32[]{:S(2)}) copy-start(bf16[4096,512]{1,0:T(8,128)(2,1)} %convert_element_type.555) | copy-start | bytes 12582916
  562.9 44.1 %copy-start.372 = (f32[512]{0:T(512)S(1)}, f32[512]{0:T(512)}, u32[]{:S(2)}) copy-start(f32[512]{0:T(512)} %dynamic-slice_divide_fusion) | copy-start | bytes 6148
  611.1 19.5 %all-to-all-start.3 = ((bf16[8,64,512]{2,1,0:T(8,128)(2,1)}), bf16[8,64,512]{2,1,0:T(8,128)(2,1)}, u32[]{:S(2)}, u32[]{:S(2)}) async-start(bf16[8,64,512]{2,1,0:T(8,128)(2,1)} %bitcast.704), calls=%async_computation.3 | async-start | bytes 1048576 | tf_op jit(solution)/shard_map/all_to_all | solution.py:825
  615.3 737.5 %reduce-scatter.3.cloned.1.call-start = ((), (), s32[]{:S(2)}) async-start(), calls=%async_computation.9 | async-start | bytes 28835840 | tf_op jit(solution)/shard_map/reduce_scatter | solution.py:848
  650.4 36.9 %copy-start.42 = (f32[512,512]{1,0:T(8,128)}, f32[512,512]{1,0:T(8,128)S(1)}, u32[]{:S(2)}) copy-start(f32[512,512]{1,0:T(8,128)S(1)} %fusion.186) | copy-start | bytes 3145732
  751.4 28.2 %copy-start.51 = (f32[2048,512]{1,0:T(8,128)}, f32[2048,512]{1,0:T(8,128)S(1)}, u32[]{:S(2)}) copy-start(f32[2048,512]{1,0:T(8,128)S(1)} %add_add_fusion.2) | copy-start | bytes 12582916
  800.4 23.5 %slice-start.8 = ((s8[16777216]{0:T(1024)(128)(4,1)}), s8[4194304]{0:T(1024)(128)(4,1)S(1)}, s32[]{:S(2)}) async-start(s8[16777216]{0:T(1024)(128)(4,1)} %bitcast.545), calls=%async_computation.20 | async-start | bytes 8388608
  800.4 23.5 %slice-start.9 = ((s8[16777216]{0:T(1024)(128)(4,1)}), s8[4194304]{0:T(1024)(128)(4,1)S(1)}, s32[]{:S(2)}) async-start(s8[16777216]{0:T(1024)(128)(4,1)} %bitcast.545), calls=%async_computation.21 | async-start | bytes 8388608
  915.1 40.7 %slice-start.26 = ((s8[8388608]{0:T(1024)(128)(4,1)}), s8[4194304]{0:T(1024)(128)(4,1)S(1)}, s32[]{:S(2)}) async-start(s8[8388608]{0:T(1024)(128)(4,1)} %bitcast.822), calls=%async_computation.38 | async-start | bytes 8388608
  934.6 21.2 %slice-start.27 = ((s8[8388608]{0:T(1024)(128)(4,1)}), s8[4194304]{0:T(1024)(128)(4,1)S(1)}, s32[]{:S(2)}) async-start(s8[8388608]{0:T(1024)(128)(4,1)} %bitcast.822), calls=%async_computation.39 | async-start | bytes 8388608
  1036.8 34.3 %copy-start.40 = (f32[2048,512]{1,0:T(8,128)S(1)}, f32[2048,512]{1,0:T(8,128)}, u32[]{:S(2)}) copy-start(f32[2048,512]{1,0:T(8,128)} %get-tuple-element.498) | copy-start | bytes 12582916
  1036.8 34.3 %copy-start.291 = (f32[2048]{0:T(1024)S(1)}, f32[2048]{0:T(1024)}, u32[]{:S(2)}) copy-start(f32[2048]{0:T(1024)} %copy-done.290) | copy-start | bytes 24580
  1036.8 34.3 %copy-start.342 = (f32[1,512]{1,0:T(1,128)S(1)}, f32[1,512]{1,0:T(1,128)}, u32[]{:S(2)}) copy-start(f32[1,512]{1,0:T(1,128)} %get-tuple-element.581) | copy-start | bytes 6148
  1154.4 98.9 %all-to-all-start.4 = ((bf16[32,128,512]{2,1,0:T(8,128)(2,1)}), bf16[32,128,512]{2,1,0:T(8,128)(2,1)}, u32[]{:S(2)}, u32[]{:S(2)}) async-start(bf16[32,128,512]{2,1,0:T(8,128)(2,1)} %bitcast.535), calls=%async_computation.6 | async-start | bytes 8388608 | tf_op jit(solution)/shard_map/all_to_all | solution.py:603
  1158.1 261.8 %reduce-scatter.5.cloned.1.call-start = ((), (), s32[]{:S(2)}) async-start(), calls=%async_computation.10 | async-start | bytes 6488064 | tf_op jit(solution)/shard_map/reduce_scatter | solution.py:847
  1178.0 20.6 %copy-start.243 = (f32[32,32]{1,0:T(8,128)S(1)}, f32[32,32]{1,0:T(8,128)}, u32[]{:S(2)}) copy-start(f32[32,32]{1,0:T(8,128)} %get-tuple-element.569) | copy-start | bytes 12292
  1352.8 268.3 %all-gather.12.cloned.1.call-start = ((), (), s32[]{:S(2)}) async-start(), calls=%async_computation.11 | async-start | bytes 5242880 | tf_op jit(solution)/shard_map/all_gather | solution.py:860
  1421.7 47.7 %copy-start.24 = (f32[88,32,64]{2,1,0:T(8,128)}, f32[88,32,64]{2,1,0:T(8,128)S(1)}, u32[]{:S(2)}) copy-start(f32[88,32,64]{2,1,0:T(8,128)S(1)} %get-tuple-element.551) | copy-start | bytes 2162692
  1421.7 47.7 %copy-start.25 = (f32[88,32,64]{2,1,0:T(8,128)}, f32[88,32,64]{2,1,0:T(8,128)S(1)}, u32[]{:S(2)}) copy-start(f32[88,32,64]{2,1,0:T(8,128)S(1)} %get-tuple-element.552) | copy-start | bytes 2162692
  (400 other events, 2103.8 us)
Sparse Core Ops, SparseCore 0:
  13.1 209.7 all-gather.7
  502.6 55.4 all-gather.9
  1104.8 247.9 reduce-scatter.2
  1355.1 64.8 reduce-scatter.4
  1424.6 51.8 all-gather.11

commit v2 on v1

--- a/solution.py
+++ b/solution.py
@@ -21,7 +21,7 @@
 GAINS = 11
 
 
-HIGHEST = lax.Precision.HIGHEST
+HIGH = lax.Precision.HIGH
 NORM_EPS = 1e-06
 CLIP_AT = 0.02
 RATE_MATRIX = 0.1
@@ -68,84 +68,148 @@
     return matrix.reshape(matrix.shape[0], HEADS, HEAD_DIM)
 
 
-def block_scores(piece_q, key_heads, valid_len, causal, start_at):
-    block_rows, key_count = (piece_q.shape[0], key_heads.shape[0])
-    scores = jnp.einsum(
-        "qhd,khd->hqk", piece_q, key_heads, preferred_element_type=jnp.float32
-    ) * HEAD_DIM ** (-0.5)
-    key_at = jnp.arange(key_count)
-    allowed = jnp.broadcast_to(key_at[None, :] < valid_len, (block_rows, key_count))
+NEVER=-1000000000.0
+PAIR=2*HEAD_DIM
+def kept_scores(query, keys, valid_len, causal, start_at):
+    scores = lax.dot_general(query, keys, (((1,), (1,)), ((), ())), preferred_element_type=jnp.float32)
+    key_at = lax.broadcasted_iota(jnp.int32, scores.shape if causal else (1, scores.shape[1]), 1)
+    allowed = key_at < valid_len
     if causal:
-        allowed = allowed & (key_at[None, :] <= start_at + jnp.arange(block_rows)[:, None])
-    return jnp.where(allowed[None], scores, -1000000000.0)
-
-
-def attend_forward(query_in, keys_in, values_in, valid_len, causal):
-    row_count = query_in.shape[0]
-    block_rows = min(512, row_count)
-    key_heads, value_heads = (split_heads(keys_in), split_heads(values_in))
-    outputs, stats_kept = ([], [])
-    for start_at in range(0, row_count, block_rows):
-        scores = block_scores(
-            split_heads(query_in[start_at : start_at + block_rows]),
-            key_heads,
-            valid_len,
-            causal,
-            start_at,
-        )
-        summit = jnp.max(scores, axis=-1, keepdims=True)
-        expo_val = jnp.exp(scores - summit)
-        totals = jnp.sum(expo_val, axis=-1, keepdims=True)
-        probs_low = (expo_val / totals).astype(jnp.bfloat16)
-        mixed_out = jnp.einsum(
-            "hqk,khd->qhd", probs_low, value_heads, preferred_element_type=jnp.float32
-        )
-        outputs.append(mixed_out.reshape(block_rows, -1))
-        stats_kept.append(summit + jnp.log(totals))
-    return (jnp.concatenate(outputs, 0).astype(jnp.bfloat16), stats_kept)
-
-
-def attend_backward(query_in, keys_in, values_in, valid_len, causal, stats_kept, grad_out):
-    row_count = query_in.shape[0]
-    block_rows = min(512, row_count)
-    key_heads, value_heads = (split_heads(keys_in), split_heads(values_in))
-    grad_keys = jnp.zeros(key_heads.shape, jnp.float32)
-    grad_values = jnp.zeros(value_heads.shape, jnp.float32)
-    grad_query = []
-    for block_no, start_at in enumerate(range(0, row_count, block_rows)):
-        piece_q = split_heads(query_in[start_at : start_at + block_rows])
-        upstream = split_heads(grad_out[start_at : start_at + block_rows])
-        probs_f = jnp.exp(
-            block_scores(piece_q, key_heads, valid_len, causal, start_at) - stats_kept[block_no]
-        )
-        grad_probs = jnp.einsum(
-            "qhd,khd->hqk", upstream, value_heads, preferred_element_type=jnp.float32
-        )
-        inner_sum = jnp.sum(probs_f * grad_probs, axis=-1, keepdims=True)
-        grad_scores = (probs_f * (grad_probs - inner_sum)).astype(jnp.bfloat16)
-        grad_query.append(
-            (
-                jnp.einsum(
-                    "hqk,khd->qhd", grad_scores, key_heads, preferred_element_type=jnp.float32
-                )
-                * HEAD_DIM ** (-0.5)
-            ).reshape(block_rows, -1)
-        )
-        grad_keys = grad_keys + jnp.einsum(
-            "hqk,qhd->khd", grad_scores, piece_q, preferred_element_type=jnp.float32
-        ) * HEAD_DIM ** (-0.5)
-        grad_values = grad_values + jnp.einsum(
-            "hqk,qhd->khd",
-            probs_f.astype(jnp.bfloat16),
-            upstream,
-            preferred_element_type=jnp.float32,
-        )
-    key_count = keys_in.shape[0]
-    return (
-        jnp.concatenate(grad_query, 0),
-        grad_keys.reshape(key_count, -1),
-        grad_values.reshape(key_count, -1),
-    )
+        allowed = allowed & (key_at <= start_at + lax.broadcasted_iota(jnp.int32, scores.shape, 0))
+    return jnp.where(allowed, scores, NEVER)
+
+def head_masks(value):
+    first = lax.broadcasted_iota(jnp.int32, value.shape, 1) < HEAD_DIM
+    zero = jnp.zeros_like(value)
+    return (jnp.where(first, value, zero), jnp.where(first, zero, value))
+
+def attend_forward(query_in, query_at, keys_in, key_at, value_at, valid_len, causal):
+    rows, keys = (query_in.shape[0] // MICRO, keys_in.shape[0] // MICRO)
+    block = min(256, rows)
+    steps = rows // block
+    scale = HEAD_DIM ** (-0.5)
+
+    def kernel(len_ref, query_ref, key_ref, value_ref, out_ref, stat_ref):
+        start_at = pl.program_id(2) * block
+        length = len_ref[pl.program_id(0)]
+        queries = head_masks((query_ref[...].astype(jnp.float32) * scale).astype(jnp.bfloat16))
+        values = head_masks(value_ref[...])
+        total = jnp.zeros((block, PAIR), jnp.float32)
+        stats = []
+        for head in range(2):
+            scores = kept_scores(queries[head], key_ref[...], length, causal, start_at)
+            summit = jnp.max(scores, axis=1, keepdims=True)
+            expo = jnp.exp(scores - summit)
+            sums = jnp.sum(expo, axis=1, keepdims=True)
+            probs = (expo * (1.0 / sums)).astype(jnp.bfloat16)
+            total += jnp.dot(probs, values[head], preferred_element_type=jnp.float32)
+            stats.append(summit + jnp.log(sums))
+        out_ref[...] = total.astype(jnp.bfloat16)
+        first = lax.broadcasted_iota(jnp.int32, (block, PAIR), 1) < HEAD_DIM
+        stat_ref[...] = jnp.where(first, stats[0], stats[1])
+
+    out_spec = pl.BlockSpec((block, PAIR), lambda seq, pair, step, lens: (seq * steps + step, pair))
+    return pl.pallas_call(
+        kernel,
+        out_shape=(
+            jax.ShapeDtypeStruct((MICRO * rows, D), jnp.bfloat16),
+            jax.ShapeDtypeStruct((MICRO * rows, D), jnp.float32),
+        ),
+        grid_spec=pltpu.PrefetchScalarGridSpec(
+            num_scalar_prefetch=1,
+            grid=(MICRO, D // PAIR, steps),
+            in_specs=[
+                pl.BlockSpec((block, PAIR), lambda seq, pair, step, lens: (seq * steps + step, query_at + pair)),
+                pl.BlockSpec((keys, PAIR), lambda seq, pair, step, lens: (seq, key_at + pair)),
+                pl.BlockSpec((keys, PAIR), lambda seq, pair, step, lens: (seq, value_at + pair)),
+            ],
+            out_specs=(out_spec, out_spec),
+        ),
+        compiler_params=pltpu.CompilerParams(vmem_limit_bytes=40 * 2**20),
+        cost_estimate=pl.CostEstimate(flops=4*MICRO*rows*keys*D, bytes_accessed=MICRO*(rows+keys)*D*8, transcendentals=MICRO*HEADS*rows*keys),
+    )(valid_len, query_in, keys_in, keys_in)
+
+def attend_backward(query_in, query_at, keys_in, key_at, value_at, valid_len, causal, stats, grad_out, first=0, seqs=MICRO, begun=()):
+    rows, keys = (query_in.shape[0] // MICRO, keys_in.shape[0] // MICRO)
+    block = min(512, rows)
+    steps = rows // block
+    scale = HEAD_DIM ** (-0.5)
+
+    def kernel(len_ref, query_ref, key_ref, value_ref, stat_ref, up_ref, *refs):
+        dq_ref, dk_ref, dv_ref, key_sum, value_sum = refs[len(begun) :]
+        step = pl.program_id(2)
+        start_at = step * block
+        length = len_ref[first + pl.program_id(0)]
+        queries = head_masks((query_ref[...].astype(jnp.float32) * scale).astype(jnp.bfloat16))
+        upstream = head_masks(up_ref[...])
+        keys_each = head_masks(key_ref[...])
+        grad_query = jnp.zeros((block, PAIR), jnp.float32)
+        grad_key = jnp.zeros((keys, PAIR), jnp.float32)
+        grad_value = jnp.zeros((keys, PAIR), jnp.float32)
+        over_rows = (((0,), (0,)), ((), ()))
+        for head in range(2):
+            scores = kept_scores(queries[head], key_ref[...], length, causal, start_at)
+            probs = jnp.exp(scores - stat_ref[:, head * HEAD_DIM : head * HEAD_DIM + 1])
+            grad_probs = lax.dot_general(upstream[head], value_ref[...], (((1,), (1,)), ((), ())), preferred_element_type=jnp.float32)
+            inner = jnp.sum(probs * grad_probs, axis=1, keepdims=True)
+            grad_scores = (probs * (grad_probs - inner)).astype(jnp.bfloat16)
+            grad_query += jnp.dot(grad_scores, keys_each[head], preferred_element_type=jnp.float32)
+            grad_key += lax.dot_general(grad_scores, queries[head], over_rows, preferred_element_type=jnp.float32)
+            grad_value += lax.dot_general(probs.astype(jnp.bfloat16), upstream[head], over_rows, preferred_element_type=jnp.float32)
+        dq_ref[...] = (grad_query * scale).astype(jnp.bfloat16)
+        if steps == 1:
+            dk_ref[...] = grad_key.astype(jnp.bfloat16)
+            dv_ref[...] = grad_value.astype(jnp.bfloat16)
+        else:
+            @pl.when(step == 0)
+            def _():
+                key_sum[...] = grad_key
+                value_sum[...] = grad_value
+
+            @pl.when(step > 0)
+            def _():
+                key_sum[...] += grad_key
+                value_sum[...] += grad_value
+
+            @pl.when(step == steps - 1)
+            def _():
+                dk_ref[...] = key_sum[...].astype(jnp.bfloat16)
+                dv_ref[...] = value_sum[...].astype(jnp.bfloat16)
+
+    def row_spec(at, begin):
+        return pl.BlockSpec(
+            (block, PAIR),
+            lambda seq, pair, step, lens: ((begin + seq) * steps + step, at + pair),
+        )
+
+    def key_spec(at, begin):
+        return pl.BlockSpec((keys, PAIR), lambda seq, pair, step, lens: (begin + seq, at + pair))
+
+    return pl.pallas_call(
+        kernel,
+        out_shape=(
+            jax.ShapeDtypeStruct((MICRO * rows, D), jnp.bfloat16),
+            jax.ShapeDtypeStruct((MICRO * keys, D), jnp.bfloat16),
+            jax.ShapeDtypeStruct((MICRO * keys, D), jnp.bfloat16),
+        ),
+        grid_spec=pltpu.PrefetchScalarGridSpec(
+            num_scalar_prefetch=1,
+            grid=(seqs, D // PAIR, steps),
+            in_specs=[
+                row_spec(query_at, first),
+                key_spec(key_at, first),
+                key_spec(value_at, first),
+                row_spec(0, first),
+                row_spec(0, first),
+            ]
+            + [pl.BlockSpec(memory_space=pl.ANY)] * len(begun),
+            out_specs=(row_spec(0, first), key_spec(0, first), key_spec(0, first)),
+            scratch_shapes=[pltpu.VMEM((keys, PAIR), jnp.float32)] * 2,
+        ),
+        input_output_aliases={6 + item: item for item in range(len(begun))},
+        compiler_params=pltpu.CompilerParams(vmem_limit_bytes=40 * 2**20),
+        cost_estimate=pl.CostEstimate(flops=10*seqs*rows*keys*D, bytes_accessed=seqs*(rows+keys)*D*16, transcendentals=seqs*HEADS*rows*keys),
+    )(valid_len, query_in, keys_in, keys_in, stats, grad_out, *begun)
 
 
 def norm_backward(stream, gain_row, grad_normed):
@@ -153,46 +217,12 @@
     return pull_back(grad_normed)
 
 
-def by_sequence(matrix):
-    return jnp.split(matrix, MICRO, axis=0)
-
-
-def attend_all(query_in, keys_in, values_in, valid_len, causal):
-    outs, stats = ([], [])
-    for seq_no, (piece_q, piece_k, piece_v) in enumerate(
-        zip(by_sequence(query_in), by_sequence(keys_in), by_sequence(values_in))
-    ):
-        out, kept = attend_forward(piece_q, piece_k, piece_v, valid_len[seq_no], causal)
-        outs.append(out)
-        stats.append(kept)
-    return (jnp.concatenate(outs, 0), stats)
-
-
-def attend_all_backward(query_in, keys_in, values_in, valid_len, causal, stats, mixed_out, grad_out):
-    parts = []
-    for seq_no, pieces in enumerate(
-        zip(
-            by_sequence(query_in), by_sequence(keys_in), by_sequence(values_in),
-            by_sequence(grad_out),
-        )
-    ):
-        piece_q, piece_k, piece_v, upstream = pieces
-        parts.append(
-            attend_backward(
-                piece_q, piece_k, piece_v, valid_len[seq_no], causal, stats[seq_no], upstream
-            )
-        )
-    return tuple(
-        jnp.concatenate([part[item] for part in parts], 0).astype(jnp.bfloat16)
-        for item in range(3)
-    )
-
-
 def self_forward(stream, gain_row, weight, valid_len, causal):
     normed = rms_norm(stream, gain_row).astype(jnp.bfloat16)
     joint_qkv = linear(normed, weight[:, : 3 * D]).astype(jnp.bfloat16)
-    mixed_out, stats_kept = attend_all(
-        joint_qkv[:, :D], joint_qkv[:, D : 2 * D], joint_qkv[:, 2 * D :], valid_len, causal
+    pairs = D // PAIR
+    mixed_out, stats_kept = attend_forward(
+        joint_qkv, 0, joint_qkv, pairs, 2 * pairs, valid_len, causal
     )
     return (
         stream + linear(mixed_out, weight[:, 3 * D :]),
@@ -200,22 +230,34 @@
     )
 
 
-def self_backward(grad_stream, kept_block, gain_row, weight, valid_len, causal):
+def self_backward(grad_stream, kept_block, gain_row, weight, valid_len, causal, between=None):
     stream, normed, joint_qkv, mixed_out, stats_kept = kept_block
     grad_low = grad_stream.astype(jnp.bfloat16)
     grad_out_w = outer_sum(mixed_out, grad_low)
     grad_mixed = linear_tr(grad_low, weight[:, 3 * D :]).astype(jnp.bfloat16)
-    grad_q, grad_k, grad_v = attend_all_backward(
-        joint_qkv[:, :D],
-        joint_qkv[:, D : 2 * D],
-        joint_qkv[:, 2 * D :],
-        valid_len,
-        causal,
-        stats_kept,
-        mixed_out,
-        grad_mixed,
-    )
-    grad_joint = jnp.concatenate([grad_q, grad_k, grad_v], 1)
+    pairs = D // PAIR
+    stages = 1 if between is None else MICRO
+    grads = ()
+    for stage in range(stages):
+        if stage > 0:
+            grad_mixed = between(grad_mixed)
+        grads = attend_backward(
+            joint_qkv,
+            0,
+            joint_qkv,
+            pairs,
+            2 * pairs,
+            valid_len,
+            causal,
+            stats_kept,
+            grad_mixed,
+            stage * MICRO // stages,
+            MICRO // stages,
+            tuple(grads),
+        )
+    grad_joint = jnp.concatenate(grads, 1)
+    if between is not None:
+        grad_joint = between(grad_joint)
     grad_x, grad_gain = norm_backward(stream, gain_row, linear_tr(grad_joint, weight[:, : 3 * D]))
     return (
         grad_stream + grad_x,
@@ -228,7 +270,9 @@
     normed = rms_norm(stream, gain_row).astype(jnp.bfloat16)
     query_in = linear(normed, weight[:, :D]).astype(jnp.bfloat16)
     pair_kv = linear(memory, weight[:, D : 3 * D]).astype(jnp.bfloat16)
-    mixed_out, stats_kept = attend_all(query_in, pair_kv[:, :D], pair_kv[:, D:], valid_len, False)
+    mixed_out, stats_kept = attend_forward(
+        query_in, 0, pair_kv, 0, D // PAIR, valid_len, False
+    )
     return (
         stream + linear(mixed_out, weight[:, 3 * D :]),
         (stream, normed, query_in, pair_kv, mixed_out, stats_kept),
@@ -240,8 +284,8 @@
     grad_low = grad_stream.astype(jnp.bfloat16)
     grad_out_w = outer_sum(mixed_out, grad_low)
     grad_mixed = linear_tr(grad_low, weight[:, 3 * D :]).astype(jnp.bfloat16)
-    grad_query, grad_k, grad_v = attend_all_backward(
-        query_in, pair_kv[:, :D], pair_kv[:, D:], valid_len, False, stats_kept, mixed_out, grad_mixed
+    grad_query, grad_k, grad_v = attend_backward(
+        query_in, 0, pair_kv, 0, D // PAIR, valid_len, False, stats_kept, grad_mixed
     )
     grad_pair = jnp.concatenate([grad_k, grad_v], 1)
     grad_weight = jnp.concatenate(
@@ -282,7 +326,15 @@
     )
 
 
-def forward_all(weights, gain_set, source_rows, target_rows, source_len, target_len, place_rows):
+def forward_all(
+    weights,
+    gain_set,
+    source_rows,
+    source_len,
+    target_len,
+    place_rows,
+    lay_decoder,
+):
     stream = source_rows
     enc_kept = []
     for layer_no in range(ENC):
@@ -296,8 +348,7 @@
             weights[2 * ENC + 3 * DEC + layer_no],
         )
         enc_kept.append((kept_self, kept_ffn))
-    memory = rms_norm(stream, gain_set[2 * ENC]).astype(jnp.bfloat16)
-    decoded = target_rows
+    memory, decoded = lay_decoder(rms_norm(stream, gain_set[2 * ENC]).astype(jnp.bfloat16))
     dec_kept, exit_in, exit_rows = ([], [], [])
     for layer_no in range(DEC):
         base_at = 2 * ENC + 1 + 3 * layer_no
@@ -323,7 +374,9 @@
     return (kept, jnp.concatenate(exit_rows, 0))
 
 
-def backward_all(weights, gain_set, kept, exit_grads, matrix_store, gain_store):
+def backward_all(
+    weights, gain_set, kept, exit_grads, matrix_store, gain_store, before_last, between_last
+):
     source_len, target_len, place_rows, enc_kept, stream, memory, dec_kept, exit_in = kept
     exit_each = jnp.split(exit_grads, DEC, axis=0)
     grad_decoded = jnp.zeros(dec_kept[0][0][0].shape, jnp.float32)
@@ -359,87 +412,31 @@
                 grad_stream, kept_ffn, gain_set[2 * layer_no + 1], weights[in_at], weights[out_at]
             )
         )
+        if layer_no == 0:
+            grad_stream = before_last(grad_stream)
         grad_stream, gain_store[2 * layer_no], matrix_store[layer_no] = self_backward(
-            grad_stream, kept_self, gain_set[2 * layer_no], weights[layer_no], source_len, False
+            grad_stream,
+            kept_self,
+            gain_set[2 * layer_no],
+            weights[layer_no],
+            source_len,
+            False,
+            between_last if layer_no == 0 else None,
         )
     return (grad_stream, grad_decoded)
 
 
-def fold_blocks(tiles):
-    return jnp.concatenate([tiles[:, : PB // 2], tiles[:, PB // 2 :]], axis=2)
-
-
-def unfold_blocks(folded):
-    return jnp.concatenate([folded[:, :, :PB], folded[:, :, PB:]], axis=1)
-
-
-def swap_halves(value):
-    return jnp.concatenate([value[:, PB:], value[:, :PB]], axis=1)
-
-
-def lay_matrices(folded_all, slot_of):
-    half = PB // 2
-    row_blocks, pairs = (D // PB, FF // (2 * PB))
-
-    def kernel(slot_ref, folded_ref, out_ref):
-        first = pl.program_id(0) * row_blocks * 2 * pairs + pl.program_id(1) * 2 * pairs
-        left_half = lax.broadcasted_iota(jnp.int32, (half, 2 * PB), 1) < PB
-        for pair_no in range(pairs):
-            even = folded_ref[slot_ref[first + 2 * pair_no]].astype(jnp.float32)
-            odd = folded_ref[slot_ref[first + 2 * pair_no + 1]].astype(jnp.float32)
-            even_turned = pltpu.roll(even, PB, 1)
-            odd_turned = pltpu.roll(odd, PB, 1)
-            columns = slice(2 * PB * pair_no, 2 * PB * (pair_no + 1))
-            out_ref[0, :half, columns] = jnp.where(left_half, even, odd_turned).astype(jnp.bfloat16)
-            out_ref[0, half:, columns] = jnp.where(left_half, even_turned, odd).astype(jnp.bfloat16)
-
-    return pl.pallas_call(
-        kernel,
-        out_shape=jax.ShapeDtypeStruct((MATS, D, FF), jnp.bfloat16),
-        grid_spec=pltpu.PrefetchScalarGridSpec(
-            num_scalar_prefetch=1,
-            grid=(MATS, row_blocks),
-            in_specs=[pl.BlockSpec(memory_space=pltpu.VMEM)],
-            out_specs=pl.BlockSpec((1, PB, FF), lambda mat_no, row_no, slots: (mat_no, row_no, 0)),
-        ),
-        compiler_params=pltpu.CompilerParams(vmem_limit_bytes=40 * 2**20),
-    )(slot_of, folded_all)
-
-
-def fold_gradients(matrices, slot_of):
-    half = PB // 2
-    row_blocks, pairs = (D // PB, FF // (2 * PB))
-    count = MATS * row_blocks * 2 * pairs
-
-    def kernel(slot_ref, *refs):
-        sources, out_ref, held, arrived = (refs[:MATS], refs[MATS], refs[MATS + 1], refs[MATS + 2])
-        left_half = lax.broadcasted_iota(jnp.int32, (half, 2 * PB), 1) < PB
-
-        def fetch(mat_no):
-            return pltpu.make_async_copy(
-                sources[mat_no], held.at[mat_no % 2], arrived.at[mat_no % 2]
-            )
-
-        fetch(0).start()
-        for mat_no in range(MATS):
-            if mat_no + 1 < MATS:
-                fetch(mat_no + 1).start()
-            fetch(mat_no).wait()
-
-            def one_row(row_no, carry, mat_no=mat_no):
-                first = (mat_no * row_blocks + row_no) * 2 * pairs
-                row_at = pl.multiple_of(row_no * PB, PB)
-                for pair_no in range(pairs):
-                    columns = slice(2 * PB * pair_no, 2 * PB * (pair_no + 1))
-                    upper = held[mat_no % 2, pl.ds(row_at, half), columns].astype(jnp.float32)
-                    lower = held[mat_no % 2, pl.ds(row_at + half, half), columns].astype(jnp.float32)
-                    even = jnp.where(left_half, upper, pltpu.roll(lower, PB, 1))
-                    odd = jnp.where(left_half, pltpu.roll(upper, PB, 1), lower)
-                    out_ref[slot_ref[first + 2 * pair_no]] = even.astype(jnp.bfloat16)
-                    out_ref[slot_ref[first + 2 * pair_no + 1]] = odd.astype(jnp.bfloat16)
-                return carry
-
-            lax.fori_loop(0, row_blocks, one_row, 0)
+def fold_ranked(tiles, rank_of):
+    count, half = (tiles.shape[0], PB // 2)
+
+    def kernel(rank_ref, tile_ref, out_ref):
+        def one_block(tile_no, carry):
+            value = tile_ref[tile_no]
+            folded = jnp.concatenate([value[:half], value[half:]], axis=1)
+            out_ref[rank_ref[tile_no]] = folded.astype(jnp.bfloat16)
+            return carry
+
+        lax.fori_loop(0, count, one_block, 0)
 
     return pl.pallas_call(
         kernel,
@@ -447,15 +444,292 @@
         grid_spec=pltpu.PrefetchScalarGridSpec(
             num_scalar_prefetch=1,
             grid=(1,),
-            in_specs=[pl.BlockSpec(memory_space=pl.ANY)] * MATS,
+            in_specs=[pl.BlockSpec(memory_space=pltpu.VMEM)],
             out_specs=pl.BlockSpec(memory_space=pltpu.VMEM),
+        ),
+        compiler_params=pltpu.CompilerParams(vmem_limit_bytes=40 * 2**20),
+    )(rank_of, tiles)
+
+
+def unfold_ranked(folded, rank_of):
+    count, half = (folded.shape[0], PB // 2)
+
+    def kernel(rank_ref, folded_ref, out_ref):
+        def one_block(tile_no, carry):
+            value = folded_ref[rank_ref[tile_no]]
+            out_ref[tile_no, :half] = value[:, :PB]
+            out_ref[tile_no, half:] = value[:, PB:]
+            return carry
+
+        lax.fori_loop(0, count, one_block, 0)
+
+    return pl.pallas_call(
+        kernel,
+        out_shape=jax.ShapeDtypeStruct((count, PB, PB), jnp.float32),
+        grid_spec=pltpu.PrefetchScalarGridSpec(
+            num_scalar_prefetch=1,
+            grid=(1,),
+            in_specs=[pl.BlockSpec(memory_space=pltpu.VMEM)],
+            out_specs=pl.BlockSpec(memory_space=pltpu.VMEM),
+        ),
+        compiler_params=pltpu.CompilerParams(vmem_limit_bytes=40 * 2**20),
+    )(rank_of, folded)
+
+
+def is_encoder(mat_no):
+    return (
+        mat_no < ENC
+        or ENC + 2 * DEC <= mat_no < 2 * ENC + 2 * DEC
+        or 2 * ENC + 3 * DEC <= mat_no < 3 * ENC + 3 * DEC
+    )
+
+
+def is_last(mat_no):
+    return mat_no == 0
+
+
+def rank_blocks(slot_list, devices, is_first):
+    blocks_each = D // PB * (FF // PB)
+    mats = slot_list // blocks_each
+    early = jnp.zeros(mats.shape, jnp.bool_)
+    for mat_no in range(MATS):
+        if is_first(mat_no):
+            early = early | (mats == mat_no)
+    early = early.reshape(devices, -1).astype(jnp.int32)
+    early_count = jnp.sum(early, axis=1)
+    ahead = jnp.cumsum(early, axis=1) - early
+    later = early_count[:, None] + jnp.arange(early.shape[1])[None, :] - ahead
+    return (jnp.where(early == 1, ahead, later), early_count)
+
+
+def room_for(per_device, chosen):
+    share = sum(chosen(mat_no) for mat_no in range(MATS)) / MATS
+    mean = per_device * share
+    return min(per_device - 1, -(-int(mean + 5.0 * math.sqrt(mean * (1 - share))) // 4) * 4)
+
+
+def by_block(slot_list, values):
+    width, base = (64, 128)
+    height = -(-slot_list.shape[0] // width)
+    rows = (slot_list[:, None] // width == jnp.arange(height)[None, :]).astype(jnp.bfloat16)
+    lanes = (slot_list[:, None] % width == jnp.arange(width)[None, :]).astype(jnp.bfloat16)
+    found = []
+    for value in values:
+        high, low = (
+            outer_sum(rows * (part.astype(jnp.bfloat16))[:, None], lanes)
+            for part in (value // base, value % base)
+        )
+        found.append((high * base + low).astype(jnp.int32).reshape(-1)[: slot_list.shape[0]])
+    return found
+
+
+def lay_matrices(buffers, place_of, mats):
+    half = PB // 2
+    row_blocks, pairs = (D // PB, FF // (2 * PB))
+    sizes = [buffer.shape[0] for buffer in buffers]
+    starts = [sum(sizes[:item]) for item in range(len(sizes))]
+    count = len(mats)
+
+    def kernel(place_ref, *refs):
+        sources, outs = (refs[: len(sizes)], refs[len(sizes) : len(sizes) + count])
+        folded_ref, made, arrived, left = refs[len(sizes) + count :]
+        left_half = lax.broadcasted_iota(jnp.int32, (half, 2 * PB), 1) < PB
+        fetches = [
+            pltpu.make_async_copy(
+                source, folded_ref.at[pl.ds(start, size)], arrived.at[item]
+            )
+            for item, (source, start, size) in enumerate(zip(sources, starts, sizes))
+        ]
+        for fetch in fetches:
+            fetch.start()
+        for fetch in fetches:
+            fetch.wait()
+
+        def send(item):
+            return pltpu.make_async_copy(made.at[item % 2], outs[item], left.at[item % 2])
+
+        for item, mat_no in enumerate(mats):
+            if item >= 2:
+                send(item - 2).wait()
+
+            def one_row(row_no, carry, item=item, mat_no=mat_no):
+                first = (mat_no * row_blocks + row_no) * 2 * pairs
+                row_at = pl.multiple_of(row_no * PB, PB)
+                for pair_no in range(pairs):
+                    even = folded_ref[place_ref[first + 2 * pair_no]].astype(jnp.float32)
+                    odd = folded_ref[place_ref[first + 2 * pair_no + 1]].astype(jnp.float32)
+                    columns = slice(2 * PB * pair_no, 2 * PB * (pair_no + 1))
+                    upper = jnp.where(left_half, even, pltpu.roll(odd, PB, 1))
+                    lower = jnp.where(left_half, pltpu.roll(even, PB, 1), odd)
+                    made[item % 2, pl.ds(row_at, half), columns] = upper.astype(jnp.bfloat16)
+                    made[item % 2, pl.ds(row_at + half, half), columns] = lower.astype(jnp.bfloat16)
+                return carry
+
+            lax.fori_loop(0, row_blocks, one_row, 0)
+            send(item).start()
+        for item in range(max(count - 2, 0), count):
+            send(item).wait()
+
+    return pl.pallas_call(
+        kernel,
+        out_shape=[jax.ShapeDtypeStruct((D, FF), jnp.bfloat16)] * count,
+        grid_spec=pltpu.PrefetchScalarGridSpec(
+            num_scalar_prefetch=1,
+            grid=(1,),
+            in_specs=[pl.BlockSpec(memory_space=pl.ANY)] * len(sizes),
+            out_specs=[pl.BlockSpec(memory_space=pl.ANY)] * count,
             scratch_shapes=[
+                pltpu.VMEM((sum(sizes), half, 2 * PB), jnp.bfloat16),
                 pltpu.VMEM((2, D, FF), jnp.bfloat16),
+                pltpu.SemaphoreType.DMA((len(sizes),)),
                 pltpu.SemaphoreType.DMA((2,)),
             ],
         ),
         compiler_params=pltpu.CompilerParams(vmem_limit_bytes=40 * 2**20),
-    )(slot_of, *matrices)
+    )(place_of, *buffers)
+
+
+def fold_gradients(matrices, mats, place_of, sizes, begun=None):
+    half = PB // 2
+    row_blocks, pairs = (D // PB, FF // (2 * PB))
+    count = len(mats)
+    whole = sum(sizes)
+    given = 0 if begun is None else 1
+    skipped = 0 if begun is None else whole - begun.shape[0]
+    kept = whole - skipped
+
+    def kernel(place_ref, *refs):
+        sources, old = (refs[:count], refs[count : count + given])
+        outs = refs[count + given : -5]
+        folded_ref, held, arrived, left, old_sem = refs[-5:]
+        left_half = lax.broadcasted_iota(jnp.int32, (half, 2 * PB), 1) < PB
+
+        def fetch(item):
+            return pltpu.make_async_copy(sources[item], held.at[item % 2], arrived.at[item % 2])
+
+        fetch(0).start()
+        if given:
+            before = pltpu.make_async_copy(
+                old[0], folded_ref.at[pl.ds(0, kept)], old_sem.at[0]
+            )
+            before.start()
+            before.wait()
+        for item, mat_no in enumerate(mats):
+            if item + 1 < count:
+                fetch(item + 1).start()
+            fetch(item).wait()
+
+            def place(block, carry=None):
+                spot = place_ref[block] - skipped
+                return jnp.where(spot < 0, kept, spot) if given else spot
+
+            def one_row(row_no, carry, item=item, mat_no=mat_no):
+                first = (mat_no * row_blocks + row_no) * 2 * pairs
+                row_at = pl.multiple_of(row_no * PB, PB)
+                for pair_no in range(pairs):
+                    columns = slice(2 * PB * pair_no, 2 * PB * (pair_no + 1))
+                    upper = held[item % 2, pl.ds(row_at, half), columns].astype(jnp.float32)
+                    lower = held[item % 2, pl.ds(row_at + half, half), columns].astype(jnp.float32)
+                    even = jnp.where(left_half, upper, pltpu.roll(lower, PB, 1))
+                    odd = jnp.where(left_half, pltpu.roll(upper, PB, 1), lower)
+                    folded_ref[place(first + 2 * pair_no)] = even.astype(jnp.bfloat16)
+                    folded_ref[place(first + 2 * pair_no + 1)] = odd.astype(jnp.bfloat16)
+                return carry
+
+            lax.fori_loop(0, row_blocks, one_row, 0)
+        begin = 0
+        sends = []
+        for item, out in enumerate(outs):
+            size = out.shape[0]
+            sends.append(
+                pltpu.make_async_copy(folded_ref.at[pl.ds(begin, size)], out, left.at[item])
+            )
+            begin += size
+        for send in sends:
+            send.start()
+        for send in sends:
+            send.wait()
+
+    shapes = [kept] if given else list(sizes)
+    return pl.pallas_call(
+        kernel,
+        out_shape=[jax.ShapeDtypeStruct((size, half, 2 * PB), jnp.bfloat16) for size in shapes],
+        grid_spec=pltpu.PrefetchScalarGridSpec(
+            num_scalar_prefetch=1,
+            grid=(1,),
+            in_specs=[pl.BlockSpec(memory_space=pl.ANY)] * (count + given),
+            out_specs=[pl.BlockSpec(memory_space=pl.ANY)] * len(shapes),
+            scratch_shapes=[
+                pltpu.VMEM((kept + given, half, 2 * PB), jnp.bfloat16),
+                pltpu.VMEM((2, D, FF), jnp.bfloat16),
+                pltpu.SemaphoreType.DMA((2,)),
+                pltpu.SemaphoreType.DMA((2,)),
+                pltpu.SemaphoreType.DMA((1,)),
+            ],
+        ),
+        compiler_params=pltpu.CompilerParams(vmem_limit_bytes=40 * 2**20),
+    )(place_of, *[matrices[mat_no] for mat_no in mats], *([begun] if given else []))
+
+
+def exchange_plan(dp_size, along, per_device):
+    low, high = (along.bit_length() - 1, dp_size.bit_length() - 1)
+    base = [low + bit for bit in range(high)] + list(range(1, low))
+    third = per_device // 3
+    sizes = [per_device - 2 * third, third, third]
+    return [(size, base[turn:] + base[:turn]) for turn, size in enumerate(sizes)]
+
+
+def places_for(ranks, plan, devices):
+    per_device = sum(size for size, _ in plan)
+    owner = jnp.arange(devices)[:, None]
+    place = jnp.zeros_like(ranks)
+    begin = 0
+    for size, order in plan:
+        spot = jnp.zeros_like(owner)
+        for bit in order:
+            spot = spot * 2 + owner // 2**bit % 2
+        here = begin * (devices // 2) + spot * size + ranks - begin
+        place = jnp.where((ranks >= begin) & (ranks < begin + size), here, place)
+        begin += size
+    return place + owner % 2 * (devices // 2 * per_device)
+
+
+def halve(value, bit, devices):
+    me = lax.axis_index("dp") * lax.axis_size("vocab") + lax.axis_index("vocab")
+
+    mine = me // 2**bit % 2
+    value = value.reshape(2, value.shape[0] // 2, *value.shape[1:])
+    sent = lax.dynamic_index_in_dim(value, 1 - mine, 0, keepdims=False)
+    kept = lax.dynamic_index_in_dim(value, mine, 0, keepdims=False)
+    pairs = [(index, index ^ 2**bit) for index in range(devices)]
+    arrived = lax.ppermute(sent, ("dp", "vocab"), pairs)
+    return kept.astype(jnp.float32) + arrived.astype(jnp.float32)
+
+
+def first_exchange(folded, devices):
+    return halve(folded, 0, devices).astype(jnp.bfloat16)
+
+
+def split_parts(total, plan, devices):
+    parts, begin = ([], 0)
+    for size, _ in plan:
+        count = size * (devices // 2)
+        parts.append(total[begin : begin + count])
+        begin += count
+    return parts
+
+
+def one_exchange(parts, plan, round_no, devices):
+    return [
+        halve(part.astype(jnp.bfloat16), order[round_no], devices)
+        for part, (_, order) in zip(parts, plan)
+    ]
+
+
+def other_exchanges(parts, plan, devices, done=0):
+    for round_no in range(done, len(plan[0][1])):
+        parts = one_exchange(parts, plan, round_no, devices)
+    return jnp.concatenate(parts, 0)
 
 
 def take_rows(source, index_at, kind):
@@ -525,6 +799,12 @@
     )(index_at, rows, total)
 
 
+def spread(value, axes, peers):
+    return lax.all_to_all(
+        jnp.broadcast_to(value[None], (peers, *value.shape)), axes, 0, 0, tiled=True
+    )
+
+
 def count_before(mask):
     size, width = (mask.shape[-1], 128)
     parts = mask.reshape(*mask.shape[:-1], size // width, width).astype(jnp.bfloat16)
@@ -540,10 +820,21 @@
     return min(count, -(-int(mean + 5.0 * math.sqrt(mean)) // 16) * 16)
 
 
-def listed(mask, rank, values, size, empty):
-    spot = jnp.arange(size)[:, None]
-    chosen = mask[..., None, :] & (rank[..., None, :] == spot)
-    return jnp.sum(jnp.where(chosen, values[..., None, :] - empty, 0), axis=-1) + empty
+def listed(mask, rank, values, size):
+    width, base = (16, 128)
+    rows = mask[..., None] & (rank[..., None] // width == jnp.arange(size // width))
+    lanes = (rank[..., None] % width == jnp.arange(width)).astype(jnp.bfloat16)
+    values = values + 1
+    high, low = (
+        jnp.einsum(
+            "...th,...tl->...hl",
+            jnp.where(rows, part[..., None].astype(jnp.bfloat16), 0),
+            lanes,
+            preferred_element_type=jnp.float32,
+        )
+        for part in (values // base, values % base)
+    )
+    return (high * base + low).astype(jnp.int32).reshape(*mask.shape[:-1], size) - 1
 
 
 def rounds_needed(owner_all, peers, size):
@@ -551,7 +842,7 @@
     return (jnp.max(held) + size - 1) // size
 
 
-def fetch_rows(table_part, tokens_all, peers_here, peer_me):
+def fetch_plan(table_part, tokens_all, peers_here, peer_me):
     peers, rows_each = (peers_here.shape[0], table_part.shape[0])
     count = tokens_all.shape[1]
     size = room(count, peers)
@@ -562,12 +853,13 @@
     own_mask = own_owner[None, :] == jnp.arange(peers)[:, None]
     own_rank = jnp.sum(jnp.where(own_mask, count_before(own_mask), 0), axis=0)
 
-    def one_round(round_no):
+    def to_send(round_no):
         wanted = listed(
-            asked, asked_rank - round_no * size, peers_here - peer_me * rows_each, size, 0
-        )
-        rows = take_rows(table_part, wanted.reshape(-1), jnp.bfloat16)
-        arrived = lax.all_to_all(rows, "vocab", 0, 0, tiled=True)
+            asked, asked_rank - round_no * size, peers_here % rows_each, size
+        )
+        return take_rows(table_part, jnp.maximum(wanted.reshape(-1), 0), jnp.bfloat16)
+
+    def found_in(arrived, round_no):
         rank_now = own_rank - round_no * size
         now = (rank_now >= 0) & (rank_now < size)
         found = take_rows(
@@ -576,14 +868,22 @@
         return (now, found)
 
     def again(round_no, rows):
-        now, found = one_round(round_no)
+        now, found = found_in(swap_rows(to_send(round_no)), round_no)
         return jnp.where(now[:, None], found, rows)
 
     rounds = rounds_needed(tokens_all // rows_each, peers, size)
-    return lax.fori_loop(1, rounds, again, one_round(0)[1])
-
-
-def return_rows(grad_rows, tokens_all, rows_each, dp_size, total):
+
+    def finish(arrived):
+        return lax.fori_loop(1, rounds, again, found_in(arrived, 0)[1])
+
+    return (to_send(0), finish)
+
+
+def swap_rows(rows):
+    return lax.all_to_all(rows, "vocab", 0, 0, tiled=True)
+
+
+def return_plan(tokens_all, rows_each, dp_size):
     peers, count = tokens_all.shape
     along = peers // dp_size
     quarter = rows_each // dp_size
@@ -597,27 +897,39 @@
     leaving_rank = count_before(leaving)
     place = jnp.broadcast_to(jnp.arange(count)[None, :], leaving.shape)
 
-    def one_round(round_no, so_far):
-        chosen = listed(leaving, leaving_rank - round_no * size, place, size, 0)
-        rows = take_rows(grad_rows, chosen.reshape(-1), jnp.bfloat16)
-        arrived = lax.all_to_all(rows, ("dp", "vocab"), 0, 0, tiled=True)
-        where = listed(
-            arriving, arriving_rank - round_no * size, tokens_all % quarter, size, -1
-        )
-        return add_rows(arrived, where.reshape(-1), so_far)
-
-    rounds = rounds_needed(owner_all, peers, size)
-    return lax.fori_loop(1, rounds, one_round, one_round(0, total))
+    def lists(round_no):
+        return (
+            jnp.maximum(
+                listed(leaving, leaving_rank - round_no * size, place, size).reshape(-1), 0
+            ),
+            listed(
+                arriving, arriving_rank - round_no * size, tokens_all % quarter, size
+            ).reshape(-1),
+        )
+
+    return (lists, rounds_needed(owner_all, peers, size))
+
+
+def return_rows(grad_rows, lists, first_lists, rounds, total, ready):
+    def swap_all(rows):
+        return lax.all_to_all(rows, ("dp", "vocab"), 0, 0, tiled=True)
+
+    def again(round_no, so_far):
+        chosen, where = lists(round_no)
+        return add_rows(swap_all(take_rows(grad_rows, chosen, jnp.bfloat16)), where, so_far)
+
+    arrived = swap_all(ready(take_rows(grad_rows, first_lists[0], jnp.bfloat16)))
+    return lax.fori_loop(1, rounds, again, add_rows(arrived, first_lists[1], total))
 
 
 def turn_in(left_basis, tiles, right_basis):
-    half = jnp.einsum("tki,tkl->til", left_basis, tiles, precision=HIGHEST)
-    return jnp.einsum("til,tlj->tij", half, right_basis, precision=HIGHEST)
+    half = jnp.einsum("tki,tkl->til", left_basis, tiles, precision=HIGH)
+    return jnp.einsum("til,tlj->tij", half, right_basis, precision=HIGH)
 
 
 def turn_out(left_basis, tiles, right_basis):
-    half = jnp.einsum("tik,tkl->til", left_basis, tiles, precision=HIGHEST)
-    return jnp.einsum("til,tjl->tij", half, right_basis, precision=HIGHEST)
+    half = jnp.einsum("tik,tkl->til", left_basis, tiles, precision=HIGH)
+    return jnp.einsum("til,tjl->tij", half, right_basis, precision=HIGH)
 
 
 def orthonormal(columns):
@@ -660,8 +972,8 @@
 def renew_bases(left_stat, right_stat, left_basis, right_basis):
     moved = jnp.concatenate(
         [
-            jnp.einsum("tij,tjk->tik", left_stat, left_basis, precision=HIGHEST),
-            jnp.einsum("tij,tjk->tik", right_stat, right_basis, precision=HIGHEST),
+            jnp.einsum("tij,tjk->tik", left_stat, left_basis, precision=HIGH),
+            jnp.einsum("tij,tjk->tik", right_stat, right_basis, precision=HIGH),
         ],
         0,
     )
@@ -673,11 +985,20 @@
 
 
 def soap_update(
-    master, grad_tiles, first_mom, second_mom, left_stat, right_stat, left_basis, right_basis
+    master,
+    grad_tiles,
+    first_mom,
+    first_turned,
+    second_mom,
+    left_stat,
+    right_stat,
+    left_basis,
+    right_basis,
+    factor,
 ):
-    first_new = BETA_FIRST * first_mom + (1 - BETA_FIRST) * grad_tiles
-    grad_turned = turn_in(left_basis, grad_tiles, right_basis)
-    first_turned = turn_in(left_basis, first_new, right_basis)
+    first_new = BETA_FIRST * first_mom + (1 - BETA_FIRST) * (factor * grad_tiles)
+    grad_turned = factor * turn_in(left_basis, grad_tiles, right_basis)
+    first_turned = BETA_FIRST * first_turned + (1 - BETA_FIRST) * grad_turned
     second_new = BETA_SECOND * second_mom + (1 - BETA_SECOND) * grad_turned * grad_turned
     direction = (
         first_turned
@@ -687,11 +1008,13 @@
     master_new = master - RATE_MATRIX * (
         turn_out(left_basis, direction, right_basis) + DECAY * master
     )
-    left_new = BETA_STAT * left_stat + (1 - BETA_STAT) * jnp.einsum(
-        "tik,tjk->tij", grad_tiles, grad_tiles, precision=HIGHEST
-    )
-    right_new = BETA_STAT * right_stat + (1 - BETA_STAT) * jnp.einsum(
-        "tki,tkj->tij", grad_tiles, grad_tiles, precision=HIGHEST
+    left_new = BETA_STAT * left_stat + (1 - BETA_STAT) * (
+        factor
+        * (factor * jnp.einsum("tik,tjk->tij", grad_tiles, grad_tiles, precision=HIGH))
+    )
+    right_new = BETA_STAT * right_stat + (1 - BETA_STAT) * (
+        factor
+        * (factor * jnp.einsum("tki,tkj->tij", grad_tiles, grad_tiles, precision=HIGH))
     )
     return (
         master_new,
@@ -758,7 +1081,8 @@
     )
     fact_count = own_facts.shape[0]
     own_facts = jnp.pad(own_facts, (0, -fact_count % 128))
-    facts = lax.all_gather(own_facts, ("dp", "vocab"), axis=0, tiled=False)
+    facts = spread(own_facts, ("dp", "vocab"), devices)
+    slots_later, facts = lax.optimization_barrier((slot_list, facts))
     tokens_all = facts[:, : tokens.shape[0]]
     after = facts[:, tokens.shape[0] :]
     labels_all = after[:, :row_count]
@@ -767,36 +1091,105 @@
     count_all = jnp.sum(counted_all)
     fraction = reach_all / jnp.sum(reach_all)
 
-    every_tile = lax.all_gather(
-        fold_blocks(master_tiles).astype(jnp.bfloat16), ("dp", "vocab"), axis=0, tiled=True
-    )
-    slot_at = jnp.arange(slot_list.shape[0])
-    slot_of = jnp.sum(
-        jnp.where(slot_list[None, :] == slot_at[:, None], slot_at[None, :], 0), axis=1
-    )
-    peers_here = lax.dynamic_slice_in_dim(tokens_all, dp_me * along, along, 0)
-    embedded = fetch_rows(table_master, tokens_all, peers_here, peer_me) * math.sqrt(D)
+    per_device = master_tiles.shape[0]
+    me = dp_me * along + peer_me
+    ranks, early_count = rank_blocks(slot_list, devices, is_encoder)
+    first_size = room_for(per_device, is_encoder)
+    second_size = per_device - first_size
+    place_at = jnp.where(
+        ranks < first_size,
+        jnp.arange(devices)[:, None] * first_size + ranks,
+        devices * first_size
+        + jnp.arange(devices)[:, None] * second_size
+        + ranks
+        - first_size,
+    )
+    late_size = room_for(per_device, is_last)
+    soon_size = per_device - late_size
+    back_ranks, soon_count = rank_blocks(slots_later, devices, lambda mat_no: not is_last(mat_no))
+    soon_plan = exchange_plan(dp_size, along, soon_size)
+    late_plan = exchange_plan(dp_size, along, late_size)
+    back_at = jnp.where(
+        back_ranks < soon_size,
+        places_for(back_ranks, soon_plan, devices),
+        devices * soon_size + places_for(back_ranks - soon_size, late_plan, devices),
+    )
+    place_of, back_of = by_block(slots_later, [place_at.reshape(-1), back_at.reshape(-1)])
+    own_folded = fold_ranked(
+        master_tiles, lax.dynamic_index_in_dim(ranks, me, 0, keepdims=False)
+    )
     src_count, tgt_count = (source_ids.shape[2], target_ids.shape[2])
+
+    def planned(first, length):
+        ids_all = tokens_all[:, first : first + MICRO * length]
+        peers_here = lax.dynamic_slice_in_dim(ids_all, dp_me * along, along, 0)
+        return fetch_plan(table_master, ids_all, peers_here, peer_me)
+
+    source_sent, source_finish = planned(0, src_count)
+    target_sent, target_finish = planned(MICRO * src_count, tgt_count)
+    first_tiles = lax.all_gather(own_folded[:first_size], ("dp", "vocab"), axis=0, tiled=True)
+    own_second, first_tiles, source_arrived = lax.optimization_barrier(
+        (own_folded[first_size:], first_tiles, swap_rows(source_sent))
+    )
+    second_tiles = lax.all_gather(own_second, ("dp", "vocab"), axis=0, tiled=True)
+    encoder_mats = [mat_no for mat_no in range(MATS) if is_encoder(mat_no)]
+    decoder_mats = [mat_no for mat_no in range(MATS) if not is_encoder(mat_no)]
+
+    def lay_with_all():
+        others = lax.all_gather(own_second, ("dp", "vocab"), axis=0, tiled=True)
+        return lay_matrices([first_tiles, others], place_of, encoder_mats)
+
+    def lay_with_first():
+        return lay_matrices([first_tiles], place_of, encoder_mats)
+
+    encoder_set = lax.cond(
+        jnp.max(early_count) > first_size, lay_with_all, lay_with_first
+    )
+    weights = [None] * MATS
+    for mat_no, matrix in zip(encoder_mats, encoder_set):
+        weights[mat_no] = matrix
+
+    def lay_decoder(memory):
+        held, tiles, arrived = lax.optimization_barrier((memory, second_tiles, target_arrived))
+        decoder_set = lay_matrices([first_tiles, tiles], place_of, decoder_mats)
+        for mat_no, matrix in zip(decoder_mats, decoder_set):
+            weights[mat_no] = matrix
+        return (held, with_waves(target_finish(arrived), tgt_count))
+
     wave_set = waves(src_count, D)
-    source_rows = embedded[: MICRO * src_count] + jnp.tile(wave_set, (MICRO, 1))
-    target_rows = embedded[MICRO * src_count :] + jnp.tile(wave_set[:tgt_count], (MICRO, 1))
-    weights = lay_matrices(every_tile, slot_of)
+
+    def with_waves(rows, length):
+        return rows * math.sqrt(D) + jnp.tile(wave_set[:length], (MICRO, 1))
+
+    lists, rounds = return_plan(tokens_all, rows_each, dp_size)
+    source_rows = with_waves(source_finish(source_arrived), src_count)
+    first_turned = turn_in(basis_left, mom1_tiles, basis_right)
+    source_rows, first_lists, first_turned, target_sent = lax.optimization_barrier(
+        (source_rows, lists(0), first_turned, target_sent)
+    )
+    target_arrived = swap_rows(target_sent)
 
     place_rows = (places + jnp.arange(MICRO)[:, None] * tgt_count).reshape(-1)
     kept, exit_rows = forward_all(
-        weights, gains, source_rows, target_rows, source_len, target_len, place_rows
+        weights,
+        gains,
+        source_rows,
+        source_len,
+        target_len,
+        place_rows,
+        lay_decoder,
     )
 
     table_low_part = table_master.astype(jnp.bfloat16)
     exit_count = DEC * row_count
     exit_all = lax.all_gather(exit_rows, ("dp", "vocab"), axis=0, tiled=True)
+    exit_here = spread(exit_rows, "vocab", along).reshape(-1, D)
     label_rows = jnp.tile(labels_all, (1, DEC)).reshape(-1)
     weight_rows = (
         jnp.repeat(fraction, row_count)[None, :] * jnp.tile(counted_all, (1, DEC))
     ).reshape(-1)
     group_rows = along * exit_count
     group_at = dp_me * group_rows
-    exit_here = lax.dynamic_slice_in_dim(exit_all, group_at, group_rows, 0)
     label_here = lax.dynamic_slice_in_dim(label_rows, group_at, group_rows, 0)
     weight_here = lax.dynamic_slice_in_dim(weight_rows, group_at, group_rows, 0)
     logits = linear_tr(exit_here, table_low_part)
@@ -804,8 +1197,8 @@
     summit = jnp.max(logits, axis=1)
     spread_part = jnp.sum(jnp.exp(logits - summit[:, None]), axis=1)
     picked_part = jnp.sum(jnp.where(hit_here, logits, 0.0), axis=1)
-    stats = lax.all_gather(
-        jnp.stack([summit, spread_part, picked_part]), ("dp", "vocab"), axis=0, tiled=False
+    stats = spread(
+        jnp.stack([summit, spread_part, picked_part]), ("dp", "vocab"), devices
     ).reshape(dp_size, along, 3, group_rows)
     summit_all = jnp.max(stats[:, :, 0], axis=1)
     total_all = jnp.sum(stats[:, :, 1] * jnp.exp(stats[:, :, 0] - summit_all[:, None]), axis=1)
@@ -829,8 +1222,36 @@
 
     matrix_store = [None] * MATS
     gain_store = [None] * GAINS
+    soon_mats = [mat_no for mat_no in range(MATS) if not is_last(mat_no)]
+    late_mats = [mat_no for mat_no in range(MATS) if is_last(mat_no)]
+    both = [devices * soon_size, devices * late_size]
+    held = {}
+
+    def before_last(grad_stream):
+        blocks, held["begun"] = fold_gradients(matrix_store, soon_mats, back_of, both)
+        grad_stream, blocks = lax.optimization_barrier((grad_stream, blocks))
+        held["total"] = first_exchange(blocks, devices)
+        return grad_stream
+
+    def between_last(value):
+        if "parts" not in held:
+            value, total = lax.optimization_barrier((value, held["total"]))
+            held["parts"], held["done"] = (split_parts(total, soon_plan, devices), 0)
+        elif held["done"] < len(soon_plan[0][1]):
+            parts = one_exchange(held["parts"], soon_plan, held["done"], devices)
+            value, held["parts"] = lax.optimization_barrier((value, parts))
+            held["done"] += 1
+        return value
+
     grad_source, grad_target = backward_all(
-        weights, gains, kept, exit_grads, matrix_store, gain_store
+        weights,
+        gains,
+        kept,
+        exit_grads,
+        matrix_store,
+        gain_store,
+        before_last,
+        between_last,
     )
 
     first_row = peer_me * rows_each + dp_me * quarter
@@ -840,21 +1261,45 @@
         linear_tr(exit_all, table_quarter), spread_all.reshape(-1), weight_rows, hit_quarter
     )
     grad_quarter = outer_sum(grads_quarter, exit_all)
+    grad_source = between_last(grad_source)
     grad_rows = jnp.concatenate([grad_source, grad_target], 0) * math.sqrt(D)
-    grad_quarter = return_rows(grad_rows, tokens_all, rows_each, dp_size, grad_quarter)
-
-    owned_grad = unfold_blocks(
-        lax.psum_scatter(
-            lax.psum_scatter(
-                fold_gradients(matrix_store, slot_of), "dp", scatter_dimension=0, tiled=True
-            ),
-            "vocab",
-            scatter_dimension=0,
-            tiled=True,
-        ).astype(jnp.float32)
+    grad_rows = between_last(grad_rows)
+    [late_blocks] = fold_gradients(matrix_store, late_mats, back_of, both, held["begun"])
+    late_parts = split_parts(first_exchange(late_blocks, devices), late_plan, devices)
+    late_parts = one_exchange(late_parts, late_plan, 0, devices)
+
+    def ready(rows):
+        rows = between_last(rows)
+        rows, held["late"] = lax.optimization_barrier((rows, late_parts))
+        return rows
+
+    grad_quarter = return_rows(grad_rows, lists, first_lists, rounds, grad_quarter, ready)
+
+    soon_sum = other_exchanges(held["parts"], soon_plan, devices, held["done"])
+    late_sum = other_exchanges(held["late"], late_plan, devices, 1)
+
+    def exchange_again():
+        blocks, _ = fold_gradients(matrix_store, list(range(MATS)), back_of, both)
+        parts = split_parts(first_exchange(blocks, devices), soon_plan, devices)
+        return other_exchanges(parts, soon_plan, devices)
+
+    soon_sum = lax.cond(
+        jnp.min(soon_count) < soon_size, exchange_again, lambda: soon_sum
+    )
+    owned_grad = unfold_ranked(
+        jnp.concatenate([soon_sum, late_sum], 0),
+        lax.dynamic_index_in_dim(back_ranks, me, 0, keepdims=False),
     )
     squares = jnp.sum(owned_grad * owned_grad) + jnp.sum(grad_quarter * grad_quarter)
-    gain_total, square_total = lax.psum((jnp.stack(gain_store), squares), ("dp", "vocab"))
+    square_total = jnp.sum(
+        spread(jnp.full((1, 128), squares), ("dp", "vocab"), devices)[:, 0, 0]
+    )
+    share = -(-GAINS * D // (devices * 128)) * 128
+    gain_flat = jnp.stack(gain_store).reshape(-1)
+    gain_flat = jnp.pad(gain_flat, (0, devices * share - GAINS * D)).reshape(devices, share)
+    gain_part = jnp.sum(lax.all_to_all(gain_flat, ("dp", "vocab"), 0, 0, tiled=True), axis=0)
+    gain_total = spread(gain_part[None], ("dp", "vocab"), devices).reshape(-1)[: GAINS * D]
+    gain_total = gain_total.reshape(GAINS, D)
     grad_norm = jnp.sqrt(square_total + jnp.sum(gain_total * gain_total))
     factor = jnp.minimum(1.0, CLIP_AT / grad_norm)
     table_grad = lax.all_gather(
@@ -862,13 +1307,15 @@
     ).astype(jnp.float32)
     master_new, mom1_new, mom2_new, left_new, right_new, bleft_new, bright_new = soap_update(
         master_tiles,
-        owned_grad * factor,
+        owned_grad,
         mom1_tiles,
+        first_turned,
         mom2_tiles,
         stat_left,
         stat_right,
         basis_left,
         basis_right,
+        factor,
     )
     table_new, table_m, table_v = adamw_update(
         table_master, table_grad * factor, table_mom1, table_mom2, RATE_MATRIX, DECAY

time: 1660 us -> 1290 us (0.78)
  matrix products: 534 us -> 265 us
  Pallas kernels: 170 us -> 392 us
  other arithmetic: 283 us -> 144 us
  blocking collectives: 127 us -> 0 us
  waiting for transfers between devices: 324 us -> 221 us
  starting transfers between devices: 12.1 us -> 72.4 us
    dot_general x82 -> x18, matrix products: 298 us -> 59.8 us  [the longest x8 10.4 us: listed(): jnp.einsum('...th,...tl->...hl', jnp.where(rows, part[..., None].astype(j...]
    pallas_call x2 -> x17, Pallas kernels: 70.5 us -> 274 us  [the longest x6 123 us: attend_backward(): pl.pallas_call(kernel, out_shape=(jax.ShapeDtypeStruct((MICRO * rows, D),...]
    reduce_scatter x2 -> x0, waiting for transfers between devices: 144 us -> none  [the longest x1 90.2 us: per_device(): lax.psum_scatter(fold_gradients(matrix_store, slot_of), 'dp', scatter_dim...]
    ppermute x0 -> x26, waiting for transfers between devices: none -> 90.5 us  [halve(): arrived = lax.ppermute(sent, ('dp', 'vocab'), pairs)]
    all_gather x2 -> x0, blocking collectives: 87.9 us -> none  [the longest x1 47.5 us: per_device(): facts = lax.all_gather(own_facts, ('dp', 'vocab'), axis=0, tiled=False)]
    reduce_sum x16 -> x4, other arithmetic: 70.7 us -> 0.91 us  [the longest x1 0.63 us: per_device(): jnp.sum(spread(jnp.full((1, 128), squares), ('dp', 'vocab'), devices)[:,...]
    convert_element_type x14 -> x19, other arithmetic: 57.7 us -> 18.9 us  [the longest x2 11 us: first_exchange(): return halve(folded, 0, devices).astype(jnp.bfloat16)]
    psum x1 -> x0, blocking collectives: 38.6 us -> none  [per_device(): lax.psum((jnp.stack(gain_store), squares), ('dp', 'vocab'))]
  transfers between devices with their start and end apart: 8 -> 40, of which waited for: 6 -> 19; matrix products, arithmetic and copies ran while one was open for 17% -> 24% of each run, Pallas kernels for 6% -> 18%
where the time goes in v2:
time: 1290 us
  Pallas kernels  392 us (30%)
  matrix products  265 us (21%)
  waiting for transfers between devices  221 us (17%)
  local copies, waits for them, and re-layouts  170 us (13%)
  other arithmetic  144 us (11%)
  starting transfers between devices  72.4 us (6%)
  between operations  25 us (2%)
    pallas_call x6, Pallas kernels, attend_backward(): pl.pallas_call(kernel, out_shape=(jax.ShapeDtypeStruct((MICRO * rows, D),...  123 us
    unnamed x515, local copies, waits for them, and re-layouts  114 us
    ppermute x26, waiting for transfers between devices, halve(): arrived = lax.ppermute(sent, ('dp', 'vocab'), pairs)  90.5 us
    pallas_call x5, Pallas kernels, attend_forward(): pl.pallas_call(kernel, out_shape=(jax.ShapeDtypeStruct((MICRO * rows, D),...  84.3 us
    dot_general x23, matrix products, outer_sum(): lax.dot_general(left_op, right_op, (((0,), (0,)), ((), ())), preferred_el...  72.3 us
    dot_general x19, matrix products, linear(): return jnp.dot(left_op, right_op, preferred_element_type=jnp.float32)  71.1 us
    all_to_all x2, waiting for transfers between devices, swap_rows(): return lax.all_to_all(rows, 'vocab', 0, 0, tiled=True)  63.2 us
    dot_general x19, matrix products, linear_tr(): lax.dot_general(left_op, right_op, (((1,), (1,)), ((), ())), preferred_el...  60.3 us
  transfers between devices with their start and end apart: 40, of which 19 were waited for; matrix products, arithmetic and copies ran while one was open for 24% of the time, Pallas kernels for 18%

profile of v2, /device:TPU:0, one launch (start us, length us, event | category | flops | bytes accessed | tf_op | source)
XLA Modules:
  0.0 1289.3 jit_solution(6654205173098343887)
XLA Ops:
  64.2 15.9 %all-to-all-done.3 = s32[32,1,2688]{2,1,0:T(1,128)S(1)} async-done(((s32[32,1,2688]{2,1,0:T(1,128)}), s32[32,1,2688]{2,1,0:T(1,128)S(1)}, u32[]{:S(2)}, u32[]{:S(2)}) %all-to-all-start.3) | async-done | bytes 344096 | tf_op jit(solution)/shard_map/all_to_all | solution.py:803
  84.5 16.6 %shard_map.332 = bf16[2688,512]{1,0:T(8,128)(2,1)} custom-call(s32[2688]{0:T(1024)S(1)} %max.32.index_ref, f32[4096,512]{1,0:T(8,128)} %source_ref.3), custom_call_target="tpu_custom_call" | custom-call | tf_op jit(solution)/shard_map/pallas_call | solution.py:754
  123.7 54.1 %all-to-all-done.4 = bf16[8,336,512]{2,1,0:T(8,128)(2,1)S(1)} async-done(((bf16[8,336,512]{2,1,0:T(8,128)(2,1)}), bf16[8,336,512]{2,1,0:T(8,128)(2,1)S(1)}, u32[]{:S(2)}, u32[]{:S(2)}) %all-to-all-start.4) | async-done | bytes 2752544 | tf_op jit(solution)/shard_map/all_to_all | solution.py:883
  177.7 14.8 %conditional.2 = (bf16[512,2048]{1,0:T(8,128)(2,1)}, bf16[512,2048]{1,0:T(8,128)(2,1)}, bf16[512,2048]{1,0:T(8,128)(2,1)S(1)}, bf16[512,2048]{1,0:T(8,128)(2,1)}, bf16[512,2048]{1,0:T(8,128)(2,1)}) conditional(s32[]{:T(128)} %convert_element_type.1086, (s32[2816]{0:T(1024)S(1)}, bf16[1408,32,128]{2,1,0:T(8,128)(2,1)}) %tuple.99, ...), branch_computations={%region_26.27_spmd, %region_27.28_spmd} | conditional | bytes 90210416 | solution.py:1145
  177.7 10.0 branch_0_fun.1
  203.3 8.6 shard_map.334
  213.9 10.7 shard_map.333
  235.3 46.6 %shard_map.335 = (bf16[2048,512]{1,0:T(8,128)(2,1)S(1)}, f32[2048,512]{1,0:T(8,128)S(1)}) custom-call(s32[2]{0:T(128)S(1)} %bitcast.503, bf16[2048,1536]{1,0:T(8,128)(2,1)S(1)} %convolution_convert_fusion.query_ref.key_ref.value_ref, bf16[2048,1536]{1,0:T(8,128)(2,1)S(1)} %convolution_convert_fusion.query_ref.key_ref.value_ref, ...), custom_call_target="tpu_custom_call" | custom-call | flops 4294967296 | bytes 16777216 | tf_op jit(solution)/shard_map/pallas_call | solution.py:112
  284.9 11.3 fusion.559
  299.8 10.7 multiply_reduce_fusion.6
  314.3 9.2 all-to-all-done.5
  324.4 20.0 %shard_map.337 = (bf16[512,2048]{1,0:T(8,128)(2,1)S(1)}, bf16[512,2048]{1,0:T(8,128)(2,1)S(1)}, bf16[512,2048]{1,0:T(8,128)(2,1)S(1)}, bf16[512,2048]{1,0:T(8,12...) custom-call(s32[2816]{0:T(1024)S(1)} %reshape.1991.place_ref, ...), custom_call_target="tpu_custom_call" | custom-call | tf_op jit(solution)/shard_map/pallas_call | solution.py:573
  369.7 12.9 %shard_map.339 = (bf16[512,512]{1,0:T(8,128)(2,1)S(1)}, f32[512,512]{1,0:T(8,128)S(1)}) custom-call(s32[2]{0:T(128)S(1)} %bitcast.504, bf16[512,512]{1,0:T(8,128)(2,1)S(1)} %convolution_convert_fusion.29.query_ref, bf16[2048,1024]{1,0:T(8,128)(2,1)S(1)} %convolution_convert_fusion.2.key_ref.value_ref, ...), custom_call_target="tpu_custom_call" | custom-call | flops 1073741824 | bytes 10485760 | tf_op jit(solution)/shard_map/pallas_call | solution.py:112
  404.6 13.1 %shard_map.341 = (bf16[512,512]{1,0:T(8,128)(2,1)S(1)}, f32[512,512]{1,0:T(8,128)S(1)}) custom-call(s32[2]{0:T(128)S(1)} %bitcast.505, bf16[512,512]{1,0:T(8,128)(2,1)S(1)} %convolution_convert_fusion.28.query_ref, bf16[2048,1024]{1,0:T(8,128)(2,1)S(1)} %convolution_convert_fusion.1.key_ref.value_ref, ...), custom_call_target="tpu_custom_call" | custom-call | flops 1073741824 | bytes 10485760 | tf_op jit(solution)/shard_map/pallas_call | solution.py:112
  487.1 11.0 all-to-all-done.8
  515.7 19.8 %shard_map.342 = (bf16[512,512]{1,0:T(8,128)(2,1)S(1)}, bf16[2048,512]{1,0:T(8,128)(2,1)S(1)}, bf16[2048,512]{1,0:T(8,128)(2,1)S(1)}) custom-call(s32[2]{0:T(128)S(1)} %bitcast.506, bf16[512,512]{1,0:T(8,128)(2,1)S(1)} %convolution_convert_fusion.28.query_ref, bf16[2048,1024]{1,0:T(8,128)(2,1)S(1)} %copy-done.7, bf16[2048,1024]{1,0:T(8,128)(2,1)S(1)} %copy-done.7, ...), custom_call_target="tpu_custom_call" | custom-call | flops 2684354560 | bytes 20971520 | tf_op jit(solution)/shard_map/pallas_call | solution.py:188
  571.1 20.0 %shard_map.344 = (bf16[512,512]{1,0:T(8,128)(2,1)S(1)}, bf16[2048,512]{1,0:T(8,128)(2,1)S(1)}, bf16[2048,512]{1,0:T(8,128)(2,1)S(1)}) custom-call(s32[2]{0:T(128)S(1)} %bitcast.507, bf16[512,512]{1,0:T(8,128)(2,1)S(1)} %convolution_convert_fusion.29.query_ref, bf16[2048,1024]{1,0:T(8,128)(2,1)S(1)} %copy-done.5, bf16[2048,1024]{1,0:T(8,128)(2,1)S(1)} %copy-done.5, ...), custom_call_target="tpu_custom_call" | custom-call | flops 2684354560 | bytes 20971520 | tf_op jit(solution)/shard_map/pallas_call | solution.py:188
  605.5 12.6 convolution_convert_fusion.11.refs_7_
  618.1 18.2 %fusion.160 = bf16[2048,2048]{1,0:T(8,128)(2,1)} fusion(f32[2048,2048]{1,0:T(8,128)} %fusion.559, bf16[512,2048]{1,0:T(8,128)(2,1)} %get-tuple-element.827, f32[2048,512]{1,0:T(8,128)S(1)} %add_add_fusion.2), kind=kOutput, calls=%fused_computation.248 | convolution fusion | flops 4379901952 | bytes 31457280 | tf_op jit(solution)/shard_map/dot_general | solution.py:52
  652.9 9.5 convolution_convert_fusion.14.refs_4_
  662.5 11.4 multiply_reduce_fusion.1
  695.5 19.6 %shard_map.346 = (bf16[2048,32,128]{2,1,0:T(8,128)(2,1)}, bf16[768,32,128]{2,1,0:T(8,128)(2,1)S(1)}) custom-call(s32[2816]{0:T(1024)S(1)} %copy-done.163, bf16[512,2048]{1,0:T(8,128)(2,1)S(1)} %pad_maximum_fusion.3.refs_0_, bf16[512,2048]{1,0:T(8,128)(2,1)S(1)} %pad_maximum_fusion.4.refs_1_, bf16[512,2048]{1,0:T(8,128)(2,1)S(1)} %pad_maximum_fusion.5.refs_2_, ...), custom_call_target="tpu_custom_call" | custom-call | tf_op jit(solution)/shard_map/pallas_call | solution.py:654
  736.3 34.3 %shard_map.347 = (bf16[2048,512]{1,0:T(8,128)(2,1)S(1)}, bf16[2048,512]{1,0:T(8,128)(2,1)S(1)}, bf16[2048,512]{1,0:T(8,128)(2,1)S(1)}) custom-call(s32[2]{0:T(128)S(1)} %bitcast.508, bf16[2048,1536]{1,0:T(8,128)(2,1)} %copy-done.1, bf16[2048,1536]{1,0:T(8,128)(2,1)} %copy-done.1, bf16[2048,1536]{1,0:T(8,128)(2,1)} %copy-done.1, f32[2048,512]{1,0:T(8,128)S(1)} %copy-done.14, ...), custom_call_target="tpu_custom_call" | custom-call | flops 5368709120 | bytes 16777216 | tf_op jit(solution)/shard_map/pallas_call | solution.py:188
  784.8 34.4 %shard_map.348 = (bf16[2048,512]{1,0:T(8,128)(2,1)S(1)}, bf16[2048,512]{1,0:T(8,128)(2,1)S(1)}, bf16[2048,512]{1,0:T(8,128)(2,1)S(1)}) custom-call(s32[2]{0:T(128)S(1)} %bitcast.509, bf16[2048,1536]{1,0:T(8,128)(2,1)} %copy-done.1, bf16[2048,1536]{1,0:T(8,128)(2,1)} %copy-done.1, ...), custom_call_target="tpu_custom_call", output_to_operand_aliasing={{0}: (6, {}), {1}: (7, {}), {2}: (8, {})} | custom-call | flops 5368709120 | bytes 16777216 | tf_op jit(solution)/shard_map/pallas_call | solution.py:188
  867.4 20.7 %all-to-all-done.11 = f32[32,1,256]{2,1,0:T(1,128)S(1)} async-done(((f32[32,1,256]{2,1,0:T(1,128)}), f32[32,1,256]{2,1,0:T(1,128)S(1)}, u32[]{:S(2)}, u32[]{:S(2)}) %all-to-all-start.11) | async-done | bytes 32800 | tf_op jit(solution)/shard_map/all_to_all | solution.py:1300
  903.0 8.4 collective-permute-done.21
  914.9 17.2 %shard_map.349 = bf16[4096,512]{1,0:T(8,128)(2,1)S(1)} custom-call(s32[4096]{0:T(1024)S(1)} %max.34.index_ref, f32[2560,512]{1,0:T(8,128)S(1)} %maximum_multiply_fusion.source_ref), custom_call_target="tpu_custom_call" | custom-call | tf_op jit(solution)/shard_map/pallas_call | solution.py:754
  1013.0 29.7 %collective-permute-done.33 = bf16[32,32,128]{2,1,0:T(8,128)(2,1)S(1)} collective-permute-done((bf16[32,32,128]{2,1,0:T(8,128)(2,1)S(1)}, bf16[32,32,128]{2,1,0:T(8,128)(2,1)S(1)}, u32[]{:S(2)}, u32[]{:S(2)}) %collective-permute-start.33) | collective-permute-done | bytes 262176 | tf_op jit(solution)/shard_map/ppermute | solution.py:705
  1049.0 27.8 %collective-permute-done.36 = bf16[32,32,128]{2,1,0:T(8,128)(2,1)S(1)} collective-permute-done((bf16[32,32,128]{2,1,0:T(8,128)(2,1)S(1)}, bf16[32,32,128]{2,1,0:T(8,128)(2,1)S(1)}, u32[]{:S(2)}, u32[]{:S(2)}) %collective-permute-start.36) | collective-permute-done | bytes 262176 | tf_op jit(solution)/shard_map/ppermute | solution.py:705
  1096.7 9.4 shard_map.352
  1168.6 51.8 %shard_map.353 = f32[64,64,256]{2,1,0:T(8,128)S(1)} custom-call(f32[64,64,256]{2,1,0:T(8,128)S(1)} %pad.19.in_ref), custom_call_target="tpu_custom_call" | custom-call | tf_op jit(solution)/shard_map/pallas_call | solution.py:962
  1258.4 23.1 %fusion.562 = (bf16[4096,512]{1,0:T(8,128)(2,1)}, f32[4096,512]{1,0:T(8,128)}, f32[4096,512]{1,0:T(8,128)}, f32[4096,512]{1,0:T(8,128)}) fusion(f32[4096,512]{1,0:T(8,128)} %get-tuple-element.1670, f32[]{:T(128)S(6)} %min.3, bf16[4096,512]{1,0:T(8,128)(2,1)} %all-gather.14.cloned.1.call-done, f32[4096,512]{1,0:T(8,128)} %param.38, f32[4096,512]{1,0:T(8,128)} %param.39), kind=kLoop, calls=%fused_computation.1112 | loop fusion | flops 37748736 | bytes 58720260 | tf_op jit(solution)/shard_map/convert_element_type | solution.py:1339
  (985 shorter events, 645.7 us)
Async XLA Ops:
  7.2 170.5 %all-gather.8.cloned.1.call-start = ((), (), s32[]{:S(2)}) async-start(), calls=%async_computation.14 | async-start | bytes 11894784 | tf_op jit(solution)/shard_map/all_gather | solution.py:1130
  56.2 23.9 %all-to-all-start.3 = ((s32[32,1,2688]{2,1,0:T(1,128)}), s32[32,1,2688]{2,1,0:T(1,128)S(1)}, u32[]{:S(2)}, u32[]{:S(2)}) async-start(s32[32,1,2688]{2,1,0:T(1,128)} %broadcast_in_dim.472), calls=%async_computation.3 | async-start | bytes 688128 | tf_op jit(solution)/shard_map/all_to_all | solution.py:803
  101.8 75.9 %all-to-all-start.4 = ((bf16[8,336,512]{2,1,0:T(8,128)(2,1)}), bf16[8,336,512]{2,1,0:T(8,128)(2,1)S(1)}, u32[]{:S(2)}, u32[]{:S(2)}) async-start(bf16[8,336,512]{2,1,0:T(8,128)(2,1)} %bitcast.58), calls=%async_computation.4 | async-start | bytes 5505024 | tf_op jit(solution)/shard_map/all_to_all | solution.py:883
  192.5 131.0 %all-gather.10.cloned.1.call-start = ((), (), s32[]{:S(2)}) async-start(), calls=%async_computation.15 | async-start | bytes 11894784 | tf_op jit(solution)/shard_map/all_gather | solution.py:1134
  296.2 27.3 %all-to-all-start.5 = ((bf16[8,112,512]{2,1,0:T(8,128)(2,1)}), bf16[8,112,512]{2,1,0:T(8,128)(2,1)S(1)}, u32[]{:S(2)}, u32[]{:S(2)}) async-start(bf16[8,112,512]{2,1,0:T(8,128)(2,1)} %bitcast.67), calls=%async_computation.5 | async-start | bytes 1835008 | tf_op jit(solution)/shard_map/all_to_all | solution.py:883
  429.2 18.8 %all-to-all-start.6 = ((bf16[8,64,512]{2,1,0:T(8,128)(2,1)}), bf16[8,64,512]{2,1,0:T(8,128)(2,1)S(1)}, u32[]{:S(2)}, u32[]{:S(2)}) async-start(bf16[8,64,512]{2,1,0:T(8,128)(2,1)} %broadcast_in_dim.492), calls=%async_computation.6 | async-start | bytes 1048576 | tf_op jit(solution)/shard_map/all_to_all | solution.py:803
  456.8 13.0 %all-to-all-start.7 = ((f32[32,3,512]{2,1,0:T(4,128)}), f32[32,3,512]{2,1,0:T(4,128)S(1)}, u32[]{:S(2)}, u32[]{:S(2)}) async-start(f32[32,3,512]{2,1,0:T(4,128)} %broadcast_in_dim.494), calls=%async_computation.7 | async-start | bytes 524288 | tf_op jit(solution)/shard_map/all_to_all | solution.py:803
  479.2 18.9 %all-to-all-start.8 = ((bf16[8,64,512]{2,1,0:T(8,128)(2,1)}), bf16[8,64,512]{2,1,0:T(8,128)(2,1)S(1)}, u32[]{:S(2)}, u32[]{:S(2)}) async-start(bf16[8,64,512]{2,1,0:T(8,128)(2,1)} %bitcast.604), calls=%async_computation.8 | async-start | bytes 1048576 | tf_op jit(solution)/shard_map/all_to_all | solution.py:1218
  482.9 502.8 %all-gather.12.cloned.1.call-start = ((), (), s32[]{:S(2)}) async-start(), calls=%async_computation.16 | async-start | bytes 2162688 | tf_op jit(solution)/shard_map/all_gather | solution.py:1185
  726.0 44.6 %collective-permute-start.13 = (bf16[1024,32,128]{2,1,0:T(8,128)(2,1)}, bf16[1024,32,128]{2,1,0:T(8,128)(2,1)}, u32[]{:S(2)}, u32[]{:S(2)}) collective-permute-start(bf16[1024,32,128]{2,1,0:T(8,128)(2,1)} %dynamic-slice_bitcast_fusion.13), channel_id=1, source_target_pairs={{0,1},{1,0},{2,3},{3,2},{4,5},{5,4},{6,7},{7,6},{8,9},{9,8},{10,11... | collective-permute-start | bytes 25165832 | tf_op jit(solution)/shard_map/ppermute | solution.py:705
  780.8 39.0 %collective-permute-start.16 = (bf16[168,32,128]{2,1,0:T(8,128)(2,1)}, bf16[168,32,128]{2,1,0:T(8,128)(2,1)}, u32[]{:S(2)}, u32[]{:S(2)}) collective-permute-start(bf16[168,32,128]{2,1,0:T(8,128)(2,1)} %dynamic-slice_bitcast_fusion.16), channel_id=1, source_target_pairs={{0,2},{1,3},{2,0},{3,1},{4,6},{5,7},{6,4},{7,5},{8,10},{9,11},{10,... | collective-permute-start | bytes 4128776 | tf_op jit(solution)/shard_map/ppermute | solution.py:705
  783.1 40.7 %collective-permute-start.15 = (bf16[168,32,128]{2,1,0:T(8,128)(2,1)}, bf16[168,32,128]{2,1,0:T(8,128)(2,1)S(1)}, u32[]{:S(2)}, u32[]{:S(2)}) collective-permute-start(bf16[168,32,128]{2,1,0:T(8,128)(2,1)} %dynamic-slice_bitcast_fusion.17), channel_id=1, source_target_pairs={{0,16},{1,17},{2,18},{3,19},{4,20},{5,21},{6,22},{7,23},{8,24},{9,... | collective-permute-start | bytes 4128776 | tf_op jit(solution)/shard_map/ppermute | solution.py:705
  783.9 41.4 %collective-permute-start.14 = (bf16[176,32,128]{2,1,0:T(8,128)(2,1)S(1)}, bf16[176,32,128]{2,1,0:T(8,128)(2,1)S(1)}, u32[]{:S(2)}, u32[]{:S(2)}) collective-permute-start(bf16[176,32,128]{2,1,0:T(8,128)(2,1)S(1)} %dynamic-slice_bitcast_fusion.15), channel_id=1, source_target_pairs={{0,8},{1,9},{2,10},{3,11},{4,12},{5,13},{6,14},{7,15},{8,0},{9,1},... | collective-permute-start | bytes 4325384 | tf_op jit(solution)/shard_map/ppermute | solution.py:705
  850.4 82.7 %collective-permute-start.26 = (bf16[384,32,128]{2,1,0:T(8,128)(2,1)}, bf16[384,32,128]{2,1,0:T(8,128)(2,1)}, u32[]{:S(2)}, u32[]{:S(2)}) collective-permute-start(bf16[384,32,128]{2,1,0:T(8,128)(2,1)} %dynamic-slice_bitcast_fusion.14), channel_id=1, source_target_pairs={{0,1},{1,0},{2,3},{3,2},{4,5},{5,4},{6,7},{7,6},{8,9},{9,8},{10,11... | collective-permute-start | bytes 9437192 | tf_op jit(solution)/shard_map/ppermute | solution.py:705
  851.3 38.3 %collective-permute-start.19 = (bf16[84,32,128]{2,1,0:T(8,128)(2,1)}, bf16[84,32,128]{2,1,0:T(8,128)(2,1)}, u32[]{:S(2)}, u32[]{:S(2)}) collective-permute-start(bf16[84,32,128]{2,1,0:T(8,128)(2,1)} %dynamic-slice_bitcast_fusion.19), channel_id=1, source_target_pairs={{0,4},{1,5},{2,6},{3,7},{4,0},{5,1},{6,2},{7,3},{8,12},{9,13},{10,... | collective-permute-start | bytes 2064392 | tf_op jit(solution)/shard_map/ppermute | solution.py:705
  853.7 34.4 %collective-permute-start.18 = (bf16[84,32,128]{2,1,0:T(8,128)(2,1)}, bf16[84,32,128]{2,1,0:T(8,128)(2,1)}, u32[]{:S(2)}, u32[]{:S(2)}) collective-permute-start(bf16[84,32,128]{2,1,0:T(8,128)(2,1)} %dynamic-slice_bitcast_fusion.20), channel_id=1, source_target_pairs={{0,2},{1,3},{2,0},{3,1},{4,6},{5,7},{6,4},{7,5},{8,10},{9,11},{10,... | collective-permute-start | bytes 2064392 | tf_op jit(solution)/shard_map/ppermute | solution.py:705
  855.0 36.1 %collective-permute-start.17 = (bf16[88,32,128]{2,1,0:T(8,128)(2,1)}, bf16[88,32,128]{2,1,0:T(8,128)(2,1)}, u32[]{:S(2)}, u32[]{:S(2)}) collective-permute-start(bf16[88,32,128]{2,1,0:T(8,128)(2,1)} %dynamic-slice_bitcast_fusion.18), channel_id=1, source_target_pairs={{0,16},{1,17},{2,18},{3,19},{4,20},{5,21},{6,22},{7,23},{8,24},{9,... | collective-permute-start | bytes 2162696 | tf_op jit(solution)/shard_map/ppermute | solution.py:705
  856.4 31.7 %all-to-all-start.11 = ((f32[32,1,256]{2,1,0:T(1,128)}), f32[32,1,256]{2,1,0:T(1,128)S(1)}, u32[]{:S(2)}, u32[]{:S(2)}) async-start(f32[32,1,256]{2,1,0:T(1,128)} %bitcast.182), calls=%async_computation.11 | async-start | bytes 65536 | tf_op jit(solution)/shard_map/all_to_all | solution.py:1300
  893.4 18.0 %collective-permute-start.21 = (bf16[42,32,128]{2,1,0:T(8,128)(2,1)S(1)}, bf16[42,32,128]{2,1,0:T(8,128)(2,1)S(1)}, u32[]{:S(2)}, u32[]{:S(2)}) collective-permute-start(bf16[42,32,128]{2,1,0:T(8,128)(2,1)S(1)} %dynamic-slice_bitcast_fusion.26), channel_id=1, source_target_pairs={{0,4},{1,5},{2,6},{3,7},{4,0},{5,1},{6,2},{7,3},{8,12},{9,13},{10,... | collective-permute-start | bytes 1032200 | tf_op jit(solution)/shard_map/ppermute | solution.py:705
  894.0 17.5 %collective-permute-start.20 = (bf16[44,32,128]{2,1,0:T(8,128)(2,1)S(1)}, bf16[44,32,128]{2,1,0:T(8,128)(2,1)S(1)}, u32[]{:S(2)}, u32[]{:S(2)}) collective-permute-start(bf16[44,32,128]{2,1,0:T(8,128)(2,1)S(1)} %dynamic-slice_bitcast_fusion.24), channel_id=1, source_target_pairs={{0,2},{1,3},{2,0},{3,1},{4,6},{5,7},{6,4},{7,5},{8,10},{9,11},{10,... | collective-permute-start | bytes 1081352 | tf_op jit(solution)/shard_map/ppermute | solution.py:705
  911.7 20.5 %collective-permute-start.25 = (bf16[21,32,128]{2,1,0:T(8,128)(2,1)S(1)}, bf16[21,32,128]{2,1,0:T(8,128)(2,1)S(1)}, u32[]{:S(2)}, u32[]{:S(2)}) collective-permute-start(bf16[21,32,128]{2,1,0:T(8,128)(2,1)S(1)} %dynamic-slice_bitcast_fusion.31), channel_id=1, source_target_pairs={{0,16},{1,17},{2,18},{3,19},{4,20},{5,21},{6,22},{7,23},{8,24},{9,... | collective-permute-start | bytes 516104 | tf_op jit(solution)/shard_map/ppermute | solution.py:705
  912.5 26.4 %collective-permute-start.24 = (bf16[21,32,128]{2,1,0:T(8,128)(2,1)S(1)}, bf16[21,32,128]{2,1,0:T(8,128)(2,1)S(1)}, u32[]{:S(2)}, u32[]{:S(2)}) collective-permute-start(bf16[21,32,128]{2,1,0:T(8,128)(2,1)S(1)} %dynamic-slice_bitcast_fusion.32), channel_id=1, source_target_pairs={{0,8},{1,9},{2,10},{3,11},{4,12},{5,13},{6,14},{7,15},{8,0},{9,1},... | collective-permute-start | bytes 516104 | tf_op jit(solution)/shard_map/ppermute | solution.py:705
  913.9 28.7 %collective-permute-start.23 = (bf16[22,32,128]{2,1,0:T(8,128)(2,1)S(1)}, bf16[22,32,128]{2,1,0:T(8,128)(2,1)S(1)}, u32[]{:S(2)}, u32[]{:S(2)}) collective-permute-start(bf16[22,32,128]{2,1,0:T(8,128)(2,1)S(1)} %dynamic-slice_bitcast_fusion.30), channel_id=1, source_target_pairs={{0,4},{1,5},{2,6},{3,7},{4,0},{5,1},{6,2},{7,3},{8,12},{9,13},{10,... | collective-permute-start | bytes 540680 | tf_op jit(solution)/shard_map/ppermute | solution.py:705
  937.0 12.6 collective-permute-start.29
  941.8 15.2 %collective-permute-start.27 = (bf16[64,32,128]{2,1,0:T(8,128)(2,1)}, bf16[64,32,128]{2,1,0:T(8,128)(2,1)}, u32[]{:S(2)}, u32[]{:S(2)}) collective-permute-start(bf16[64,32,128]{2,1,0:T(8,128)(2,1)} %dynamic-slice_bitcast_fusion.23), channel_id=1, source_target_pairs={{0,8},{1,9},{2,10},{3,11},{4,12},{5,13},{6,14},{7,15},{8,0},{9,1},... | collective-permute-start | bytes 1572872 | tf_op jit(solution)/shard_map/ppermute | solution.py:705
  964.3 132.3 %all-to-all-start.9 = ((bf16[32,128,512]{2,1,0:T(8,128)(2,1)}), bf16[32,128,512]{2,1,0:T(8,128)(2,1)}, u32[]{:S(2)}, u32[]{:S(2)}) async-start(bf16[32,128,512]{2,1,0:T(8,128)(2,1)} %bitcast.501), calls=%async_computation.9 | async-start | bytes 8388608 | tf_op jit(solution)/shard_map/all_to_all | solution.py:915
  994.8 15.2 %collective-permute-start.30 = (bf16[32,32,128]{2,1,0:T(8,128)(2,1)}, bf16[32,32,128]{2,1,0:T(8,128)(2,1)}, u32[]{:S(2)}, u32[]{:S(2)}) collective-permute-start(bf16[32,32,128]{2,1,0:T(8,128)(2,1)} %dynamic-slice_bitcast_fusion.29), channel_id=1, source_target_pairs={{0,16},{1,17},{2,18},{3,19},{4,20},{5,21},{6,22},{7,23},{8,24},{9,... | collective-permute-start | bytes 786440 | tf_op jit(solution)/shard_map/ppermute | solution.py:705
  999.9 42.8 %collective-permute-start.33 = (bf16[32,32,128]{2,1,0:T(8,128)(2,1)S(1)}, bf16[32,32,128]{2,1,0:T(8,128)(2,1)S(1)}, u32[]{:S(2)}, u32[]{:S(2)}) collective-permute-start(bf16[32,32,128]{2,1,0:T(8,128)(2,1)S(1)} %dynamic-slice_bitcast_fusion.28), channel_id=1, source_target_pairs={{0,2},{1,3},{2,0},{3,1},{4,6},{5,7},{6,4},{7,5},{8,10},{9,11},{10,... | collective-permute-start | bytes 786440 | tf_op jit(solution)/shard_map/ppermute | solution.py:705
  1001.5 75.2 %collective-permute-start.36 = (bf16[32,32,128]{2,1,0:T(8,128)(2,1)S(1)}, bf16[32,32,128]{2,1,0:T(8,128)(2,1)S(1)}, u32[]{:S(2)}, u32[]{:S(2)}) collective-permute-start(bf16[32,32,128]{2,1,0:T(8,128)(2,1)S(1)} %dynamic-slice_bitcast_fusion.27), channel_id=1, source_target_pairs={{0,4},{1,5},{2,6},{3,7},{4,0},{5,1},{6,2},{7,3},{8,12},{9,13},{10,... | collective-permute-start | bytes 786440 | tf_op jit(solution)/shard_map/ppermute | solution.py:705
  1011.1 67.1 %collective-permute-start.31 = (bf16[16,32,128]{2,1,0:T(8,128)(2,1)S(1)}, bf16[16,32,128]{2,1,0:T(8,128)(2,1)S(1)}, u32[]{:S(2)}, u32[]{:S(2)}) collective-permute-start(bf16[16,32,128]{2,1,0:T(8,128)(2,1)S(1)} %dynamic-slice_bitcast_fusion.35), channel_id=1, source_target_pairs={{0,2},{1,3},{2,0},{3,1},{4,6},{5,7},{6,4},{7,5},{8,10},{9,11},{10,... | collective-permute-start | bytes 393224 | tf_op jit(solution)/shard_map/ppermute | solution.py:705
  1043.8 35.3 %collective-permute-start.34 = (bf16[16,32,128]{2,1,0:T(8,128)(2,1)S(1)}, bf16[16,32,128]{2,1,0:T(8,128)(2,1)S(1)}, u32[]{:S(2)}, u32[]{:S(2)}) collective-permute-start(bf16[16,32,128]{2,1,0:T(8,128)(2,1)S(1)} %dynamic-slice_bitcast_fusion.34), channel_id=1, source_target_pairs={{0,4},{1,5},{2,6},{3,7},{4,0},{5,1},{6,2},{7,3},{8,12},{9,13},{10,... | collective-permute-start | bytes 393224 | tf_op jit(solution)/shard_map/ppermute | solution.py:705
  1115.3 143.1 %all-gather.14.cloned.1.call-start = ((), (), s32[]{:S(2)}) async-start(), calls=%async_computation.17 | async-start | bytes 5242880 | tf_op jit(solution)/shard_map/all_gather | solution.py:1305
  (251 other events, 2134.6 us)
Sparse Core Ops, SparseCore 0:
  20.6 109.7 all-gather.7
  196.8 89.4 all-gather.9
  726.1 53.8 all-gather.11
  1117.6 53.9 all-gather.13

commit v3 on v2

--- a/solution.py
+++ b/solution.py
@@ -505,7 +505,7 @@
 def room_for(per_device, chosen):
     share = sum(chosen(mat_no) for mat_no in range(MATS)) / MATS
     mean = per_device * share
-    return min(per_device - 1, -(-int(mean + 5.0 * math.sqrt(mean * (1 - share))) // 4) * 4)
+    return min(per_device - 1, -(-int(mean + 4.2 * math.sqrt(mean * (1 - share))) // 4) * 4)
 
 
 def by_block(slot_list, values):
@@ -910,7 +910,7 @@
     return (lists, rounds_needed(owner_all, peers, size))
 
 
-def return_rows(grad_rows, lists, first_lists, rounds, total, ready):
+def return_rows(grad_rows, lists, first_lists, rounds, total, ready, landed):
     def swap_all(rows):
         return lax.all_to_all(rows, ("dp", "vocab"), 0, 0, tiled=True)
 
@@ -918,7 +918,7 @@
         chosen, where = lists(round_no)
         return add_rows(swap_all(take_rows(grad_rows, chosen, jnp.bfloat16)), where, so_far)
 
-    arrived = swap_all(ready(take_rows(grad_rows, first_lists[0], jnp.bfloat16)))
+    arrived = landed(swap_all(ready(take_rows(grad_rows, first_lists[0], jnp.bfloat16))))
     return lax.fori_loop(1, rounds, again, add_rows(arrived, first_lists[1], total))
 
 
@@ -987,6 +987,9 @@
 def soap_update(
     master,
     grad_tiles,
+    grad_turned,
+    left_outer,
+    right_outer,
     first_mom,
     first_turned,
     second_mom,
@@ -997,7 +1000,7 @@
     factor,
 ):
     first_new = BETA_FIRST * first_mom + (1 - BETA_FIRST) * (factor * grad_tiles)
-    grad_turned = factor * turn_in(left_basis, grad_tiles, right_basis)
+    grad_turned = factor * grad_turned
     first_turned = BETA_FIRST * first_turned + (1 - BETA_FIRST) * grad_turned
     second_new = BETA_SECOND * second_mom + (1 - BETA_SECOND) * grad_turned * grad_turned
     direction = (
@@ -1008,14 +1011,8 @@
     master_new = master - RATE_MATRIX * (
         turn_out(left_basis, direction, right_basis) + DECAY * master
     )
-    left_new = BETA_STAT * left_stat + (1 - BETA_STAT) * (
-        factor
-        * (factor * jnp.einsum("tik,tjk->tij", grad_tiles, grad_tiles, precision=HIGH))
-    )
-    right_new = BETA_STAT * right_stat + (1 - BETA_STAT) * (
-        factor
-        * (factor * jnp.einsum("tki,tkj->tij", grad_tiles, grad_tiles, precision=HIGH))
-    )
+    left_new = BETA_STAT * left_stat + (1 - BETA_STAT) * (factor * (factor * left_outer))
+    right_new = BETA_STAT * right_stat + (1 - BETA_STAT) * (factor * (factor * right_outer))
     return (
         master_new,
         first_new,
@@ -1082,7 +1079,9 @@
     fact_count = own_facts.shape[0]
     own_facts = jnp.pad(own_facts, (0, -fact_count % 128))
     facts = spread(own_facts, ("dp", "vocab"), devices)
-    slots_later, facts = lax.optimization_barrier((slot_list, facts))
+    slots_later, facts, mom1_later, left_later, right_later = lax.optimization_barrier(
+        (slot_list, facts, mom1_tiles, basis_left, basis_right)
+    )
     tokens_all = facts[:, : tokens.shape[0]]
     after = facts[:, tokens.shape[0] :]
     labels_all = after[:, :row_count]
@@ -1163,7 +1162,7 @@
 
     lists, rounds = return_plan(tokens_all, rows_each, dp_size)
     source_rows = with_waves(source_finish(source_arrived), src_count)
-    first_turned = turn_in(basis_left, mom1_tiles, basis_right)
+    first_turned = turn_in(left_later, mom1_later, right_later)
     source_rows, first_lists, first_turned, target_sent = lax.optimization_barrier(
         (source_rows, lists(0), first_turned, target_sent)
     )
@@ -1222,6 +1221,13 @@
 
     matrix_store = [None] * MATS
     gain_store = [None] * GAINS
+    first_row = peer_me * rows_each + dp_me * quarter
+    table_quarter = lax.dynamic_slice_in_dim(table_low_part, dp_me * quarter, quarter, 0)
+    hit_quarter = label_rows[:, None] - first_row == jnp.arange(quarter)[None, :]
+    grads_quarter = logit_grads(
+        linear_tr(exit_all, table_quarter), spread_all.reshape(-1), weight_rows, hit_quarter
+    )
+    grad_quarter = outer_sum(grads_quarter, exit_all)
     soon_mats = [mat_no for mat_no in range(MATS) if not is_last(mat_no)]
     late_mats = [mat_no for mat_no in range(MATS) if is_last(mat_no)]
     both = [devices * soon_size, devices * late_size]
@@ -1229,7 +1235,9 @@
 
     def before_last(grad_stream):
         blocks, held["begun"] = fold_gradients(matrix_store, soon_mats, back_of, both)
-        grad_stream, blocks = lax.optimization_barrier((grad_stream, blocks))
+        grad_stream, blocks, held["quarter"] = lax.optimization_barrier(
+            (grad_stream, blocks, grad_quarter)
+        )
         held["total"] = first_exchange(blocks, devices)
         return grad_stream
 
@@ -1254,13 +1262,6 @@
         between_last,
     )
 
-    first_row = peer_me * rows_each + dp_me * quarter
-    table_quarter = lax.dynamic_slice_in_dim(table_low_part, dp_me * quarter, quarter, 0)
-    hit_quarter = label_rows[:, None] - first_row == jnp.arange(quarter)[None, :]
-    grads_quarter = logit_grads(
-        linear_tr(exit_all, table_quarter), spread_all.reshape(-1), weight_rows, hit_quarter
-    )
-    grad_quarter = outer_sum(grads_quarter, exit_all)
     grad_source = between_last(grad_source)
     grad_rows = jnp.concatenate([grad_source, grad_target], 0) * math.sqrt(D)
     grad_rows = between_last(grad_rows)
@@ -1268,36 +1269,52 @@
     late_parts = split_parts(first_exchange(late_blocks, devices), late_plan, devices)
     late_parts = one_exchange(late_parts, late_plan, 0, devices)
 
-    def ready(rows):
-        rows = between_last(rows)
-        rows, held["late"] = lax.optimization_barrier((rows, late_parts))
-        return rows
-
-    grad_quarter = return_rows(grad_rows, lists, first_lists, rounds, grad_quarter, ready)
-
-    soon_sum = other_exchanges(held["parts"], soon_plan, devices, held["done"])
-    late_sum = other_exchanges(held["late"], late_plan, devices, 1)
+    late_sum = other_exchanges(late_parts, late_plan, devices, 1)
 
     def exchange_again():
         blocks, _ = fold_gradients(matrix_store, list(range(MATS)), back_of, both)
         parts = split_parts(first_exchange(blocks, devices), soon_plan, devices)
         return other_exchanges(parts, soon_plan, devices)
 
-    soon_sum = lax.cond(
-        jnp.min(soon_count) < soon_size, exchange_again, lambda: soon_sum
-    )
-    owned_grad = unfold_ranked(
-        jnp.concatenate([soon_sum, late_sum], 0),
-        lax.dynamic_index_in_dim(back_ranks, me, 0, keepdims=False),
-    )
-    squares = jnp.sum(owned_grad * owned_grad) + jnp.sum(grad_quarter * grad_quarter)
-    square_total = jnp.sum(
-        spread(jnp.full((1, 128), squares), ("dp", "vocab"), devices)[:, 0, 0]
-    )
     share = -(-GAINS * D // (devices * 128)) * 128
     gain_flat = jnp.stack(gain_store).reshape(-1)
     gain_flat = jnp.pad(gain_flat, (0, devices * share - GAINS * D)).reshape(devices, share)
-    gain_part = jnp.sum(lax.all_to_all(gain_flat, ("dp", "vocab"), 0, 0, tiled=True), axis=0)
+
+    def ready(rows):
+        sums = other_exchanges(held["parts"], soon_plan, devices, held["done"])
+        rows, sums, late, held["gains"] = lax.optimization_barrier(
+            (rows, sums, late_sum, gain_flat)
+        )
+        sums = lax.cond(jnp.min(soon_count) < soon_size, exchange_again, lambda: sums)
+        owned_grad = unfold_ranked(
+            jnp.concatenate([sums, late], 0),
+            lax.dynamic_index_in_dim(back_ranks, me, 0, keepdims=False),
+        )
+        held["owned"] = (
+            owned_grad,
+            turn_in(basis_left, owned_grad, basis_right),
+            jnp.einsum("tik,tjk->tij", owned_grad, owned_grad, precision=HIGH),
+            jnp.einsum("tki,tkj->tij", owned_grad, owned_grad, precision=HIGH),
+            jnp.sum(owned_grad * owned_grad),
+        )
+        return rows
+
+    def landed(arrived):
+        arrived, held["owned"] = lax.optimization_barrier((arrived, held["owned"]))
+        return arrived
+
+    grad_quarter = return_rows(
+        grad_rows, lists, first_lists, rounds, held["quarter"], ready, landed
+    )
+
+    owned_grad, owned_turned, left_outer, right_outer, owned_squares = held["owned"]
+    squares = owned_squares + jnp.sum(grad_quarter * grad_quarter)
+    square_total = jnp.sum(
+        spread(jnp.full((1, 128), squares), ("dp", "vocab"), devices)[:, 0, 0]
+    )
+    gain_part = jnp.sum(
+        lax.all_to_all(held["gains"], ("dp", "vocab"), 0, 0, tiled=True), axis=0
+    )
     gain_total = spread(gain_part[None], ("dp", "vocab"), devices).reshape(-1)[: GAINS * D]
     gain_total = gain_total.reshape(GAINS, D)
     grad_norm = jnp.sqrt(square_total + jnp.sum(gain_total * gain_total))
@@ -1308,6 +1325,9 @@
     master_new, mom1_new, mom2_new, left_new, right_new, bleft_new, bright_new = soap_update(
         master_tiles,
         owned_grad,
+        owned_turned,
+        left_outer,
+        right_outer,
         mom1_tiles,
         first_turned,
         mom2_tiles,

time: 1290 us -> 1310 us (1.016)
  waiting for transfers between devices: 221 us -> 240 us
  local copies, waits for them, and re-layouts: 170 us -> 187 us
    all_to_all x1, waiting for transfers between devices: 0.01 us -> 57.7 us  [swap_all(): return lax.all_to_all(rows, ('dp', 'vocab'), 0, 0, tiled=True)]
    ppermute x26, waiting for transfers between devices: 90.5 us -> 61.7 us  [halve(): arrived = lax.ppermute(sent, ('dp', 'vocab'), pairs)]
    all_to_all x1, waiting for transfers between devices: 20.7 us -> 0.01 us  [per_device(): lax.all_to_all(held['gains'], ('dp', 'vocab'), 0, 0, tiled=True)]
    unnamed x515 -> x513, local copies, waits for them, and re-layouts: 114 us -> 107 us
  transfers between devices with their start and end apart: 40 -> 40, of which waited for: 19 -> 21; matrix products, arithmetic and copies ran while one was open for 24% -> 31% of each run, Pallas kernels for 18% -> 23%
where the time goes in v3:
time: 1310 us; the launch traced here: 1300 us
  Pallas kernels  382 us (29%)
  matrix products  257 us (20%)
  waiting for transfers between devices  240 us (18%)
  local copies, waits for them, and re-layouts  187 us (14%)
  other arithmetic  145 us (11%)
  starting transfers between devices  62.9 us (5%)
  between operations  25.1 us (2%)
    pallas_call x6, Pallas kernels, attend_backward(): pl.pallas_call(kernel, out_shape=(jax.ShapeDtypeStruct((MICRO * rows, D),...  123 us
    unnamed x513, local copies, waits for them, and re-layouts  107 us
    pallas_call x5, Pallas kernels, attend_forward(): pl.pallas_call(kernel, out_shape=(jax.ShapeDtypeStruct((MICRO * rows, D),...  84.4 us
    dot_general x19, matrix products, linear(): return jnp.dot(left_op, right_op, preferred_element_type=jnp.float32)  77.4 us
    dot_general x23, matrix products, outer_sum(): lax.dot_general(left_op, right_op, (((0,), (0,)), ((), ())), preferred_el...  67.1 us
    all_to_all x2, waiting for transfers between devices, swap_rows(): return lax.all_to_all(rows, 'vocab', 0, 0, tiled=True)  65 us
    ppermute x26, waiting for transfers between devices, halve(): arrived = lax.ppermute(sent, ('dp', 'vocab'), pairs)  61.7 us
    dot_general x19, matrix products, linear_tr(): lax.dot_general(left_op, right_op, (((1,), (1,)), ((), ())), preferred_el...  60.9 us
  transfers between devices with their start and end apart: 40, of which 21 were waited for; matrix products, arithmetic and copies ran while one was open for 31% of the time, Pallas kernels for 23%

profile of v3, /device:TPU:0, one launch (start us, length us, event | category | flops | bytes accessed | tf_op | source)
XLA Modules:
  0.0 1299.7 jit_solution(2633024168912262670)
XLA Ops:
  52.0 20.8 %all-to-all-done.3 = s32[32,1,2688]{2,1,0:T(1,128)S(1)} async-done(((s32[32,1,2688]{2,1,0:T(1,128)}), s32[32,1,2688]{2,1,0:T(1,128)S(1)}, u32[]{:S(2)}, u32[]{:S(2)}) %all-to-all-start.3) | async-done | bytes 344096 | tf_op jit(solution)/shard_map/all_to_all | solution.py:803
  75.7 16.6 %shard_map.332 = bf16[2688,512]{1,0:T(8,128)(2,1)} custom-call(s32[2688]{0:T(1024)S(1)} %max.32.index_ref, f32[4096,512]{1,0:T(8,128)} %source_ref.3), custom_call_target="tpu_custom_call" | custom-call | tf_op jit(solution)/shard_map/pallas_call | solution.py:754
  118.5 55.8 %all-to-all-done.4 = bf16[8,336,512]{2,1,0:T(8,128)(2,1)S(1)} async-done(((bf16[8,336,512]{2,1,0:T(8,128)(2,1)}), bf16[8,336,512]{2,1,0:T(8,128)(2,1)S(1)}, u32[]{:S(2)}, u32[]{:S(2)}) %all-to-all-start.4) | async-done | bytes 2752544 | tf_op jit(solution)/shard_map/all_to_all | solution.py:883
  175.9 14.8 %conditional.2 = (bf16[512,2048]{1,0:T(8,128)(2,1)}, bf16[512,2048]{1,0:T(8,128)(2,1)}, bf16[512,2048]{1,0:T(8,128)(2,1)S(1)}, bf16[512,2048]{1,0:T(8,128)(2,1)}, bf16[512,2048]{1,0:T(8,128)(2,1)}) conditional(s32[]{:T(128)} %convert_element_type.1086, (s32[2816]{0:T(1024)S(1)}, bf16[1408,32,128]{2,1,0:T(8,128)(2,1)}) %tuple.99, ...), branch_computations={%region_26.27_spmd, %region_27.28_spmd} | conditional | bytes 90210416 | solution.py:1144
  175.9 10.0 branch_0_fun.1
  205.2 8.6 shard_map.334
  222.4 10.7 shard_map.333
  244.0 46.6 %shard_map.335 = (bf16[2048,512]{1,0:T(8,128)(2,1)S(1)}, f32[2048,512]{1,0:T(8,128)S(1)}) custom-call(s32[2]{0:T(128)S(1)} %bitcast.504, bf16[2048,1536]{1,0:T(8,128)(2,1)S(1)} %convolution_convert_fusion.query_ref.key_ref.value_ref, bf16[2048,1536]{1,0:T(8,128)(2,1)S(1)} %convolution_convert_fusion.query_ref.key_ref.value_ref, ...), custom_call_target="tpu_custom_call" | custom-call | flops 4294967296 | bytes 16777216 | tf_op jit(solution)/shard_map/pallas_call | solution.py:112
  293.6 11.3 fusion.562
  308.5 10.7 multiply_reduce_fusion.6
  323.0 9.2 all-to-all-done.5
  332.4 20.1 %shard_map.337 = (bf16[512,2048]{1,0:T(8,128)(2,1)S(1)}, bf16[512,2048]{1,0:T(8,128)(2,1)S(1)}, bf16[512,2048]{1,0:T(8,128)(2,1)S(1)}, bf16[512,2048]{1,0:T(8,12...) custom-call(s32[2816]{0:T(1024)S(1)} %reshape.1992.place_ref, ...), custom_call_target="tpu_custom_call" | custom-call | tf_op jit(solution)/shard_map/pallas_call | solution.py:573
  379.1 12.9 shard_map.339
  410.2 13.1 %shard_map.341 = (bf16[512,512]{1,0:T(8,128)(2,1)S(1)}, f32[512,512]{1,0:T(8,128)S(1)}) custom-call(s32[2]{0:T(128)S(1)} %bitcast.506, bf16[512,512]{1,0:T(8,128)(2,1)S(1)} %convolution_convert_fusion.28.query_ref, bf16[2048,1024]{1,0:T(8,128)(2,1)S(1)} %convolution_convert_fusion.1.key_ref.value_ref, ...), custom_call_target="tpu_custom_call" | custom-call | flops 1073741824 | bytes 10485760 | tf_op jit(solution)/shard_map/pallas_call | solution.py:112
  482.0 8.0 fusion.250
  499.7 9.9 all-to-all-done.8
  525.5 19.8 %shard_map.342 = (bf16[512,512]{1,0:T(8,128)(2,1)S(1)}, bf16[2048,512]{1,0:T(8,128)(2,1)S(1)}, bf16[2048,512]{1,0:T(8,128)(2,1)S(1)}) custom-call(s32[2]{0:T(128)S(1)} %bitcast.507, bf16[512,512]{1,0:T(8,128)(2,1)S(1)} %convolution_convert_fusion.28.query_ref, bf16[2048,1024]{1,0:T(8,128)(2,1)S(1)} %copy-done.7, bf16[2048,1024]{1,0:T(8,128)(2,1)S(1)} %copy-done.7, ...), custom_call_target="tpu_custom_call" | custom-call | flops 2684354560 | bytes 20971520 | tf_op jit(solution)/shard_map/pallas_call | solution.py:188
  572.1 19.8 %shard_map.344 = (bf16[512,512]{1,0:T(8,128)(2,1)S(1)}, bf16[2048,512]{1,0:T(8,128)(2,1)S(1)}, bf16[2048,512]{1,0:T(8,128)(2,1)S(1)}) custom-call(s32[2]{0:T(128)S(1)} %bitcast.508, bf16[512,512]{1,0:T(8,128)(2,1)S(1)} %convolution_convert_fusion.29.query_ref, bf16[2048,1024]{1,0:T(8,128)(2,1)S(1)} %copy-done.5, bf16[2048,1024]{1,0:T(8,128)(2,1)S(1)} %copy-done.5, ...), custom_call_target="tpu_custom_call" | custom-call | flops 2684354560 | bytes 20971520 | tf_op jit(solution)/shard_map/pallas_call | solution.py:188
  625.3 17.6 %fusion.161 = bf16[2048,2048]{1,0:T(8,128)(2,1)} fusion(f32[2048,2048]{1,0:T(8,128)} %fusion.562, bf16[512,2048]{1,0:T(8,128)(2,1)} %get-tuple-element.836, f32[2048,512]{1,0:T(8,128)S(1)} %add_add_fusion.2), kind=kOutput, calls=%fused_computation.250 | convolution fusion | flops 4379901952 | bytes 31457280 | tf_op jit(solution)/shard_map/dot_general | solution.py:52
  642.8 11.4 convolution_convert_fusion.11.refs_7_
  679.5 10.1 convolution_convert_fusion.14.refs_4_
  689.7 20.1 %shard_map.346 = (bf16[2176,32,128]{2,1,0:T(8,128)(2,1)}, bf16[640,32,128]{2,1,0:T(8,128)(2,1)S(1)}) custom-call(s32[2816]{0:T(1024)S(1)} %copy-done.163, bf16[512,2048]{1,0:T(8,128)(2,1)S(1)} %pad_maximum_fusion.3.refs_0_, bf16[512,2048]{1,0:T(8,128)(2,1)S(1)} %pad_maximum_fusion.4.refs_1_, bf16[512,2048]{1,0:T(8,128)(2,1)S(1)} %pad_maximum_fusion.5.refs_2_, ...), custom_call_target="tpu_custom_call" | custom-call | tf_op jit(solution)/shard_map/pallas_call | solution.py:654
  709.8 10.0 multiply_reduce_fusion.1
  748.9 34.8 %shard_map.347 = (bf16[2048,512]{1,0:T(8,128)(2,1)S(1)}, bf16[2048,512]{1,0:T(8,128)(2,1)S(1)}, bf16[2048,512]{1,0:T(8,128)(2,1)S(1)}) custom-call(s32[2]{0:T(128)S(1)} %bitcast.509, bf16[2048,1536]{1,0:T(8,128)(2,1)} %copy-done.1, bf16[2048,1536]{1,0:T(8,128)(2,1)} %copy-done.1, bf16[2048,1536]{1,0:T(8,128)(2,1)} %copy-done.1, f32[2048,512]{1,0:T(8,128)S(1)} %copy-done.14, ...), custom_call_target="tpu_custom_call" | custom-call | flops 5368709120 | bytes 16777216 | tf_op jit(solution)/shard_map/pallas_call | solution.py:188
  810.3 34.4 %shard_map.348 = (bf16[2048,512]{1,0:T(8,128)(2,1)S(1)}, bf16[2048,512]{1,0:T(8,128)(2,1)S(1)}, bf16[2048,512]{1,0:T(8,128)(2,1)S(1)}) custom-call(s32[2]{0:T(128)S(1)} %bitcast.510, bf16[2048,1536]{1,0:T(8,128)(2,1)} %copy-done.1, bf16[2048,1536]{1,0:T(8,128)(2,1)} %copy-done.1, ...), custom_call_target="tpu_custom_call", output_to_operand_aliasing={{0}: (6, {}), {1}: (7, {}), {2}: (8, {})} | custom-call | flops 5368709120 | bytes 16777216 | tf_op jit(solution)/shard_map/pallas_call | solution.py:188
  881.7 16.9 %collective-permute-done.18 = bf16[88,32,128]{2,1,0:T(8,128)(2,1)S(1)} collective-permute-done((bf16[88,32,128]{2,1,0:T(8,128)(2,1)}, bf16[88,32,128]{2,1,0:T(8,128)(2,1)S(1)}, u32[]{:S(2)}, u32[]{:S(2)}) %collective-permute-start.18) | collective-permute-done | bytes 720928 | tf_op jit(solution)/shard_map/ppermute | solution.py:705
  911.3 13.1 %collective-permute-done.21 = bf16[44,32,128]{2,1,0:T(8,128)(2,1)S(1)} collective-permute-done((bf16[44,32,128]{2,1,0:T(8,128)(2,1)S(1)}, bf16[44,32,128]{2,1,0:T(8,128)(2,1)S(1)}, u32[]{:S(2)}, u32[]{:S(2)}) %collective-permute-start.21) | collective-permute-done | bytes 360480 | tf_op jit(solution)/shard_map/ppermute | solution.py:705
  928.0 17.6 %shard_map.349 = bf16[4096,512]{1,0:T(8,128)(2,1)S(1)} custom-call(s32[4096]{0:T(1024)S(1)} %max.34.index_ref, f32[2560,512]{1,0:T(8,128)S(1)} %maximum_multiply_fusion.source_ref), custom_call_target="tpu_custom_call" | custom-call | tf_op jit(solution)/shard_map/pallas_call | solution.py:754
  1030.6 57.7 %all-to-all-done.9 = bf16[32,128,512]{2,1,0:T(8,128)(2,1)} async-done(((bf16[32,128,512]{2,1,0:T(8,128)(2,1)}), bf16[32,128,512]{2,1,0:T(8,128)(2,1)}, u32[]{:S(2)}, u32[]{:S(2)}) %all-to-all-start.9) | async-done | bytes 4194336 | tf_op jit(solution)/shard_map/all_to_all | solution.py:915
  1088.3 9.4 shard_map.352
  1221.3 40.7 %shard_map.353 = f32[64,64,256]{2,1,0:T(8,128)S(1)} custom-call(f32[64,64,256]{2,1,0:T(8,128)S(1)} %pad.19.in_ref), custom_call_target="tpu_custom_call" | custom-call | tf_op jit(solution)/shard_map/pallas_call | solution.py:962
  1268.9 22.8 %fusion.565 = (bf16[4096,512]{1,0:T(8,128)(2,1)}, f32[4096,512]{1,0:T(8,128)}, f32[4096,512]{1,0:T(8,128)}, f32[4096,512]{1,0:T(8,128)}) fusion(f32[4096,512]{1,0:T(8,128)} %get-tuple-element.1679, f32[]{:T(128)S(6)} %min.3, bf16[4096,512]{1,0:T(8,128)(2,1)} %all-gather.14.cloned.1.call-done, f32[4096,512]{1,0:T(8,128)} %param.38, f32[4096,512]{1,0:T(8,128)} %param.39), kind=kLoop, calls=%fused_computation.1116 | loop fusion | flops 37748736 | bytes 58720260 | tf_op jit(solution)/shard_map/convert_element_type | solution.py:1359
  (994 shorter events, 654.1 us)
Async XLA Ops:
  7.2 167.1 %all-gather.8.cloned.1.call-start = ((), (), s32[]{:S(2)}) async-start(), calls=%async_computation.14 | async-start | bytes 11894784 | tf_op jit(solution)/shard_map/all_gather | solution.py:1129
  44.0 28.8 %all-to-all-start.3 = ((s32[32,1,2688]{2,1,0:T(1,128)}), s32[32,1,2688]{2,1,0:T(1,128)S(1)}, u32[]{:S(2)}, u32[]{:S(2)}) async-start(s32[32,1,2688]{2,1,0:T(1,128)} %broadcast_in_dim.472), calls=%async_computation.3 | async-start | bytes 688128 | tf_op jit(solution)/shard_map/all_to_all | solution.py:803
  94.7 79.7 %all-to-all-start.4 = ((bf16[8,336,512]{2,1,0:T(8,128)(2,1)}), bf16[8,336,512]{2,1,0:T(8,128)(2,1)S(1)}, u32[]{:S(2)}, u32[]{:S(2)}) async-start(bf16[8,336,512]{2,1,0:T(8,128)(2,1)} %bitcast.58), calls=%async_computation.4 | async-start | bytes 5505024 | tf_op jit(solution)/shard_map/all_to_all | solution.py:883
  190.6 141.6 %all-gather.10.cloned.1.call-start = ((), (), s32[]{:S(2)}) async-start(), calls=%async_computation.15 | async-start | bytes 11894784 | tf_op jit(solution)/shard_map/all_gather | solution.py:1133
  304.9 27.3 %all-to-all-start.5 = ((bf16[8,112,512]{2,1,0:T(8,128)(2,1)}), bf16[8,112,512]{2,1,0:T(8,128)(2,1)S(1)}, u32[]{:S(2)}, u32[]{:S(2)}) async-start(bf16[8,112,512]{2,1,0:T(8,128)(2,1)} %bitcast.67), calls=%async_computation.5 | async-start | bytes 1835008 | tf_op jit(solution)/shard_map/all_to_all | solution.py:883
  437.9 19.5 %all-to-all-start.6 = ((bf16[8,64,512]{2,1,0:T(8,128)(2,1)}), bf16[8,64,512]{2,1,0:T(8,128)(2,1)}, u32[]{:S(2)}, u32[]{:S(2)}) async-start(bf16[8,64,512]{2,1,0:T(8,128)(2,1)} %broadcast_in_dim.492), calls=%async_computation.6 | async-start | bytes 1048576 | tf_op jit(solution)/shard_map/all_to_all | solution.py:803
  466.4 13.9 %all-to-all-start.7 = ((f32[32,3,512]{2,1,0:T(4,128)}), f32[32,3,512]{2,1,0:T(4,128)}, u32[]{:S(2)}, u32[]{:S(2)}) async-start(f32[32,3,512]{2,1,0:T(4,128)} %broadcast_in_dim.494), calls=%async_computation.7 | async-start | bytes 524288 | tf_op jit(solution)/shard_map/all_to_all | solution.py:803
  490.0 19.7 %all-to-all-start.8 = ((bf16[8,64,512]{2,1,0:T(8,128)(2,1)}), bf16[8,64,512]{2,1,0:T(8,128)(2,1)}, u32[]{:S(2)}, u32[]{:S(2)}) async-start(bf16[8,64,512]{2,1,0:T(8,128)(2,1)} %bitcast.604), calls=%async_computation.8 | async-start | bytes 1048576 | tf_op jit(solution)/shard_map/all_to_all | solution.py:1217
  494.3 228.3 %all-gather.12.cloned.1.call-start = ((), (), s32[]{:S(2)}) async-start(), calls=%async_computation.16 | async-start | bytes 2162688 | tf_op jit(solution)/shard_map/all_gather | solution.py:1184
  738.2 45.5 %collective-permute-start.13 = (bf16[1088,32,128]{2,1,0:T(8,128)(2,1)}, bf16[1088,32,128]{2,1,0:T(8,128)(2,1)}, u32[]{:S(2)}, u32[]{:S(2)}) collective-permute-start(bf16[1088,32,128]{2,1,0:T(8,128)(2,1)} %dynamic-slice_bitcast_fusion.13), channel_id=1, source_target_pairs={{0,1},{1,0},{2,3},{3,2},{4,5},{5,4},{6,7},{7,6},{8,9},{9,8},{10,11... | collective-permute-start | bytes 26738696 | tf_op jit(solution)/shard_map/ppermute | solution.py:705
  805.8 39.6 %collective-permute-start.15 = (bf16[176,32,128]{2,1,0:T(8,128)(2,1)}, bf16[176,32,128]{2,1,0:T(8,128)(2,1)S(1)}, u32[]{:S(2)}, u32[]{:S(2)}) collective-permute-start(bf16[176,32,128]{2,1,0:T(8,128)(2,1)} %dynamic-slice_bitcast_fusion.17), channel_id=1, source_target_pairs={{0,16},{1,17},{2,18},{3,19},{4,20},{5,21},{6,22},{7,23},{8,24},{9,... | collective-permute-start | bytes 4325384 | tf_op jit(solution)/shard_map/ppermute | solution.py:705
  808.0 42.1 %collective-permute-start.14 = (bf16[192,32,128]{2,1,0:T(8,128)(2,1)S(1)}, bf16[192,32,128]{2,1,0:T(8,128)(2,1)}, u32[]{:S(2)}, u32[]{:S(2)}) collective-permute-start(bf16[192,32,128]{2,1,0:T(8,128)(2,1)S(1)} %dynamic-slice_bitcast_fusion.15), channel_id=1, source_target_pairs={{0,8},{1,9},{2,10},{3,11},{4,12},{5,13},{6,14},{7,15},{8,0},{9,1},... | collective-permute-start | bytes 4718600 | tf_op jit(solution)/shard_map/ppermute | solution.py:705
  810.3 36.6 %collective-permute-start.16 = (bf16[176,32,128]{2,1,0:T(8,128)(2,1)}, bf16[176,32,128]{2,1,0:T(8,128)(2,1)}, u32[]{:S(2)}, u32[]{:S(2)}) collective-permute-start(bf16[176,32,128]{2,1,0:T(8,128)(2,1)} %dynamic-slice_bitcast_fusion.16), channel_id=1, source_target_pairs={{0,2},{1,3},{2,0},{3,1},{4,6},{5,7},{6,4},{7,5},{8,10},{9,11},{10,... | collective-permute-start | bytes 4325384 | tf_op jit(solution)/shard_map/ppermute | solution.py:705
  865.2 40.4 %collective-permute-start.17 = (bf16[96,32,128]{2,1,0:T(8,128)(2,1)}, bf16[96,32,128]{2,1,0:T(8,128)(2,1)}, u32[]{:S(2)}, u32[]{:S(2)}) collective-permute-start(bf16[96,32,128]{2,1,0:T(8,128)(2,1)} %dynamic-slice_bitcast_fusion.18), channel_id=1, source_target_pairs={{0,16},{1,17},{2,18},{3,19},{4,20},{5,21},{6,22},{7,23},{8,24},{9,... | collective-permute-start | bytes 2359304 | tf_op jit(solution)/shard_map/ppermute | solution.py:705
  867.3 31.3 %collective-permute-start.18 = (bf16[88,32,128]{2,1,0:T(8,128)(2,1)}, bf16[88,32,128]{2,1,0:T(8,128)(2,1)S(1)}, u32[]{:S(2)}, u32[]{:S(2)}) collective-permute-start(bf16[88,32,128]{2,1,0:T(8,128)(2,1)} %dynamic-slice_bitcast_fusion.20), channel_id=1, source_target_pairs={{0,2},{1,3},{2,0},{3,1},{4,6},{5,7},{6,4},{7,5},{8,10},{9,11},{10,... | collective-permute-start | bytes 2162696 | tf_op jit(solution)/shard_map/ppermute | solution.py:705
  870.3 33.8 %collective-permute-start.19 = (bf16[88,32,128]{2,1,0:T(8,128)(2,1)}, bf16[88,32,128]{2,1,0:T(8,128)(2,1)}, u32[]{:S(2)}, u32[]{:S(2)}) collective-permute-start(bf16[88,32,128]{2,1,0:T(8,128)(2,1)} %dynamic-slice_bitcast_fusion.19), channel_id=1, source_target_pairs={{0,4},{1,5},{2,6},{3,7},{4,0},{5,1},{6,2},{7,3},{8,12},{9,13},{10,... | collective-permute-start | bytes 2162696 | tf_op jit(solution)/shard_map/ppermute | solution.py:705
  875.4 70.4 %collective-permute-start.26 = (bf16[320,32,128]{2,1,0:T(8,128)(2,1)}, bf16[320,32,128]{2,1,0:T(8,128)(2,1)}, u32[]{:S(2)}, u32[]{:S(2)}) collective-permute-start(bf16[320,32,128]{2,1,0:T(8,128)(2,1)} %dynamic-slice_bitcast_fusion.14), channel_id=1, source_target_pairs={{0,1},{1,0},{2,3},{3,2},{4,5},{5,4},{6,7},{7,6},{8,9},{9,8},{10,11... | collective-permute-start | bytes 7864328 | tf_op jit(solution)/shard_map/ppermute | solution.py:705
  907.1 17.6 %collective-permute-start.20 = (bf16[48,32,128]{2,1,0:T(8,128)(2,1)S(1)}, bf16[48,32,128]{2,1,0:T(8,128)(2,1)S(1)}, u32[]{:S(2)}, u32[]{:S(2)}) collective-permute-start(bf16[48,32,128]{2,1,0:T(8,128)(2,1)S(1)} %dynamic-slice_bitcast_fusion.24), channel_id=1, source_target_pairs={{0,2},{1,3},{2,0},{3,1},{4,6},{5,7},{6,4},{7,5},{8,10},{9,11},{10,... | collective-permute-start | bytes 1179656 | tf_op jit(solution)/shard_map/ppermute | solution.py:705
  907.2 17.3 %collective-permute-start.21 = (bf16[44,32,128]{2,1,0:T(8,128)(2,1)S(1)}, bf16[44,32,128]{2,1,0:T(8,128)(2,1)S(1)}, u32[]{:S(2)}, u32[]{:S(2)}) collective-permute-start(bf16[44,32,128]{2,1,0:T(8,128)(2,1)S(1)} %dynamic-slice_bitcast_fusion.26), channel_id=1, source_target_pairs={{0,4},{1,5},{2,6},{3,7},{4,0},{5,1},{6,2},{7,3},{8,12},{9,13},{10,... | collective-permute-start | bytes 1081352 | tf_op jit(solution)/shard_map/ppermute | solution.py:705
  909.3 15.3 %collective-permute-start.22 = (bf16[44,32,128]{2,1,0:T(8,128)(2,1)S(1)}, bf16[44,32,128]{2,1,0:T(8,128)(2,1)S(1)}, u32[]{:S(2)}, u32[]{:S(2)}) collective-permute-start(bf16[44,32,128]{2,1,0:T(8,128)(2,1)S(1)} %dynamic-slice_bitcast_fusion.25), channel_id=1, source_target_pairs={{0,8},{1,9},{2,10},{3,11},{4,12},{5,13},{6,14},{7,15},{8,0},{9,1},... | collective-permute-start | bytes 1081352 | tf_op jit(solution)/shard_map/ppermute | solution.py:705
  924.8 20.8 %collective-permute-start.25 = (bf16[22,32,128]{2,1,0:T(8,128)(2,1)S(1)}, bf16[22,32,128]{2,1,0:T(8,128)(2,1)S(1)}, u32[]{:S(2)}, u32[]{:S(2)}) collective-permute-start(bf16[22,32,128]{2,1,0:T(8,128)(2,1)S(1)} %dynamic-slice_bitcast_fusion.31), channel_id=1, source_target_pairs={{0,16},{1,17},{2,18},{3,19},{4,20},{5,21},{6,22},{7,23},{8,24},{9,... | collective-permute-start | bytes 540680 | tf_op jit(solution)/shard_map/ppermute | solution.py:705
  925.8 19.9 %collective-permute-start.24 = (bf16[22,32,128]{2,1,0:T(8,128)(2,1)S(1)}, bf16[22,32,128]{2,1,0:T(8,128)(2,1)S(1)}, u32[]{:S(2)}, u32[]{:S(2)}) collective-permute-start(bf16[22,32,128]{2,1,0:T(8,128)(2,1)S(1)} %dynamic-slice_bitcast_fusion.32), channel_id=1, source_target_pairs={{0,8},{1,9},{2,10},{3,11},{4,12},{5,13},{6,14},{7,15},{8,0},{9,1},... | collective-permute-start | bytes 540680 | tf_op jit(solution)/shard_map/ppermute | solution.py:705
  927.1 22.9 %collective-permute-start.23 = (bf16[24,32,128]{2,1,0:T(8,128)(2,1)S(1)}, bf16[24,32,128]{2,1,0:T(8,128)(2,1)S(1)}, u32[]{:S(2)}, u32[]{:S(2)}) collective-permute-start(bf16[24,32,128]{2,1,0:T(8,128)(2,1)S(1)} %dynamic-slice_bitcast_fusion.30), channel_id=1, source_target_pairs={{0,4},{1,5},{2,6},{3,7},{4,0},{5,1},{6,2},{7,3},{8,12},{9,13},{10,... | collective-permute-start | bytes 589832 | tf_op jit(solution)/shard_map/ppermute | solution.py:705
  951.3 10.8 collective-permute-start.31
  952.9 10.3 collective-permute-start.27
  959.7 10.2 collective-permute-start.36
  963.4 14.9 %collective-permute-start.28 = (bf16[32,32,128]{2,1,0:T(8,128)(2,1)S(1)}, bf16[32,32,128]{2,1,0:T(8,128)(2,1)S(1)}, u32[]{:S(2)}, u32[]{:S(2)}) collective-permute-start(bf16[32,32,128]{2,1,0:T(8,128)(2,1)S(1)} %dynamic-slice_bitcast_fusion.27), channel_id=1, source_target_pairs={{0,16},{1,17},{2,18},{3,19},{4,20},{5,21},{6,22},{7,23},{8,24},{9,... | collective-permute-start | bytes 786440 | tf_op jit(solution)/shard_map/ppermute | solution.py:705
  989.7 98.7 %all-to-all-start.9 = ((bf16[32,128,512]{2,1,0:T(8,128)(2,1)}), bf16[32,128,512]{2,1,0:T(8,128)(2,1)}, u32[]{:S(2)}, u32[]{:S(2)}) async-start(bf16[32,128,512]{2,1,0:T(8,128)(2,1)} %bitcast.500), calls=%async_computation.9 | async-start | bytes 8388608 | tf_op jit(solution)/shard_map/all_to_all | solution.py:915
  993.2 275.7 %all-gather.14.cloned.1.call-start = ((), (), s32[]{:S(2)}) async-start(), calls=%async_computation.17 | async-start | bytes 5242880 | tf_op jit(solution)/shard_map/all_gather | solution.py:1322
  1103.0 18.8 %all-to-all-start.11 = ((f32[32,1,256]{2,1,0:T(1,128)}), f32[32,1,256]{2,1,0:T(1,128)S(1)}, u32[]{:S(2)}, u32[]{:S(2)}) async-start(f32[32,1,256]{2,1,0:T(1,128)} %all_to_all.99), calls=%async_computation.11 | async-start | bytes 65536 | tf_op jit(solution)/shard_map/all_to_all | solution.py:1316
  1122.6 13.1 %all-to-all-start.12 = ((f32[32,1,256]{2,1,0:T(1,128)}), f32[32,1,256]{2,1,0:T(1,128)S(1)}, u32[]{:S(2)}, u32[]{:S(2)}) async-start(f32[32,1,256]{2,1,0:T(1,128)} %broadcast_in_dim.510), calls=%async_computation.12 | async-start | bytes 65536 | tf_op jit(solution)/shard_map/all_to_all | solution.py:803
  1136.3 10.1 all-to-all-start.10
  (250 other events, 1922.6 us)
Sparse Core Ops, SparseCore 0:
  20.6 109.7 all-gather.7
  194.9 90.2 all-gather.9
  499.3 56.1 all-gather.11
  1102.5 50.7 all-gather.13

commit v4 on v3

--- a/solution.py
+++ b/solution.py
@@ -938,25 +938,34 @@
     def kernel(in_ref, out_ref):
         out_ref[...] = in_ref[...]
 
-        def one_column(column_no, carry):
-            pivot = out_ref[column_no]
-            pivot = pivot / jnp.sqrt(jnp.sum(pivot * pivot, axis=0, keepdims=True))
-            out_ref[column_no] = pivot
+        def four_columns(group_at, carry):
+            first = group_at * group
+            pivots = []
+            for item in range(group):
+                pivot = out_ref[first + item]
+                for before in pivots:
+                    pivot = pivot - jnp.sum(before * pivot, axis=0, keepdims=True) * before
+                pivot = pivot / jnp.sqrt(jnp.sum(pivot * pivot, axis=0, keepdims=True))
+                out_ref[first + item] = pivot
+                pivots.append(pivot)
 
             def one_group(group_no, inner):
-                first = group_no * group
-                held = [out_ref[first + item] for item in range(group)]
+                held = [out_ref[group_no * group + item] for item in range(group)]
                 for item in range(group):
-                    share = jnp.sum(pivot * held[item], axis=0, keepdims=True)
-                    share = jnp.where(first + item > column_no, share, 0.0)
-                    held[item] = held[item] - share * pivot
+                    value = held[item]
+                    shares = [
+                        jnp.sum(pivot * value, axis=0, keepdims=True) for pivot in pivots
+                    ]
+                    for pivot, share in zip(pivots, shares):
+                        value = value - share * pivot
+                    held[item] = value
                 for item in range(group):
-                    out_ref[first + item] = held[item]
+                    out_ref[group_no * group + item] = held[item]
                 return inner
 
-            return lax.fori_loop((column_no + 1) // group, PB // group, one_group, carry)
-
-        lax.fori_loop(0, PB, one_column, 0)
+            return lax.fori_loop(group_at + 1, PB // group, one_group, carry)
+
+        lax.fori_loop(0, PB // group, four_columns, 0)
 
     spec = pl.BlockSpec((PB, PB, lanes), lambda step: (0, 0, step))
     return pl.pallas_call(
@@ -969,19 +978,17 @@
     )(columns)
 
 
-def renew_bases(left_stat, right_stat, left_basis, right_basis):
-    moved = jnp.concatenate(
-        [
-            jnp.einsum("tij,tjk->tik", left_stat, left_basis, precision=HIGH),
-            jnp.einsum("tij,tjk->tik", right_stat, right_basis, precision=HIGH),
-        ],
-        0,
-    )
+def renew_bases(left_moved, right_moved):
+    moved = jnp.concatenate([left_moved, right_moved], 0)
     count = moved.shape[0]
     whole = -(-count // 128) * 128
     columns = jnp.pad(jnp.transpose(moved, (2, 1, 0)), ((0, 0), (0, 0), (0, whole - count)))
     renewed = jnp.transpose(orthonormal(columns)[:, :, :count], (2, 1, 0))
     return (renewed[: count // 2], renewed[count // 2 :])
+
+
+def turned_by(stat, basis):
+    return jnp.einsum("tij,tjk->tik", stat, basis, precision=HIGH)
 
 
 def soap_update(
@@ -990,6 +997,8 @@
     grad_turned,
     left_outer,
     right_outer,
+    left_moves,
+    right_moves,
     first_mom,
     first_turned,
     second_mom,
@@ -1019,7 +1028,12 @@
         second_new,
         left_new,
         right_new,
-        *renew_bases(left_new, right_new, left_basis, right_basis),
+        *renew_bases(
+            *(
+                BETA_STAT * before + (1 - BETA_STAT) * (factor * (factor * change))
+                for before, change in (left_moves, right_moves)
+            )
+        ),
     )
 
 
@@ -1127,8 +1141,25 @@
     source_sent, source_finish = planned(0, src_count)
     target_sent, target_finish = planned(MICRO * src_count, tgt_count)
     first_tiles = lax.all_gather(own_folded[:first_size], ("dp", "vocab"), axis=0, tiled=True)
-    own_second, first_tiles, source_arrived = lax.optimization_barrier(
-        (own_folded[first_size:], first_tiles, swap_rows(source_sent))
+    lists, rounds = return_plan(tokens_all, rows_each, dp_size)
+    (
+        own_second,
+        first_tiles,
+        source_arrived,
+        first_lists,
+        first_turned,
+        target_sent,
+        place_of,
+    ) = lax.optimization_barrier(
+        (
+            own_folded[first_size:],
+            first_tiles,
+            swap_rows(source_sent),
+            lists(0),
+            turn_in(left_later, mom1_later, right_later),
+            target_sent,
+            place_of,
+        )
     )
     second_tiles = lax.all_gather(own_second, ("dp", "vocab"), axis=0, tiled=True)
     encoder_mats = [mat_no for mat_no in range(MATS) if is_encoder(mat_no)]
@@ -1160,12 +1191,8 @@
     def with_waves(rows, length):
         return rows * math.sqrt(D) + jnp.tile(wave_set[:length], (MICRO, 1))
 
-    lists, rounds = return_plan(tokens_all, rows_each, dp_size)
     source_rows = with_waves(source_finish(source_arrived), src_count)
-    first_turned = turn_in(left_later, mom1_later, right_later)
-    source_rows, first_lists, first_turned, target_sent = lax.optimization_barrier(
-        (source_rows, lists(0), first_turned, target_sent)
-    )
+    source_rows, target_sent = lax.optimization_barrier((source_rows, target_sent))
     target_arrived = swap_rows(target_sent)
 
     place_rows = (places + jnp.arange(MICRO)[:, None] * tgt_count).reshape(-1)
@@ -1290,12 +1317,21 @@
             jnp.concatenate([sums, late], 0),
             lax.dynamic_index_in_dim(back_ranks, me, 0, keepdims=False),
         )
+        left_outer = jnp.einsum("tik,tjk->tij", owned_grad, owned_grad, precision=HIGH)
+        right_outer = jnp.einsum("tki,tkj->tij", owned_grad, owned_grad, precision=HIGH)
+        gain_part = jnp.sum(
+            lax.all_to_all(held["gains"], ("dp", "vocab"), 0, 0, tiled=True), axis=0
+        )
+        gain_total = spread(gain_part[None], ("dp", "vocab"), devices)
         held["owned"] = (
             owned_grad,
             turn_in(basis_left, owned_grad, basis_right),
-            jnp.einsum("tik,tjk->tij", owned_grad, owned_grad, precision=HIGH),
-            jnp.einsum("tki,tkj->tij", owned_grad, owned_grad, precision=HIGH),
+            left_outer,
+            right_outer,
+            (turned_by(stat_left, basis_left), turned_by(left_outer, basis_left)),
+            (turned_by(stat_right, basis_right), turned_by(right_outer, basis_right)),
             jnp.sum(owned_grad * owned_grad),
+            gain_total.reshape(-1)[: GAINS * D].reshape(GAINS, D),
         )
         return rows
 
@@ -1307,16 +1343,20 @@
         grad_rows, lists, first_lists, rounds, held["quarter"], ready, landed
     )
 
-    owned_grad, owned_turned, left_outer, right_outer, owned_squares = held["owned"]
+    (
+        owned_grad,
+        owned_turned,
+        left_outer,
+        right_outer,
+        left_moves,
+        right_moves,
+        owned_squares,
+        gain_total,
+    ) = held["owned"]
     squares = owned_squares + jnp.sum(grad_quarter * grad_quarter)
     square_total = jnp.sum(
         spread(jnp.full((1, 128), squares), ("dp", "vocab"), devices)[:, 0, 0]
     )
-    gain_part = jnp.sum(
-        lax.all_to_all(held["gains"], ("dp", "vocab"), 0, 0, tiled=True), axis=0
-    )
-    gain_total = spread(gain_part[None], ("dp", "vocab"), devices).reshape(-1)[: GAINS * D]
-    gain_total = gain_total.reshape(GAINS, D)
     grad_norm = jnp.sqrt(square_total + jnp.sum(gain_total * gain_total))
     factor = jnp.minimum(1.0, CLIP_AT / grad_norm)
     table_grad = lax.all_gather(
@@ -1328,6 +1368,8 @@
         owned_turned,
         left_outer,
         right_outer,
+        left_moves,
+        right_moves,
         mom1_tiles,
         first_turned,
         mom2_tiles,

time: 1310 us -> 1270 us (0.969)
  waiting for transfers between devices: 240 us -> 183 us
  local copies, waits for them, and re-layouts: 187 us -> 211 us
  blocking collectives: 0 us -> 19.2 us
  Pallas kernels: 382 us -> 368 us
    optimization_barrier x0 -> x9, local copies, waits for them, and re-layouts: none -> 35.1 us  [the longest x8 31.8 us: landed(): arrived, held['owned'] = lax.optimization_barrier((arrived, held['owned']))]
    all_to_all x1, waiting for transfers between devices: 57.7 us -> 35.8 us  [swap_all(): return lax.all_to_all(rows, ('dp', 'vocab'), 0, 0, tiled=True)]
    all_to_all x0 -> x2, blocking collectives: none -> 19.2 us  [the longest x1 10.2 us: ready(): lax.all_to_all(held['gains'], ('dp', 'vocab'), 0, 0, tiled=True)]
    all_to_all x5 -> x4, waiting for transfers between devices: 45.5 us -> 26.4 us  [spread(): lax.all_to_all(jnp.broadcast_to(value[None], (peers, *value.shape)), axes...]
    all_to_all x2, waiting for transfers between devices: 65 us -> 48.1 us  [swap_rows(): return lax.all_to_all(rows, 'vocab', 0, 0, tiled=True)]
    unnamed x513 -> x559, local copies, waits for them, and re-layouts: 107 us -> 98.8 us
  transfers between devices with their start and end apart: 40 -> 38, of which waited for: 21 -> 19; matrix products, arithmetic and copies ran while one was open for 31% -> 33% of each run, Pallas kernels for 23% -> 22%
where the time goes in v4:
time: 1270 us; the launch traced here: 1260 us
  Pallas kernels  368 us (29%)
  matrix products  251 us (20%)
  local copies, waits for them, and re-layouts  211 us (17%)
  waiting for transfers between devices  183 us (14%)
  other arithmetic  143 us (11%)
  starting transfers between devices  54.9 us (4%)
  between operations  25.8 us (2%)
  blocking collectives  19.2 us (2%)
    pallas_call x6, Pallas kernels, attend_backward(): pl.pallas_call(kernel, out_shape=(jax.ShapeDtypeStruct((MICRO * rows, D),...  124 us
    unnamed x559, local copies, waits for them, and re-layouts  98.8 us
    pallas_call x5, Pallas kernels, attend_forward(): pl.pallas_call(kernel, out_shape=(jax.ShapeDtypeStruct((MICRO * rows, D),...  84.3 us
    dot_general x19, matrix products, linear(): return jnp.dot(left_op, right_op, preferred_element_type=jnp.float32)  73.4 us
    dot_general x23, matrix products, outer_sum(): lax.dot_general(left_op, right_op, (((0,), (0,)), ((), ())), preferred_el...  67.1 us
    ppermute x26, waiting for transfers between devices, halve(): arrived = lax.ppermute(sent, ('dp', 'vocab'), pairs)  62.3 us
    dot_general x19, matrix products, linear_tr(): lax.dot_general(left_op, right_op, (((1,), (1,)), ((), ())), preferred_el...  60.9 us
    pallas_call x5, Pallas kernels, take_rows(): pl.pallas_call(kernel, out_shape=jax.ShapeDtypeStruct((whole, width), kin...  56.7 us
  transfers between devices with their start and end apart: 38, of which 19 were waited for; matrix products, arithmetic and copies ran while one was open for 33% of the time, Pallas kernels for 22%

profile of v4, /device:TPU:0, one launch (start us, length us, event | category | flops | bytes accessed | tf_op | source)
XLA Modules:
  0.0 1256.8 jit_solution(14616950192350546715)
XLA Ops:
  44.1 13.5 %all-to-all-done.3 = s32[32,1,2688]{2,1,0:T(1,128)S(1)} async-done(((s32[32,1,2688]{2,1,0:T(1,128)}), s32[32,1,2688]{2,1,0:T(1,128)S(1)}, u32[]{:S(2)}, u32[]{:S(2)}) %all-to-all-start.3) | async-done | bytes 344096 | tf_op jit(solution)/shard_map/all_to_all | solution.py:803
  62.5 16.6 %shard_map.332 = bf16[2688,512]{1,0:T(8,128)(2,1)} custom-call(s32[2688]{0:T(1024)S(1)} %max.32.index_ref, f32[4096,512]{1,0:T(8,128)} %source_ref.3), custom_call_target="tpu_custom_call" | custom-call | tf_op jit(solution)/shard_map/pallas_call | solution.py:754
  130.8 38.9 %all-to-all-done.4 = bf16[8,336,512]{2,1,0:T(8,128)(2,1)} async-done(((bf16[8,336,512]{2,1,0:T(8,128)(2,1)}), bf16[8,336,512]{2,1,0:T(8,128)(2,1)}, u32[]{:S(2)}, u32[]{:S(2)}) %all-to-all-start.4) | async-done | bytes 2752544 | tf_op jit(solution)/shard_map/all_to_all | solution.py:883
  169.7 13.7 %conditional.2 = (bf16[512,2048]{1,0:T(8,128)(2,1)}, bf16[512,2048]{1,0:T(8,128)(2,1)S(1)}, bf16[512,2048]{1,0:T(8,128)(2,1)S(1)}, bf16[512,2048]{1,0:T(8,128)(2,1)}, bf16[512,2048]{1,0:T(8,128)(2,1)}) conditional(s32[]{:T(128)} %convert_element_type.1090, (s32[2816]{0:T(1024)S(1)}, bf16[1408,32,128]{2,1,0:T(8,128)(2,1)}) %tuple.99, ...), branch_computations={%region_26.27_spmd, %region_27.28_spmd} | conditional | bytes 90210416 | solution.py:1175
  170.1 10.0 branch_0_fun.1
  200.7 10.7 shard_map.334
  222.6 46.6 %shard_map.335 = (bf16[2048,512]{1,0:T(8,128)(2,1)S(1)}, f32[2048,512]{1,0:T(8,128)S(1)}) custom-call(s32[2]{0:T(128)S(1)} %bitcast.509, bf16[2048,1536]{1,0:T(8,128)(2,1)S(1)} %convolution_convert_fusion.query_ref.key_ref.value_ref, bf16[2048,1536]{1,0:T(8,128)(2,1)S(1)} %convolution_convert_fusion.query_ref.key_ref.value_ref, ...), custom_call_target="tpu_custom_call" | custom-call | flops 4294967296 | bytes 16777216 | tf_op jit(solution)/shard_map/pallas_call | solution.py:112
  272.0 11.3 fusion.544
  286.9 10.7 multiply_reduce_fusion.6
  301.4 9.2 all-to-all-done.5
  310.8 20.1 %shard_map.337 = (bf16[512,2048]{1,0:T(8,128)(2,1)S(1)}, bf16[512,2048]{1,0:T(8,128)(2,1)S(1)}, bf16[512,2048]{1,0:T(8,128)(2,1)S(1)}, bf16[512,2048]{1,0:T(8,12...) custom-call(s32[2816]{0:T(1024)S(1)} %reshape.1992.place_ref, ...), custom_call_target="tpu_custom_call" | custom-call | tf_op jit(solution)/shard_map/pallas_call | solution.py:573
  357.4 12.9 %shard_map.339 = (bf16[512,512]{1,0:T(8,128)(2,1)S(1)}, f32[512,512]{1,0:T(8,128)S(1)}) custom-call(s32[2]{0:T(128)S(1)} %bitcast.510, bf16[512,512]{1,0:T(8,128)(2,1)S(1)} %convolution_convert_fusion.29.query_ref, bf16[2048,1024]{1,0:T(8,128)(2,1)S(1)} %convolution_convert_fusion.2.key_ref.value_ref, ...), custom_call_target="tpu_custom_call" | custom-call | flops 1073741824 | bytes 10485760 | tf_op jit(solution)/shard_map/pallas_call | solution.py:112
  388.4 13.1 %shard_map.341 = (bf16[512,512]{1,0:T(8,128)(2,1)S(1)}, f32[512,512]{1,0:T(8,128)S(1)}) custom-call(s32[2]{0:T(128)S(1)} %bitcast.511, bf16[512,512]{1,0:T(8,128)(2,1)S(1)} %convolution_convert_fusion.28.query_ref, bf16[2048,1024]{1,0:T(8,128)(2,1)S(1)} %convolution_convert_fusion.1.key_ref.value_ref, ...), custom_call_target="tpu_custom_call" | custom-call | flops 1073741824 | bytes 10485760 | tf_op jit(solution)/shard_map/pallas_call | solution.py:112
  477.7 9.9 all-to-all-done.8
  503.4 19.8 %shard_map.342 = (bf16[512,512]{1,0:T(8,128)(2,1)S(1)}, bf16[2048,512]{1,0:T(8,128)(2,1)S(1)}, bf16[2048,512]{1,0:T(8,128)(2,1)S(1)}) custom-call(s32[2]{0:T(128)S(1)} %bitcast.512, bf16[512,512]{1,0:T(8,128)(2,1)S(1)} %convolution_convert_fusion.28.query_ref, bf16[2048,1024]{1,0:T(8,128)(2,1)S(1)} %copy-done.7, bf16[2048,1024]{1,0:T(8,128)(2,1)S(1)} %copy-done.7, ...), custom_call_target="tpu_custom_call" | custom-call | flops 2684354560 | bytes 20971520 | tf_op jit(solution)/shard_map/pallas_call | solution.py:188
  550.0 19.8 %shard_map.344 = (bf16[512,512]{1,0:T(8,128)(2,1)S(1)}, bf16[2048,512]{1,0:T(8,128)(2,1)S(1)}, bf16[2048,512]{1,0:T(8,128)(2,1)S(1)}) custom-call(s32[2]{0:T(128)S(1)} %bitcast.513, bf16[512,512]{1,0:T(8,128)(2,1)S(1)} %convolution_convert_fusion.29.query_ref, bf16[2048,1024]{1,0:T(8,128)(2,1)S(1)} %copy-done.5, bf16[2048,1024]{1,0:T(8,128)(2,1)S(1)} %copy-done.5, ...), custom_call_target="tpu_custom_call" | custom-call | flops 2684354560 | bytes 20971520 | tf_op jit(solution)/shard_map/pallas_call | solution.py:188
  603.2 17.6 %fusion.161 = bf16[2048,2048]{1,0:T(8,128)(2,1)} fusion(f32[2048,2048]{1,0:T(8,128)} %fusion.544, bf16[512,2048]{1,0:T(8,128)(2,1)} %get-tuple-element.845, f32[2048,512]{1,0:T(8,128)S(1)} %add_add_fusion.2), kind=kOutput, calls=%fused_computation.250 | convolution fusion | flops 4379901952 | bytes 31457280 | tf_op jit(solution)/shard_map/dot_general | solution.py:52
  620.8 11.4 convolution_convert_fusion.11.refs_7_
  657.5 10.1 convolution_convert_fusion.14.refs_4_
  667.7 20.1 %shard_map.346 = (bf16[2176,32,128]{2,1,0:T(8,128)(2,1)}, bf16[640,32,128]{2,1,0:T(8,128)(2,1)S(1)}) custom-call(s32[2816]{0:T(1024)S(1)} %copy-done.180, bf16[512,2048]{1,0:T(8,128)(2,1)S(1)} %pad_maximum_fusion.3.refs_0_, bf16[512,2048]{1,0:T(8,128)(2,1)S(1)} %pad_maximum_fusion.4.refs_1_, bf16[512,2048]{1,0:T(8,128)(2,1)S(1)} %pad_maximum_fusion.5.refs_2_, ...), custom_call_target="tpu_custom_call" | custom-call | tf_op jit(solution)/shard_map/pallas_call | solution.py:654
  687.8 10.0 multiply_reduce_fusion.1
  726.9 34.8 %shard_map.347 = (bf16[2048,512]{1,0:T(8,128)(2,1)S(1)}, bf16[2048,512]{1,0:T(8,128)(2,1)S(1)}, bf16[2048,512]{1,0:T(8,128)(2,1)S(1)}) custom-call(s32[2]{0:T(128)S(1)} %bitcast.514, bf16[2048,1536]{1,0:T(8,128)(2,1)} %copy-done.1, bf16[2048,1536]{1,0:T(8,128)(2,1)} %copy-done.1, bf16[2048,1536]{1,0:T(8,128)(2,1)} %copy-done.1, f32[2048,512]{1,0:T(8,128)S(1)} %copy-done.12, ...), custom_call_target="tpu_custom_call" | custom-call | flops 5368709120 | bytes 16777216 | tf_op jit(solution)/shard_map/pallas_call | solution.py:188
  788.1 34.4 %shard_map.348 = (bf16[2048,512]{1,0:T(8,128)(2,1)S(1)}, bf16[2048,512]{1,0:T(8,128)(2,1)S(1)}, bf16[2048,512]{1,0:T(8,128)(2,1)S(1)}) custom-call(s32[2]{0:T(128)S(1)} %bitcast.515, bf16[2048,1536]{1,0:T(8,128)(2,1)} %copy-done.1, bf16[2048,1536]{1,0:T(8,128)(2,1)} %copy-done.1, ...), custom_call_target="tpu_custom_call", output_to_operand_aliasing={{0}: (6, {}), {1}: (7, {}), {2}: (8, {})} | custom-call | flops 5368709120 | bytes 16777216 | tf_op jit(solution)/shard_map/pallas_call | solution.py:188
  858.9 17.5 %collective-permute-done.18 = bf16[88,32,128]{2,1,0:T(8,128)(2,1)S(1)} collective-permute-done((bf16[88,32,128]{2,1,0:T(8,128)(2,1)}, bf16[88,32,128]{2,1,0:T(8,128)(2,1)S(1)}, u32[]{:S(2)}, u32[]{:S(2)}) %collective-permute-start.18) | collective-permute-done | bytes 720928 | tf_op jit(solution)/shard_map/ppermute | solution.py:705
  889.1 13.1 %collective-permute-done.21 = bf16[44,32,128]{2,1,0:T(8,128)(2,1)S(1)} collective-permute-done((bf16[44,32,128]{2,1,0:T(8,128)(2,1)S(1)}, bf16[44,32,128]{2,1,0:T(8,128)(2,1)S(1)}, u32[]{:S(2)}, u32[]{:S(2)}) %collective-permute-start.21) | collective-permute-done | bytes 360480 | tf_op jit(solution)/shard_map/ppermute | solution.py:705
  905.8 17.2 %shard_map.349 = bf16[4096,512]{1,0:T(8,128)(2,1)S(1)} custom-call(s32[4096]{0:T(1024)S(1)} %max.34.index_ref, f32[2560,512]{1,0:T(8,128)S(1)} %maximum_multiply_fusion.source_ref), custom_call_target="tpu_custom_call" | custom-call | tf_op jit(solution)/shard_map/pallas_call | solution.py:754
  967.1 10.2 all_to_all.127
  977.4 8.9 all_to_all.128
  1049.2 35.8 %all-to-all-done.9 = bf16[32,128,512]{2,1,0:T(8,128)(2,1)} async-done(((bf16[32,128,512]{2,1,0:T(8,128)(2,1)}), bf16[32,128,512]{2,1,0:T(8,128)(2,1)}, u32[]{:S(2)}, u32[]{:S(2)}) %all-to-all-start.9) | async-done | bytes 4194336 | tf_op jit(solution)/shard_map/all_to_all | solution.py:915
  1085.0 9.4 shard_map.352
  1191.4 27.7 %shard_map.353 = f32[64,64,256]{2,1,0:T(8,128)S(1)} custom-call(f32[64,64,256]{2,1,0:T(8,128)S(1)} %pad.19.in_ref), custom_call_target="tpu_custom_call" | custom-call | tf_op jit(solution)/shard_map/pallas_call | solution.py:971
  1225.9 22.8 %fusion.546 = (bf16[4096,512]{1,0:T(8,128)(2,1)}, f32[4096,512]{1,0:T(8,128)}, f32[4096,512]{1,0:T(8,128)}, f32[4096,512]{1,0:T(8,128)}) fusion(f32[4096,512]{1,0:T(8,128)} %get-tuple-element.1695, f32[]{:T(128)S(6)} %min.3, bf16[4096,512]{1,0:T(8,128)(2,1)} %all-gather.14.cloned.1.call-done, f32[4096,512]{1,0:T(8,128)} %param.38, f32[4096,512]{1,0:T(8,128)} %param.39), kind=kLoop, calls=%fused_computation.1102 | loop fusion | flops 37748736 | bytes 58720260 | tf_op jit(solution)/shard_map/convert_element_type | solution.py:1401
  (1052 shorter events, 666.4 us)
Async XLA Ops:
  7.2 162.5 %all-gather.8.cloned.1.call-start = ((), (), s32[]{:S(2)}) async-start(), calls=%async_computation.14 | async-start | bytes 11894784 | tf_op jit(solution)/shard_map/all_gather | solution.py:1143
  36.8 20.8 %all-to-all-start.3 = ((s32[32,1,2688]{2,1,0:T(1,128)}), s32[32,1,2688]{2,1,0:T(1,128)S(1)}, u32[]{:S(2)}, u32[]{:S(2)}) async-start(s32[32,1,2688]{2,1,0:T(1,128)} %broadcast_in_dim.472), calls=%async_computation.3 | async-start | bytes 688128 | tf_op jit(solution)/shard_map/all_to_all | solution.py:803
  83.6 86.1 %all-to-all-start.4 = ((bf16[8,336,512]{2,1,0:T(8,128)(2,1)}), bf16[8,336,512]{2,1,0:T(8,128)(2,1)}, u32[]{:S(2)}, u32[]{:S(2)}) async-start(bf16[8,336,512]{2,1,0:T(8,128)(2,1)} %bitcast.58), calls=%async_computation.4 | async-start | bytes 5505024 | tf_op jit(solution)/shard_map/all_to_all | solution.py:883
  183.3 127.2 %all-gather.10.cloned.1.call-start = ((), (), s32[]{:S(2)}) async-start(), calls=%async_computation.15 | async-start | bytes 11894784 | tf_op jit(solution)/shard_map/all_gather | solution.py:1164
  283.3 27.3 %all-to-all-start.5 = ((bf16[8,112,512]{2,1,0:T(8,128)(2,1)}), bf16[8,112,512]{2,1,0:T(8,128)(2,1)S(1)}, u32[]{:S(2)}, u32[]{:S(2)}) async-start(bf16[8,112,512]{2,1,0:T(8,128)(2,1)} %bitcast.67), calls=%async_computation.5 | async-start | bytes 1835008 | tf_op jit(solution)/shard_map/all_to_all | solution.py:883
  416.1 19.5 %all-to-all-start.6 = ((bf16[8,64,512]{2,1,0:T(8,128)(2,1)}), bf16[8,64,512]{2,1,0:T(8,128)(2,1)}, u32[]{:S(2)}, u32[]{:S(2)}) async-start(bf16[8,64,512]{2,1,0:T(8,128)(2,1)} %broadcast_in_dim.492), calls=%async_computation.6 | async-start | bytes 1048576 | tf_op jit(solution)/shard_map/all_to_all | solution.py:803
  444.6 13.7 %all-to-all-start.7 = ((f32[32,3,512]{2,1,0:T(4,128)}), f32[32,3,512]{2,1,0:T(4,128)}, u32[]{:S(2)}, u32[]{:S(2)}) async-start(f32[32,3,512]{2,1,0:T(4,128)} %broadcast_in_dim.494), calls=%async_computation.7 | async-start | bytes 524288 | tf_op jit(solution)/shard_map/all_to_all | solution.py:803
  468.0 19.6 %all-to-all-start.8 = ((bf16[8,64,512]{2,1,0:T(8,128)(2,1)}), bf16[8,64,512]{2,1,0:T(8,128)(2,1)}, u32[]{:S(2)}, u32[]{:S(2)}) async-start(bf16[8,64,512]{2,1,0:T(8,128)(2,1)} %bitcast.608), calls=%async_computation.8 | async-start | bytes 1048576 | tf_op jit(solution)/shard_map/all_to_all | solution.py:1244
  472.2 228.3 %all-gather.12.cloned.1.call-start = ((), (), s32[]{:S(2)}) async-start(), calls=%async_computation.16 | async-start | bytes 2162688 | tf_op jit(solution)/shard_map/all_gather | solution.py:1211
  716.1 45.5 %collective-permute-start.13 = (bf16[1088,32,128]{2,1,0:T(8,128)(2,1)}, bf16[1088,32,128]{2,1,0:T(8,128)(2,1)}, u32[]{:S(2)}, u32[]{:S(2)}) collective-permute-start(bf16[1088,32,128]{2,1,0:T(8,128)(2,1)} %dynamic-slice_bitcast_fusion.13), channel_id=1, source_target_pairs={{0,1},{1,0},{2,3},{3,2},{4,5},{5,4},{6,7},{7,6},{8,9},{9,8},{10,11... | collective-permute-start | bytes 26738696 | tf_op jit(solution)/shard_map/ppermute | solution.py:705
  783.7 39.6 %collective-permute-start.15 = (bf16[176,32,128]{2,1,0:T(8,128)(2,1)}, bf16[176,32,128]{2,1,0:T(8,128)(2,1)S(1)}, u32[]{:S(2)}, u32[]{:S(2)}) collective-permute-start(bf16[176,32,128]{2,1,0:T(8,128)(2,1)} %dynamic-slice_bitcast_fusion.17), channel_id=1, source_target_pairs={{0,16},{1,17},{2,18},{3,19},{4,20},{5,21},{6,22},{7,23},{8,24},{9,... | collective-permute-start | bytes 4325384 | tf_op jit(solution)/shard_map/ppermute | solution.py:705
  785.8 42.1 %collective-permute-start.14 = (bf16[192,32,128]{2,1,0:T(8,128)(2,1)S(1)}, bf16[192,32,128]{2,1,0:T(8,128)(2,1)}, u32[]{:S(2)}, u32[]{:S(2)}) collective-permute-start(bf16[192,32,128]{2,1,0:T(8,128)(2,1)S(1)} %dynamic-slice_bitcast_fusion.15), channel_id=1, source_target_pairs={{0,8},{1,9},{2,10},{3,11},{4,12},{5,13},{6,14},{7,15},{8,0},{9,1},... | collective-permute-start | bytes 4718600 | tf_op jit(solution)/shard_map/ppermute | solution.py:705
  788.1 36.6 %collective-permute-start.16 = (bf16[176,32,128]{2,1,0:T(8,128)(2,1)}, bf16[176,32,128]{2,1,0:T(8,128)(2,1)}, u32[]{:S(2)}, u32[]{:S(2)}) collective-permute-start(bf16[176,32,128]{2,1,0:T(8,128)(2,1)} %dynamic-slice_bitcast_fusion.16), channel_id=1, source_target_pairs={{0,2},{1,3},{2,0},{3,1},{4,6},{5,7},{6,4},{7,5},{8,10},{9,11},{10,... | collective-permute-start | bytes 4325384 | tf_op jit(solution)/shard_map/ppermute | solution.py:705
  843.0 40.4 %collective-permute-start.17 = (bf16[96,32,128]{2,1,0:T(8,128)(2,1)}, bf16[96,32,128]{2,1,0:T(8,128)(2,1)}, u32[]{:S(2)}, u32[]{:S(2)}) collective-permute-start(bf16[96,32,128]{2,1,0:T(8,128)(2,1)} %dynamic-slice_bitcast_fusion.18), channel_id=1, source_target_pairs={{0,16},{1,17},{2,18},{3,19},{4,20},{5,21},{6,22},{7,23},{8,24},{9,... | collective-permute-start | bytes 2359304 | tf_op jit(solution)/shard_map/ppermute | solution.py:705
  845.1 31.3 %collective-permute-start.18 = (bf16[88,32,128]{2,1,0:T(8,128)(2,1)}, bf16[88,32,128]{2,1,0:T(8,128)(2,1)S(1)}, u32[]{:S(2)}, u32[]{:S(2)}) collective-permute-start(bf16[88,32,128]{2,1,0:T(8,128)(2,1)} %dynamic-slice_bitcast_fusion.20), channel_id=1, source_target_pairs={{0,2},{1,3},{2,0},{3,1},{4,6},{5,7},{6,4},{7,5},{8,10},{9,11},{10,... | collective-permute-start | bytes 2162696 | tf_op jit(solution)/shard_map/ppermute | solution.py:705
  848.1 33.8 %collective-permute-start.19 = (bf16[88,32,128]{2,1,0:T(8,128)(2,1)}, bf16[88,32,128]{2,1,0:T(8,128)(2,1)}, u32[]{:S(2)}, u32[]{:S(2)}) collective-permute-start(bf16[88,32,128]{2,1,0:T(8,128)(2,1)} %dynamic-slice_bitcast_fusion.19), channel_id=1, source_target_pairs={{0,4},{1,5},{2,6},{3,7},{4,0},{5,1},{6,2},{7,3},{8,12},{9,13},{10,... | collective-permute-start | bytes 2162696 | tf_op jit(solution)/shard_map/ppermute | solution.py:705
  853.1 70.0 %collective-permute-start.26 = (bf16[320,32,128]{2,1,0:T(8,128)(2,1)}, bf16[320,32,128]{2,1,0:T(8,128)(2,1)}, u32[]{:S(2)}, u32[]{:S(2)}) collective-permute-start(bf16[320,32,128]{2,1,0:T(8,128)(2,1)} %dynamic-slice_bitcast_fusion.14), channel_id=1, source_target_pairs={{0,1},{1,0},{2,3},{3,2},{4,5},{5,4},{6,7},{7,6},{8,9},{9,8},{10,11... | collective-permute-start | bytes 7864328 | tf_op jit(solution)/shard_map/ppermute | solution.py:705
  884.8 17.6 %collective-permute-start.20 = (bf16[48,32,128]{2,1,0:T(8,128)(2,1)S(1)}, bf16[48,32,128]{2,1,0:T(8,128)(2,1)S(1)}, u32[]{:S(2)}, u32[]{:S(2)}) collective-permute-start(bf16[48,32,128]{2,1,0:T(8,128)(2,1)S(1)} %dynamic-slice_bitcast_fusion.24), channel_id=1, source_target_pairs={{0,2},{1,3},{2,0},{3,1},{4,6},{5,7},{6,4},{7,5},{8,10},{9,11},{10,... | collective-permute-start | bytes 1179656 | tf_op jit(solution)/shard_map/ppermute | solution.py:705
  885.0 17.3 %collective-permute-start.21 = (bf16[44,32,128]{2,1,0:T(8,128)(2,1)S(1)}, bf16[44,32,128]{2,1,0:T(8,128)(2,1)S(1)}, u32[]{:S(2)}, u32[]{:S(2)}) collective-permute-start(bf16[44,32,128]{2,1,0:T(8,128)(2,1)S(1)} %dynamic-slice_bitcast_fusion.26), channel_id=1, source_target_pairs={{0,4},{1,5},{2,6},{3,7},{4,0},{5,1},{6,2},{7,3},{8,12},{9,13},{10,... | collective-permute-start | bytes 1081352 | tf_op jit(solution)/shard_map/ppermute | solution.py:705
  887.0 15.3 %collective-permute-start.22 = (bf16[44,32,128]{2,1,0:T(8,128)(2,1)S(1)}, bf16[44,32,128]{2,1,0:T(8,128)(2,1)S(1)}, u32[]{:S(2)}, u32[]{:S(2)}) collective-permute-start(bf16[44,32,128]{2,1,0:T(8,128)(2,1)S(1)} %dynamic-slice_bitcast_fusion.25), channel_id=1, source_target_pairs={{0,8},{1,9},{2,10},{3,11},{4,12},{5,13},{6,14},{7,15},{8,0},{9,1},... | collective-permute-start | bytes 1081352 | tf_op jit(solution)/shard_map/ppermute | solution.py:705
  902.6 20.4 %collective-permute-start.25 = (bf16[22,32,128]{2,1,0:T(8,128)(2,1)S(1)}, bf16[22,32,128]{2,1,0:T(8,128)(2,1)S(1)}, u32[]{:S(2)}, u32[]{:S(2)}) collective-permute-start(bf16[22,32,128]{2,1,0:T(8,128)(2,1)S(1)} %dynamic-slice_bitcast_fusion.31), channel_id=1, source_target_pairs={{0,16},{1,17},{2,18},{3,19},{4,20},{5,21},{6,22},{7,23},{8,24},{9,... | collective-permute-start | bytes 540680 | tf_op jit(solution)/shard_map/ppermute | solution.py:705
  903.6 19.5 %collective-permute-start.24 = (bf16[22,32,128]{2,1,0:T(8,128)(2,1)S(1)}, bf16[22,32,128]{2,1,0:T(8,128)(2,1)S(1)}, u32[]{:S(2)}, u32[]{:S(2)}) collective-permute-start(bf16[22,32,128]{2,1,0:T(8,128)(2,1)S(1)} %dynamic-slice_bitcast_fusion.32), channel_id=1, source_target_pairs={{0,8},{1,9},{2,10},{3,11},{4,12},{5,13},{6,14},{7,15},{8,0},{9,1},... | collective-permute-start | bytes 540680 | tf_op jit(solution)/shard_map/ppermute | solution.py:705
  904.9 22.5 %collective-permute-start.23 = (bf16[24,32,128]{2,1,0:T(8,128)(2,1)S(1)}, bf16[24,32,128]{2,1,0:T(8,128)(2,1)S(1)}, u32[]{:S(2)}, u32[]{:S(2)}) collective-permute-start(bf16[24,32,128]{2,1,0:T(8,128)(2,1)S(1)} %dynamic-slice_bitcast_fusion.30), channel_id=1, source_target_pairs={{0,4},{1,5},{2,6},{3,7},{4,0},{5,1},{6,2},{7,3},{8,12},{9,13},{10,... | collective-permute-start | bytes 589832 | tf_op jit(solution)/shard_map/ppermute | solution.py:705
  927.3 9.6 collective-permute-start.35
  928.7 10.8 collective-permute-start.31
  930.4 10.3 collective-permute-start.27
  937.1 10.2 collective-permute-start.36
  939.6 8.8 collective-permute-start.32
  940.9 14.9 %collective-permute-start.28 = (bf16[32,32,128]{2,1,0:T(8,128)(2,1)S(1)}, bf16[32,32,128]{2,1,0:T(8,128)(2,1)S(1)}, u32[]{:S(2)}, u32[]{:S(2)}) collective-permute-start(bf16[32,32,128]{2,1,0:T(8,128)(2,1)S(1)} %dynamic-slice_bitcast_fusion.27), channel_id=1, source_target_pairs={{0,16},{1,17},{2,18},{3,19},{4,20},{5,21},{6,22},{7,23},{8,24},{9,... | collective-permute-start | bytes 786440 | tf_op jit(solution)/shard_map/ppermute | solution.py:705
  986.4 98.7 %all-to-all-start.9 = ((bf16[32,128,512]{2,1,0:T(8,128)(2,1)}), bf16[32,128,512]{2,1,0:T(8,128)(2,1)}, u32[]{:S(2)}, u32[]{:S(2)}) async-start(bf16[32,128,512]{2,1,0:T(8,128)(2,1)} %bitcast.505), calls=%async_computation.9 | async-start | bytes 8388608 | tf_op jit(solution)/shard_map/all_to_all | solution.py:915
  990.0 236.0 %all-gather.14.cloned.1.call-start = ((), (), s32[]{:S(2)}) async-start(), calls=%async_computation.17 | async-start | bytes 5242880 | tf_op jit(solution)/shard_map/all_gather | solution.py:1362
  1105.3 35.5 %all-to-all-start.12 = ((f32[32,1,128]{2,1,0:T(1,128)}), f32[32,1,128]{2,1,0:T(1,128)S(1)}, u32[]{:S(2)}, u32[]{:S(2)}) async-start(f32[32,1,128]{2,1,0:T(1,128)} %broadcast_in_dim_broadcast_in_dim_broadcast_in_dim.3), calls=%async_computation.12 | async-start | bytes 32768 | tf_op jit(solution)/shard_map/all_to_all | solution.py:803
  (272 other events, 2022.8 us)
Sparse Core Ops, SparseCore 0:
  20.5 110.2 all-gather.7
  187.6 90.3 all-gather.9
  477.2 56.1 all-gather.11
  1099.0 50.3 all-gather.13

commit v5 on v4

--- a/solution.py
+++ b/solution.py
@@ -1150,6 +1150,7 @@
         first_turned,
         target_sent,
         place_of,
+        wave_set,
     ) = lax.optimization_barrier(
         (
             own_folded[first_size:],
@@ -1159,6 +1160,7 @@
             turn_in(left_later, mom1_later, right_later),
             target_sent,
             place_of,
+            waves(src_count, D),
         )
     )
     second_tiles = lax.all_gather(own_second, ("dp", "vocab"), axis=0, tiled=True)
@@ -1185,8 +1187,6 @@
         for mat_no, matrix in zip(decoder_mats, decoder_set):
             weights[mat_no] = matrix
         return (held, with_waves(target_finish(arrived), tgt_count))
-
-    wave_set = waves(src_count, D)
 
     def with_waves(rows, length):
         return rows * math.sqrt(D) + jnp.tile(wave_set[:length], (MICRO, 1))
@@ -1260,7 +1260,18 @@
     both = [devices * soon_size, devices * late_size]
     held = {}
 
+    def gain_sums(gain_rows):
+        count = gain_rows.shape[0] * D
+        share = -(-count // (devices * 128)) * 128
+        flat = jnp.pad(gain_rows.reshape(-1), (0, devices * share - count))
+        parts = lax.all_to_all(
+            flat.reshape(devices, share), ("dp", "vocab"), 0, 0, tiled=True
+        )
+        summed = spread(jnp.sum(parts, axis=0)[None], ("dp", "vocab"), devices)
+        return summed.reshape(-1)[:count].reshape(gain_rows.shape)
+
     def before_last(grad_stream):
+        held["gains"] = gain_sums(jnp.stack(gain_store[1:]))
         blocks, held["begun"] = fold_gradients(matrix_store, soon_mats, back_of, both)
         grad_stream, blocks, held["quarter"] = lax.optimization_barrier(
             (grad_stream, blocks, grad_quarter)
@@ -1270,7 +1281,9 @@
 
     def between_last(value):
         if "parts" not in held:
-            value, total = lax.optimization_barrier((value, held["total"]))
+            value, total, held["gains"] = lax.optimization_barrier(
+                (value, held["total"], held["gains"])
+            )
             held["parts"], held["done"] = (split_parts(total, soon_plan, devices), 0)
         elif held["done"] < len(soon_plan[0][1]):
             parts = one_exchange(held["parts"], soon_plan, held["done"], devices)
@@ -1293,7 +1306,9 @@
     grad_rows = jnp.concatenate([grad_source, grad_target], 0) * math.sqrt(D)
     grad_rows = between_last(grad_rows)
     [late_blocks] = fold_gradients(matrix_store, late_mats, back_of, both, held["begun"])
-    late_parts = split_parts(first_exchange(late_blocks, devices), late_plan, devices)
+    late_total = first_exchange(late_blocks, devices)
+    grad_rows, late_total = lax.optimization_barrier((grad_rows, late_total))
+    late_parts = split_parts(late_total, late_plan, devices)
     late_parts = one_exchange(late_parts, late_plan, 0, devices)
 
     late_sum = other_exchanges(late_parts, late_plan, devices, 1)
@@ -1303,15 +1318,9 @@
         parts = split_parts(first_exchange(blocks, devices), soon_plan, devices)
         return other_exchanges(parts, soon_plan, devices)
 
-    share = -(-GAINS * D // (devices * 128)) * 128
-    gain_flat = jnp.stack(gain_store).reshape(-1)
-    gain_flat = jnp.pad(gain_flat, (0, devices * share - GAINS * D)).reshape(devices, share)
-
     def ready(rows):
         sums = other_exchanges(held["parts"], soon_plan, devices, held["done"])
-        rows, sums, late, held["gains"] = lax.optimization_barrier(
-            (rows, sums, late_sum, gain_flat)
-        )
+        rows, sums, late = lax.optimization_barrier((rows, sums, late_sum))
         sums = lax.cond(jnp.min(soon_count) < soon_size, exchange_again, lambda: sums)
         owned_grad = unfold_ranked(
             jnp.concatenate([sums, late], 0),
@@ -1319,10 +1328,6 @@
         )
         left_outer = jnp.einsum("tik,tjk->tij", owned_grad, owned_grad, precision=HIGH)
         right_outer = jnp.einsum("tki,tkj->tij", owned_grad, owned_grad, precision=HIGH)
-        gain_part = jnp.sum(
-            lax.all_to_all(held["gains"], ("dp", "vocab"), 0, 0, tiled=True), axis=0
-        )
-        gain_total = spread(gain_part[None], ("dp", "vocab"), devices)
         held["owned"] = (
             owned_grad,
             turn_in(basis_left, owned_grad, basis_right),
@@ -1331,7 +1336,6 @@
             (turned_by(stat_left, basis_left), turned_by(left_outer, basis_left)),
             (turned_by(stat_right, basis_right), turned_by(right_outer, basis_right)),
             jnp.sum(owned_grad * owned_grad),
-            gain_total.reshape(-1)[: GAINS * D].reshape(GAINS, D),
         )
         return rows
 
@@ -1351,12 +1355,13 @@
         left_moves,
         right_moves,
         owned_squares,
-        gain_total,
     ) = held["owned"]
     squares = owned_squares + jnp.sum(grad_quarter * grad_quarter)
-    square_total = jnp.sum(
-        spread(jnp.full((1, 128), squares), ("dp", "vocab"), devices)[:, 0, 0]
-    )
+    last_facts = jnp.concatenate([gain_store[0].reshape(-1, 128), jnp.full((1, 128), squares)], 0)
+    last_facts = spread(last_facts, ("dp", "vocab"), devices)
+    last_facts = jnp.sum(last_facts.reshape(devices, -1, 128), axis=0)
+    square_total = last_facts[-1, 0]
+    gain_total = jnp.concatenate([last_facts[:-1].reshape(1, D), held["gains"]], 0)
     grad_norm = jnp.sqrt(square_total + jnp.sum(gain_total * gain_total))
     factor = jnp.minimum(1.0, CLIP_AT / grad_norm)
     table_grad = lax.all_gather(

time: 1270 us -> 1270 us (level)
  waiting for transfers between devices: 183 us -> 207 us
  blocking collectives: 19.2 us -> 0 us
  local copies, waits for them, and re-layouts: 211 us -> 195 us
    all_to_all x2 -> x0, blocking collectives: 19.2 us -> none  [the longest x1 10.2 us: ready(): lax.all_to_all(held['gains'], ('dp', 'vocab'), 0, 0, tiled=True)]
    unnamed x559 -> x541, local copies, waits for them, and re-layouts: 98.8 us -> 92.3 us
    all_to_all x4 -> x5, waiting for transfers between devices: 26.4 us -> 30.1 us  [spread(): lax.all_to_all(jnp.broadcast_to(value[None], (peers, *value.shape)), axes...]
  transfers between devices with their start and end apart: 38 -> 40, of which waited for: 19 -> 22; matrix products, arithmetic and copies ran while one was open for 33% -> 33% of each run, Pallas kernels for 22% -> 22%
where the time goes in v5:
time: 1270 us; the launch traced here: 1260 us
  Pallas kernels  368 us (29%)
  matrix products  260 us (20%)
  waiting for transfers between devices  207 us (16%)
  local copies, waits for them, and re-layouts  195 us (15%)
  other arithmetic  139 us (11%)
  starting transfers between devices  63.3 us (5%)
  between operations  25.4 us (2%)
    pallas_call x6, Pallas kernels, attend_backward(): pl.pallas_call(kernel, out_shape=(jax.ShapeDtypeStruct((MICRO * rows, D),...  123 us
    unnamed x541, local copies, waits for them, and re-layouts  92.3 us
    pallas_call x5, Pallas kernels, attend_forward(): pl.pallas_call(kernel, out_shape=(jax.ShapeDtypeStruct((MICRO * rows, D),...  83.9 us
    dot_general x19, matrix products, linear(): return jnp.dot(left_op, right_op, preferred_element_type=jnp.float32)  77.5 us
    ppermute x26, waiting for transfers between devices, halve(): arrived = lax.ppermute(sent, ('dp', 'vocab'), pairs)  69.4 us
    dot_general x23, matrix products, outer_sum(): lax.dot_general(left_op, right_op, (((0,), (0,)), ((), ())), preferred_el...  67.9 us
    dot_general x19, matrix products, linear_tr(): lax.dot_general(left_op, right_op, (((1,), (1,)), ((), ())), preferred_el...  65.7 us
    pallas_call x5, Pallas kernels, take_rows(): pl.pallas_call(kernel, out_shape=jax.ShapeDtypeStruct((whole, width), kin...  56.7 us
  transfers between devices with their start and end apart: 40, of which 22 were waited for; matrix products, arithmetic and copies ran while one was open for 33% of the time, Pallas kernels for 22%

profile of v5, /device:TPU:0, one launch (start us, length us, event | category | flops | bytes accessed | tf_op | source)
XLA Modules:
  0.0 1259.0 jit_solution(17597331424369913672)
XLA Ops:
  41.7 12.7 %all-to-all-done.3 = s32[32,1,2688]{2,1,0:T(1,128)S(1)} async-done(((s32[32,1,2688]{2,1,0:T(1,128)}), s32[32,1,2688]{2,1,0:T(1,128)S(1)}, u32[]{:S(2)}, u32[]{:S(2)}) %all-to-all-start.3) | async-done | bytes 344096 | tf_op jit(solution)/shard_map/all_to_all | solution.py:803
  60.0 16.6 %shard_map.332 = bf16[2688,512]{1,0:T(8,128)(2,1)} custom-call(s32[2688]{0:T(1024)S(1)} %max.32.index_ref, f32[4096,512]{1,0:T(8,128)} %source_ref.3), custom_call_target="tpu_custom_call" | custom-call | tf_op jit(solution)/shard_map/pallas_call | solution.py:754
  84.8 8.6 shard_map.333
  125.8 44.8 %all-to-all-done.4 = bf16[8,336,512]{2,1,0:T(8,128)(2,1)} async-done(((bf16[8,336,512]{2,1,0:T(8,128)(2,1)}), bf16[8,336,512]{2,1,0:T(8,128)(2,1)}, u32[]{:S(2)}, u32[]{:S(2)}) %all-to-all-start.4) | async-done | bytes 2752544 | tf_op jit(solution)/shard_map/all_to_all | solution.py:883
  170.7 13.2 %conditional.2 = (bf16[512,2048]{1,0:T(8,128)(2,1)}, bf16[512,2048]{1,0:T(8,128)(2,1)S(1)}, bf16[512,2048]{1,0:T(8,128)(2,1)S(1)}, bf16[512,2048]{1,0:T(8,128)(2,1)}, bf16[512,2048]{1,0:T(8,128)(2,1)}) conditional(s32[]{:T(128)} %convert_element_type.1090, (s32[2816]{0:T(1024)S(1)}, bf16[1408,32,128]{2,1,0:T(8,128)(2,1)}) %tuple.100, ...), branch_computations={%region_26.27_spmd, %region_27.28_spmd} | conditional | bytes 91652232 | solution.py:1177
  170.7 10.0 branch_0_fun.1
  195.0 10.7 shard_map.334
  216.7 46.6 %shard_map.335 = (bf16[2048,512]{1,0:T(8,128)(2,1)S(1)}, f32[2048,512]{1,0:T(8,128)S(1)}) custom-call(s32[2]{0:T(128)S(1)} %bitcast.510, bf16[2048,1536]{1,0:T(8,128)(2,1)S(1)} %convolution_convert_fusion.query_ref.key_ref.value_ref, bf16[2048,1536]{1,0:T(8,128)(2,1)S(1)} %convolution_convert_fusion.query_ref.key_ref.value_ref, ...), custom_call_target="tpu_custom_call" | custom-call | flops 4294967296 | bytes 16777216 | tf_op jit(solution)/shard_map/pallas_call | solution.py:112
  266.1 11.5 fusion.543
  281.2 10.7 multiply_reduce_fusion.6
  295.7 9.2 all-to-all-done.5
  305.9 20.0 %shard_map.337 = (bf16[512,2048]{1,0:T(8,128)(2,1)S(1)}, bf16[512,2048]{1,0:T(8,128)(2,1)S(1)}, bf16[512,2048]{1,0:T(8,128)(2,1)S(1)}, bf16[512,2048]{1,0:T(8,12...) custom-call(s32[2816]{0:T(1024)S(1)} %reshape.1997.place_ref, ...), custom_call_target="tpu_custom_call" | custom-call | tf_op jit(solution)/shard_map/pallas_call | solution.py:573
  353.2 12.9 %shard_map.339 = (bf16[512,512]{1,0:T(8,128)(2,1)S(1)}, f32[512,512]{1,0:T(8,128)S(1)}) custom-call(s32[2]{0:T(128)S(1)} %bitcast.511, bf16[512,512]{1,0:T(8,128)(2,1)S(1)} %convolution_convert_fusion.29.query_ref, bf16[2048,1024]{1,0:T(8,128)(2,1)S(1)} %convolution_convert_fusion.2.key_ref.value_ref, ...), custom_call_target="tpu_custom_call" | custom-call | flops 1073741824 | bytes 10485760 | tf_op jit(solution)/shard_map/pallas_call | solution.py:112
  388.1 13.1 %shard_map.341 = (bf16[512,512]{1,0:T(8,128)(2,1)S(1)}, f32[512,512]{1,0:T(8,128)S(1)}) custom-call(s32[2]{0:T(128)S(1)} %bitcast.512, bf16[512,512]{1,0:T(8,128)(2,1)S(1)} %convolution_convert_fusion.28.query_ref, bf16[2048,1024]{1,0:T(8,128)(2,1)S(1)} %convolution_convert_fusion.1.key_ref.value_ref, ...), custom_call_target="tpu_custom_call" | custom-call | flops 1073741824 | bytes 10485760 | tf_op jit(solution)/shard_map/pallas_call | solution.py:112
  472.0 9.8 all-to-all-done.8
  499.9 19.8 %shard_map.342 = (bf16[512,512]{1,0:T(8,128)(2,1)S(1)}, bf16[2048,512]{1,0:T(8,128)(2,1)S(1)}, bf16[2048,512]{1,0:T(8,128)(2,1)S(1)}) custom-call(s32[2]{0:T(128)S(1)} %bitcast.513, bf16[512,512]{1,0:T(8,128)(2,1)S(1)} %convolution_convert_fusion.28.query_ref, bf16[2048,1024]{1,0:T(8,128)(2,1)S(1)} %copy-done.7, bf16[2048,1024]{1,0:T(8,128)(2,1)S(1)} %copy-done.7, ...), custom_call_target="tpu_custom_call" | custom-call | flops 2684354560 | bytes 20971520 | tf_op jit(solution)/shard_map/pallas_call | solution.py:188
  552.7 19.8 %shard_map.344 = (bf16[512,512]{1,0:T(8,128)(2,1)S(1)}, bf16[2048,512]{1,0:T(8,128)(2,1)S(1)}, bf16[2048,512]{1,0:T(8,128)(2,1)S(1)}) custom-call(s32[2]{0:T(128)S(1)} %bitcast.514, bf16[512,512]{1,0:T(8,128)(2,1)S(1)} %convolution_convert_fusion.29.query_ref, bf16[2048,1024]{1,0:T(8,128)(2,1)S(1)} %copy-done.5, bf16[2048,1024]{1,0:T(8,128)(2,1)S(1)} %copy-done.5, ...), custom_call_target="tpu_custom_call" | custom-call | flops 2684354560 | bytes 20971520 | tf_op jit(solution)/shard_map/pallas_call | solution.py:188
  590.3 17.6 %fusion.161 = bf16[2048,2048]{1,0:T(8,128)(2,1)} fusion(f32[2048,2048]{1,0:T(8,128)} %fusion.543, bf16[512,2048]{1,0:T(8,128)(2,1)} %get-tuple-element.848, f32[2048,512]{1,0:T(8,128)S(1)} %add_add_fusion.2), kind=kOutput, calls=%fused_computation.250 | convolution fusion | flops 4379901952 | bytes 31457280 | tf_op jit(solution)/shard_map/dot_general | solution.py:52
  607.9 11.6 convolution_convert_fusion.11.refs_7_
  659.0 10.1 convolution_convert_fusion.14.refs_4_
  669.1 20.1 %shard_map.346 = (bf16[2176,32,128]{2,1,0:T(8,128)(2,1)}, bf16[640,32,128]{2,1,0:T(8,128)(2,1)S(1)}) custom-call(s32[2816]{0:T(1024)S(1)} %copy-done.186, bf16[512,2048]{1,0:T(8,128)(2,1)S(1)} %pad_maximum_fusion.3.refs_0_, bf16[512,2048]{1,0:T(8,128)(2,1)S(1)} %pad_maximum_fusion.4.refs_1_, bf16[512,2048]{1,0:T(8,128)(2,1)S(1)} %pad_maximum_fusion.5.refs_2_, ...), custom_call_target="tpu_custom_call" | custom-call | tf_op jit(solution)/shard_map/pallas_call | solution.py:654
  689.3 10.0 multiply_reduce_fusion.3
  750.5 34.3 %shard_map.347 = (bf16[2048,512]{1,0:T(8,128)(2,1)S(1)}, bf16[2048,512]{1,0:T(8,128)(2,1)S(1)}, bf16[2048,512]{1,0:T(8,128)(2,1)S(1)}) custom-call(s32[2]{0:T(128)S(1)} %bitcast.515, bf16[2048,1536]{1,0:T(8,128)(2,1)} %copy-done.1, bf16[2048,1536]{1,0:T(8,128)(2,1)} %copy-done.1, bf16[2048,1536]{1,0:T(8,128)(2,1)} %copy-done.1, f32[2048,512]{1,0:T(8,128)S(1)} %copy-done.11, ...), custom_call_target="tpu_custom_call" | custom-call | flops 5368709120 | bytes 16777216 | tf_op jit(solution)/shard_map/pallas_call | solution.py:188
  784.9 10.1 fusion.154
  811.2 34.5 %shard_map.348 = (bf16[2048,512]{1,0:T(8,128)(2,1)S(1)}, bf16[2048,512]{1,0:T(8,128)(2,1)S(1)}, bf16[2048,512]{1,0:T(8,128)(2,1)S(1)}) custom-call(s32[2]{0:T(128)S(1)} %bitcast.516, bf16[2048,1536]{1,0:T(8,128)(2,1)} %copy-done.1, bf16[2048,1536]{1,0:T(8,128)(2,1)} %copy-done.1, ...), custom_call_target="tpu_custom_call", output_to_operand_aliasing={{0}: (6, {}), {1}: (7, {}), {2}: (8, {})} | custom-call | flops 5368709120 | bytes 16777216 | tf_op jit(solution)/shard_map/pallas_call | solution.py:188
  875.1 26.4 %collective-permute-done.18 = bf16[88,32,128]{2,1,0:T(8,128)(2,1)S(1)} collective-permute-done((bf16[88,32,128]{2,1,0:T(8,128)(2,1)S(1)}, bf16[88,32,128]{2,1,0:T(8,128)(2,1)S(1)}, u32[]{:S(2)}, u32[]{:S(2)}) %collective-permute-start.18) | collective-permute-done | bytes 720928 | tf_op jit(solution)/shard_map/ppermute | solution.py:705
  915.4 8.8 collective-permute-done.21
  940.5 17.2 %shard_map.350 = bf16[4096,512]{1,0:T(8,128)(2,1)S(1)} custom-call(s32[4096]{0:T(1024)S(1)} %max.34.index_ref, f32[2560,512]{1,0:T(8,128)S(1)} %maximum_multiply_fusion.source_ref), custom_call_target="tpu_custom_call" | custom-call | tf_op jit(solution)/shard_map/pallas_call | solution.py:754
  1053.1 35.8 %all-to-all-done.11 = bf16[32,128,512]{2,1,0:T(8,128)(2,1)} async-done(((bf16[32,128,512]{2,1,0:T(8,128)(2,1)}), bf16[32,128,512]{2,1,0:T(8,128)(2,1)}, u32[]{:S(2)}, u32[]{:S(2)}) %all-to-all-start.11) | async-done | bytes 4194336 | tf_op jit(solution)/shard_map/all_to_all | solution.py:915
  1088.9 9.4 shard_map.352
  1151.8 27.8 %shard_map.353 = f32[64,64,256]{2,1,0:T(8,128)S(1)} custom-call(f32[64,64,256]{2,1,0:T(8,128)S(1)} %pad.20.in_ref), custom_call_target="tpu_custom_call" | custom-call | tf_op jit(solution)/shard_map/pallas_call | solution.py:971
  1228.0 22.8 %fusion.545 = (bf16[4096,512]{1,0:T(8,128)(2,1)}, f32[4096,512]{1,0:T(8,128)}, f32[4096,512]{1,0:T(8,128)}, f32[4096,512]{1,0:T(8,128)}) fusion(f32[4096,512]{1,0:T(8,128)} %get-tuple-element.1699, f32[]{:T(128)S(6)} %min.3, bf16[4096,512]{1,0:T(8,128)(2,1)} %all-gather.14.cloned.1.call-done, f32[4096,512]{1,0:T(8,128)} %param.38, f32[4096,512]{1,0:T(8,128)} %param.39), kind=kLoop, calls=%fused_computation.1099 | loop fusion | flops 37748736 | bytes 58720260 | tf_op jit(solution)/shard_map/convert_element_type | solution.py:1406
  (1037 shorter events, 660.0 us)
Async XLA Ops:
  7.2 163.4 %all-gather.8.cloned.1.call-start = ((), (), s32[]{:S(2)}) async-start(), calls=%async_computation.14 | async-start | bytes 11894784 | tf_op jit(solution)/shard_map/all_gather | solution.py:1143
  34.4 20.0 %all-to-all-start.3 = ((s32[32,1,2688]{2,1,0:T(1,128)}), s32[32,1,2688]{2,1,0:T(1,128)S(1)}, u32[]{:S(2)}, u32[]{:S(2)}) async-start(s32[32,1,2688]{2,1,0:T(1,128)} %broadcast_in_dim.479), calls=%async_computation.3 | async-start | bytes 688128 | tf_op jit(solution)/shard_map/all_to_all | solution.py:803
  79.5 91.2 %all-to-all-start.4 = ((bf16[8,336,512]{2,1,0:T(8,128)(2,1)}), bf16[8,336,512]{2,1,0:T(8,128)(2,1)}, u32[]{:S(2)}, u32[]{:S(2)}) async-start(bf16[8,336,512]{2,1,0:T(8,128)(2,1)} %bitcast.58), calls=%async_computation.4 | async-start | bytes 5505024 | tf_op jit(solution)/shard_map/all_to_all | solution.py:883
  183.9 121.0 %all-gather.10.cloned.1.call-start = ((), (), s32[]{:S(2)}) async-start(), calls=%async_computation.15 | async-start | bytes 11894784 | tf_op jit(solution)/shard_map/all_gather | solution.py:1166
  277.7 27.3 %all-to-all-start.5 = ((bf16[8,112,512]{2,1,0:T(8,128)(2,1)}), bf16[8,112,512]{2,1,0:T(8,128)(2,1)S(1)}, u32[]{:S(2)}, u32[]{:S(2)}) async-start(bf16[8,112,512]{2,1,0:T(8,128)(2,1)} %bitcast.67), calls=%async_computation.5 | async-start | bytes 1835008 | tf_op jit(solution)/shard_map/all_to_all | solution.py:883
  412.8 18.8 %all-to-all-start.6 = ((bf16[8,64,512]{2,1,0:T(8,128)(2,1)}), bf16[8,64,512]{2,1,0:T(8,128)(2,1)S(1)}, u32[]{:S(2)}, u32[]{:S(2)}) async-start(bf16[8,64,512]{2,1,0:T(8,128)(2,1)} %broadcast_in_dim.499), calls=%async_computation.6 | async-start | bytes 1048576 | tf_op jit(solution)/shard_map/all_to_all | solution.py:803
  440.4 13.8 %all-to-all-start.7 = ((f32[32,3,512]{2,1,0:T(4,128)}), f32[32,3,512]{2,1,0:T(4,128)S(1)}, u32[]{:S(2)}, u32[]{:S(2)}) async-start(f32[32,3,512]{2,1,0:T(4,128)} %broadcast_in_dim.501), calls=%async_computation.7 | async-start | bytes 524288 | tf_op jit(solution)/shard_map/all_to_all | solution.py:803
  462.9 18.9 %all-to-all-start.8 = ((bf16[8,64,512]{2,1,0:T(8,128)(2,1)}), bf16[8,64,512]{2,1,0:T(8,128)(2,1)S(1)}, u32[]{:S(2)}, u32[]{:S(2)}) async-start(bf16[8,64,512]{2,1,0:T(8,128)(2,1)} %bitcast.610), calls=%async_computation.8 | async-start | bytes 1048576 | tf_op jit(solution)/shard_map/all_to_all | solution.py:1244
  466.6 235.5 %all-gather.12.cloned.1.call-start = ((), (), s32[]{:S(2)}) async-start(), calls=%async_computation.16 | async-start | bytes 2162688 | tf_op jit(solution)/shard_map/all_gather | solution.py:1211
  717.7 67.2 %collective-permute-start.13 = (bf16[1088,32,128]{2,1,0:T(8,128)(2,1)}, bf16[1088,32,128]{2,1,0:T(8,128)(2,1)}, u32[]{:S(2)}, u32[]{:S(2)}) collective-permute-start(bf16[1088,32,128]{2,1,0:T(8,128)(2,1)} %dynamic-slice_bitcast_fusion.13), channel_id=1, source_target_pairs={{0,1},{1,0},{2,3},{3,2},{4,5},{5,4},{6,7},{7,6},{8,9},{9,8},{10,11... | collective-permute-start | bytes 26738696 | tf_op jit(solution)/shard_map/ppermute | solution.py:705
  722.7 9.8 all-to-all-start.9
  733.2 10.2 all-to-all-start.10
  805.2 41.2 %collective-permute-start.16 = (bf16[176,32,128]{2,1,0:T(8,128)(2,1)}, bf16[176,32,128]{2,1,0:T(8,128)(2,1)}, u32[]{:S(2)}, u32[]{:S(2)}) collective-permute-start(bf16[176,32,128]{2,1,0:T(8,128)(2,1)} %dynamic-slice_bitcast_fusion.16), channel_id=1, source_target_pairs={{0,2},{1,3},{2,0},{3,1},{4,6},{5,7},{6,4},{7,5},{8,10},{9,11},{10,... | collective-permute-start | bytes 4325384 | tf_op jit(solution)/shard_map/ppermute | solution.py:705
  808.6 41.9 %collective-permute-start.15 = (bf16[176,32,128]{2,1,0:T(8,128)(2,1)}, bf16[176,32,128]{2,1,0:T(8,128)(2,1)S(1)}, u32[]{:S(2)}, u32[]{:S(2)}) collective-permute-start(bf16[176,32,128]{2,1,0:T(8,128)(2,1)} %dynamic-slice_bitcast_fusion.17), channel_id=1, source_target_pairs={{0,16},{1,17},{2,18},{3,19},{4,20},{5,21},{6,22},{7,23},{8,24},{9,... | collective-permute-start | bytes 4325384 | tf_op jit(solution)/shard_map/ppermute | solution.py:705
  810.7 41.3 %collective-permute-start.14 = (bf16[192,32,128]{2,1,0:T(8,128)(2,1)}, bf16[192,32,128]{2,1,0:T(8,128)(2,1)S(1)}, u32[]{:S(2)}, u32[]{:S(2)}) collective-permute-start(bf16[192,32,128]{2,1,0:T(8,128)(2,1)} %dynamic-slice_bitcast_fusion.15), channel_id=1, source_target_pairs={{0,8},{1,9},{2,10},{3,11},{4,12},{5,13},{6,14},{7,15},{8,0},{9,1},... | collective-permute-start | bytes 4718600 | tf_op jit(solution)/shard_map/ppermute | solution.py:705
  869.4 62.5 %collective-permute-start.23 = (bf16[320,32,128]{2,1,0:T(8,128)(2,1)}, bf16[320,32,128]{2,1,0:T(8,128)(2,1)}, u32[]{:S(2)}, u32[]{:S(2)}) collective-permute-start(bf16[320,32,128]{2,1,0:T(8,128)(2,1)} %dynamic-slice_bitcast_fusion.14), channel_id=1, source_target_pairs={{0,1},{1,0},{2,3},{3,2},{4,5},{5,4},{6,7},{7,6},{8,9},{9,8},{10,11... | collective-permute-start | bytes 7864328 | tf_op jit(solution)/shard_map/ppermute | solution.py:705
  869.5 34.9 %collective-permute-start.19 = (bf16[88,32,128]{2,1,0:T(8,128)(2,1)S(1)}, bf16[88,32,128]{2,1,0:T(8,128)(2,1)S(1)}, u32[]{:S(2)}, u32[]{:S(2)}) collective-permute-start(bf16[88,32,128]{2,1,0:T(8,128)(2,1)S(1)} %dynamic-slice_bitcast_fusion.19), channel_id=1, source_target_pairs={{0,4},{1,5},{2,6},{3,7},{4,0},{5,1},{6,2},{7,3},{8,12},{9,13},{10,... | collective-permute-start | bytes 2162696 | tf_op jit(solution)/shard_map/ppermute | solution.py:705
  870.2 31.3 %collective-permute-start.18 = (bf16[88,32,128]{2,1,0:T(8,128)(2,1)S(1)}, bf16[88,32,128]{2,1,0:T(8,128)(2,1)S(1)}, u32[]{:S(2)}, u32[]{:S(2)}) collective-permute-start(bf16[88,32,128]{2,1,0:T(8,128)(2,1)S(1)} %dynamic-slice_bitcast_fusion.20), channel_id=1, source_target_pairs={{0,2},{1,3},{2,0},{3,1},{4,6},{5,7},{6,4},{7,5},{8,10},{9,11},{10,... | collective-permute-start | bytes 2162696 | tf_op jit(solution)/shard_map/ppermute | solution.py:705
  871.3 33.2 %collective-permute-start.17 = (bf16[96,32,128]{2,1,0:T(8,128)(2,1)S(1)}, bf16[96,32,128]{2,1,0:T(8,128)(2,1)S(1)}, u32[]{:S(2)}, u32[]{:S(2)}) collective-permute-start(bf16[96,32,128]{2,1,0:T(8,128)(2,1)S(1)} %dynamic-slice_bitcast_fusion.18), channel_id=1, source_target_pairs={{0,16},{1,17},{2,18},{3,19},{4,20},{5,21},{6,22},{7,23},{8,24},{9,... | collective-permute-start | bytes 2359304 | tf_op jit(solution)/shard_map/ppermute | solution.py:705
  904.8 10.5 collective-permute-start.22
  906.4 17.9 %collective-permute-start.21 = (bf16[44,32,128]{2,1,0:T(8,128)(2,1)S(1)}, bf16[44,32,128]{2,1,0:T(8,128)(2,1)S(1)}, u32[]{:S(2)}, u32[]{:S(2)}) collective-permute-start(bf16[44,32,128]{2,1,0:T(8,128)(2,1)S(1)} %dynamic-slice_bitcast_fusion.26), channel_id=1, source_target_pairs={{0,4},{1,5},{2,6},{3,7},{4,0},{5,1},{6,2},{7,3},{8,12},{9,13},{10,... | collective-permute-start | bytes 1081352 | tf_op jit(solution)/shard_map/ppermute | solution.py:705
  907.3 18.0 %collective-permute-start.20 = (bf16[48,32,128]{2,1,0:T(8,128)(2,1)S(1)}, bf16[48,32,128]{2,1,0:T(8,128)(2,1)S(1)}, u32[]{:S(2)}, u32[]{:S(2)}) collective-permute-start(bf16[48,32,128]{2,1,0:T(8,128)(2,1)S(1)} %dynamic-slice_bitcast_fusion.24), channel_id=1, source_target_pairs={{0,2},{1,3},{2,0},{3,1},{4,6},{5,7},{6,4},{7,5},{8,10},{9,11},{10,... | collective-permute-start | bytes 1179656 | tf_op jit(solution)/shard_map/ppermute | solution.py:705
  926.1 10.1 collective-permute-start.24
  934.7 23.0 %collective-permute-start.31 = (bf16[48,32,128]{2,1,0:T(8,128)(2,1)S(1)}, bf16[48,32,128]{2,1,0:T(8,128)(2,1)S(1)}, u32[]{:S(2)}, u32[]{:S(2)}) collective-permute-start(bf16[48,32,128]{2,1,0:T(8,128)(2,1)S(1)} %dynamic-slice_bitcast_fusion.23), channel_id=1, source_target_pairs={{0,16},{1,17},{2,18},{3,19},{4,20},{5,21},{6,22},{7,23},{8,24},{9,... | collective-permute-start | bytes 1179656 | tf_op jit(solution)/shard_map/ppermute | solution.py:705
  937.5 21.1 %collective-permute-start.35 = (bf16[48,32,128]{2,1,0:T(8,128)(2,1)S(1)}, bf16[48,32,128]{2,1,0:T(8,128)(2,1)S(1)}, u32[]{:S(2)}, u32[]{:S(2)}) collective-permute-start(bf16[48,32,128]{2,1,0:T(8,128)(2,1)S(1)} %dynamic-slice_bitcast_fusion.22), channel_id=1, source_target_pairs={{0,2},{1,3},{2,0},{3,1},{4,6},{5,7},{6,4},{7,5},{8,10},{9,11},{10,... | collective-permute-start | bytes 1179656 | tf_op jit(solution)/shard_map/ppermute | solution.py:705
  939.0 22.6 %collective-permute-start.27 = (bf16[64,32,128]{2,1,0:T(8,128)(2,1)S(1)}, bf16[64,32,128]{2,1,0:T(8,128)(2,1)S(1)}, u32[]{:S(2)}, u32[]{:S(2)}) collective-permute-start(bf16[64,32,128]{2,1,0:T(8,128)(2,1)S(1)} %dynamic-slice_bitcast_fusion.21), channel_id=1, source_target_pairs={{0,8},{1,9},{2,10},{3,11},{4,12},{5,13},{6,14},{7,15},{8,0},{9,1},... | collective-permute-start | bytes 1572872 | tf_op jit(solution)/shard_map/ppermute | solution.py:705
  958.7 13.5 %collective-permute-start.36 = (bf16[24,32,128]{2,1,0:T(8,128)(2,1)S(1)}, bf16[24,32,128]{2,1,0:T(8,128)(2,1)S(1)}, u32[]{:S(2)}, u32[]{:S(2)}) collective-permute-start(bf16[24,32,128]{2,1,0:T(8,128)(2,1)S(1)} %dynamic-slice_bitcast_fusion.28), channel_id=1, source_target_pairs={{0,4},{1,5},{2,6},{3,7},{4,0},{5,1},{6,2},{7,3},{8,12},{9,13},{10,... | collective-permute-start | bytes 589832 | tf_op jit(solution)/shard_map/ppermute | solution.py:705
  961.7 16.6 %collective-permute-start.28 = (bf16[32,32,128]{2,1,0:T(8,128)(2,1)S(1)}, bf16[32,32,128]{2,1,0:T(8,128)(2,1)S(1)}, u32[]{:S(2)}, u32[]{:S(2)}) collective-permute-start(bf16[32,32,128]{2,1,0:T(8,128)(2,1)S(1)} %dynamic-slice_bitcast_fusion.27), channel_id=1, source_target_pairs={{0,16},{1,17},{2,18},{3,19},{4,20},{5,21},{6,22},{7,23},{8,24},{9,... | collective-permute-start | bytes 786440 | tf_op jit(solution)/shard_map/ppermute | solution.py:705
  964.7 8.6 collective-permute-start.33
  990.2 98.7 %all-to-all-start.11 = ((bf16[32,128,512]{2,1,0:T(8,128)(2,1)}), bf16[32,128,512]{2,1,0:T(8,128)(2,1)}, u32[]{:S(2)}, u32[]{:S(2)}) async-start(bf16[32,128,512]{2,1,0:T(8,128)(2,1)} %bitcast.506), calls=%async_computation.11 | async-start | bytes 8388608 | tf_op jit(solution)/shard_map/all_to_all | solution.py:915
  993.8 234.2 %all-gather.14.cloned.1.call-start = ((), (), s32[]{:S(2)}) async-start(), calls=%async_computation.17 | async-start | bytes 5242880 | tf_op jit(solution)/shard_map/all_gather | solution.py:1367
  1104.8 39.6 %all-to-all-start.12 = ((f32[32,5,128]{2,1,0:T(8,128)}), f32[32,5,128]{2,1,0:T(8,128)S(1)}, u32[]{:S(2)}, u32[]{:S(2)}) async-start(f32[32,5,128]{2,1,0:T(8,128)} %broadcast_in_dim.518), calls=%async_computation.12 | async-start | bytes 262144 | tf_op jit(solution)/shard_map/all_to_all | solution.py:803
  (266 other events, 1979.9 us)
Sparse Core Ops, SparseCore 0:
  20.4 116.2 all-gather.7
  188.1 90.5 all-gather.9
  471.6 56.2 all-gather.11
  1102.8 50.5 all-gather.13

commit v6 on v4

--- a/solution.py
+++ b/solution.py
@@ -978,13 +978,14 @@
     )(columns)
 
 
-def renew_bases(left_moved, right_moved):
-    moved = jnp.concatenate([left_moved, right_moved], 0)
-    count = moved.shape[0]
-    whole = -(-count // 128) * 128
-    columns = jnp.pad(jnp.transpose(moved, (2, 1, 0)), ((0, 0), (0, 0), (0, whole - count)))
-    renewed = jnp.transpose(orthonormal(columns)[:, :, :count], (2, 1, 0))
-    return (renewed[: count // 2], renewed[count // 2 :])
+def as_columns(left, right):
+    both = jnp.transpose(jnp.concatenate([left, right], 0), (2, 1, 0))
+    return jnp.pad(both, ((0, 0), (0, 0), (0, -both.shape[2] % 128)))
+
+
+def renew_bases(columns, count):
+    renewed = jnp.transpose(orthonormal(columns)[:, :, : 2 * count], (2, 1, 0))
+    return (renewed[:count], renewed[count:])
 
 
 def turned_by(stat, basis):
@@ -997,8 +998,8 @@
     grad_turned,
     left_outer,
     right_outer,
-    left_moves,
-    right_moves,
+    columns_before,
+    columns_change,
     first_mom,
     first_turned,
     second_mom,
@@ -1029,10 +1030,8 @@
         left_new,
         right_new,
         *renew_bases(
-            *(
-                BETA_STAT * before + (1 - BETA_STAT) * (factor * (factor * change))
-                for before, change in (left_moves, right_moves)
-            )
+            BETA_STAT * columns_before + (1 - BETA_STAT) * (factor * (factor * columns_change)),
+            master.shape[0],
         ),
     )
 
@@ -1150,6 +1149,7 @@
         first_turned,
         target_sent,
         place_of,
+        wave_set,
     ) = lax.optimization_barrier(
         (
             own_folded[first_size:],
@@ -1159,6 +1159,7 @@
             turn_in(left_later, mom1_later, right_later),
             target_sent,
             place_of,
+            waves(src_count, D),
         )
     )
     second_tiles = lax.all_gather(own_second, ("dp", "vocab"), axis=0, tiled=True)
@@ -1185,8 +1186,6 @@
         for mat_no, matrix in zip(decoder_mats, decoder_set):
             weights[mat_no] = matrix
         return (held, with_waves(target_finish(arrived), tgt_count))
-
-    wave_set = waves(src_count, D)
 
     def with_waves(rows, length):
         return rows * math.sqrt(D) + jnp.tile(wave_set[:length], (MICRO, 1))
@@ -1309,9 +1308,7 @@
 
     def ready(rows):
         sums = other_exchanges(held["parts"], soon_plan, devices, held["done"])
-        rows, sums, late, held["gains"] = lax.optimization_barrier(
-            (rows, sums, late_sum, gain_flat)
-        )
+        rows, sums, late = lax.optimization_barrier((rows, sums, late_sum))
         sums = lax.cond(jnp.min(soon_count) < soon_size, exchange_again, lambda: sums)
         owned_grad = unfold_ranked(
             jnp.concatenate([sums, late], 0),
@@ -1319,24 +1316,21 @@
         )
         left_outer = jnp.einsum("tik,tjk->tij", owned_grad, owned_grad, precision=HIGH)
         right_outer = jnp.einsum("tki,tkj->tij", owned_grad, owned_grad, precision=HIGH)
-        gain_part = jnp.sum(
-            lax.all_to_all(held["gains"], ("dp", "vocab"), 0, 0, tiled=True), axis=0
-        )
-        gain_total = spread(gain_part[None], ("dp", "vocab"), devices)
         held["owned"] = (
             owned_grad,
             turn_in(basis_left, owned_grad, basis_right),
             left_outer,
             right_outer,
-            (turned_by(stat_left, basis_left), turned_by(left_outer, basis_left)),
-            (turned_by(stat_right, basis_right), turned_by(right_outer, basis_right)),
+            as_columns(turned_by(stat_left, basis_left), turned_by(stat_right, basis_right)),
+            as_columns(turned_by(left_outer, basis_left), turned_by(right_outer, basis_right)),
             jnp.sum(owned_grad * owned_grad),
-            gain_total.reshape(-1)[: GAINS * D].reshape(GAINS, D),
         )
         return rows
 
     def landed(arrived):
-        arrived, held["owned"] = lax.optimization_barrier((arrived, held["owned"]))
+        arrived, held["owned"], held["gains"] = lax.optimization_barrier(
+            (arrived, held["owned"], gain_flat)
+        )
         return arrived
 
     grad_quarter = return_rows(
@@ -1348,15 +1342,18 @@
         owned_turned,
         left_outer,
         right_outer,
-        left_moves,
-        right_moves,
+        columns_before,
+        columns_change,
         owned_squares,
-        gain_total,
     ) = held["owned"]
     squares = owned_squares + jnp.sum(grad_quarter * grad_quarter)
-    square_total = jnp.sum(
-        spread(jnp.full((1, 128), squares), ("dp", "vocab"), devices)[:, 0, 0]
-    )
+    gain_part = jnp.sum(
+        lax.all_to_all(held["gains"], ("dp", "vocab"), 0, 0, tiled=True), axis=0
+    )
+    last_facts = jnp.concatenate([gain_part.reshape(-1, 128), jnp.full((1, 128), squares)], 0)
+    last_facts = spread(last_facts, ("dp", "vocab"), devices).reshape(devices, -1, 128)
+    square_total = jnp.sum(last_facts[:, -1, 0])
+    gain_total = last_facts[:, :-1].reshape(-1)[: GAINS * D].reshape(GAINS, D)
     grad_norm = jnp.sqrt(square_total + jnp.sum(gain_total * gain_total))
     factor = jnp.minimum(1.0, CLIP_AT / grad_norm)
     table_grad = lax.all_gather(
@@ -1368,8 +1365,8 @@
         owned_turned,
         left_outer,
         right_outer,
-        left_moves,
-        right_moves,
+        columns_before,
+        columns_change,
         mom1_tiles,
         first_turned,
         mom2_tiles,

time: 1270 us -> 1250 us (0.984)
  waiting for transfers between devices: 183 us -> 159 us
  blocking collectives: 19.2 us -> 0 us
    optimization_barrier x9 -> x0, local copies, waits for them, and re-layouts: 35.1 us -> none  [the longest x8 31.8 us: landed(): arrived, held['owned'] = lax.optimization_barrier((arrived, held['owned']))]
    all_to_all x1, waiting for transfers between devices: 35.8 us -> 2.76 us  [swap_all(): return lax.all_to_all(rows, ('dp', 'vocab'), 0, 0, tiled=True)]
    all_to_all x2 -> x0, blocking collectives: 19.2 us -> none  [the longest x1 10.2 us: ready(): lax.all_to_all(held['gains'], ('dp', 'vocab'), 0, 0, tiled=True)]
    unnamed x559 -> x547, local copies, waits for them, and re-layouts: 98.8 us -> 114 us
    dot_general x1 -> x4, local copies, waits for them, and re-layouts: 3.3 us -> 18.4 us  [turned_by(): return jnp.einsum('tij,tjk->tik', stat, basis, precision=HIGH)]
  transfers between devices with their start and end apart: 38 -> 39, of which waited for: 19 -> 20; matrix products, arithmetic and copies ran while one was open for 33% -> 34% of each run, Pallas kernels for 22% -> 23%
where the time goes in v6:
time: 1250 us; the launch traced here: 1230 us
  Pallas kernels  368 us (29%)
  matrix products  256 us (20%)
  local copies, waits for them, and re-layouts  205 us (16%)
  waiting for transfers between devices  159 us (13%)
  other arithmetic  149 us (12%)
  starting transfers between devices  61.5 us (5%)
  between operations  25.4 us (2%)
    pallas_call x6, Pallas kernels, attend_backward(): pl.pallas_call(kernel, out_shape=(jax.ShapeDtypeStruct((MICRO * rows, D),...  124 us
    unnamed x547, local copies, waits for them, and re-layouts  114 us
    pallas_call x5, Pallas kernels, attend_forward(): pl.pallas_call(kernel, out_shape=(jax.ShapeDtypeStruct((MICRO * rows, D),...  84.3 us
    dot_general x19, matrix products, linear(): return jnp.dot(left_op, right_op, preferred_element_type=jnp.float32)  73.6 us
    dot_general x23, matrix products, outer_sum(): lax.dot_general(left_op, right_op, (((0,), (0,)), ((), ())), preferred_el...  68.4 us
    ppermute x26, waiting for transfers between devices, halve(): arrived = lax.ppermute(sent, ('dp', 'vocab'), pairs)  65.7 us
    dot_general x19, matrix products, linear_tr(): lax.dot_general(left_op, right_op, (((1,), (1,)), ((), ())), preferred_el...  58.8 us
    pallas_call x5, Pallas kernels, take_rows(): pl.pallas_call(kernel, out_shape=jax.ShapeDtypeStruct((whole, width), kin...  56.6 us
  transfers between devices with their start and end apart: 39, of which 20 were waited for; matrix products, arithmetic and copies ran while one was open for 34% of the time, Pallas kernels for 23%

profile of v6, /device:TPU:0, one launch (start us, length us, event | category | flops | bytes accessed | tf_op | source)
XLA Modules:
  0.0 1234.2 jit_solution(4092707347908120039)
XLA Ops:
  49.0 17.1 %all-to-all-done.3 = s32[32,1,2688]{2,1,0:T(1,128)S(1)} async-done(((s32[32,1,2688]{2,1,0:T(1,128)}), s32[32,1,2688]{2,1,0:T(1,128)S(1)}, u32[]{:S(2)}, u32[]{:S(2)}) %all-to-all-start.3) | async-done | bytes 344096 | tf_op jit(solution)/shard_map/all_to_all | solution.py:803
  71.0 16.6 %shard_map.332 = bf16[2688,512]{1,0:T(8,128)(2,1)} custom-call(s32[2688]{0:T(1024)S(1)} %max.32.index_ref, f32[4096,512]{1,0:T(8,128)} %source_ref.3), custom_call_target="tpu_custom_call" | custom-call | tf_op jit(solution)/shard_map/pallas_call | solution.py:754
  119.0 8.6 shard_map.333
  139.2 34.2 %all-to-all-done.4 = bf16[8,336,512]{2,1,0:T(8,128)(2,1)} async-done(((bf16[8,336,512]{2,1,0:T(8,128)(2,1)}), bf16[8,336,512]{2,1,0:T(8,128)(2,1)}, u32[]{:S(2)}, u32[]{:S(2)}) %all-to-all-start.4) | async-done | bytes 2752544 | tf_op jit(solution)/shard_map/all_to_all | solution.py:883
  173.4 22.7 %conditional.2 = (bf16[512,2048]{1,0:T(8,128)(2,1)}, bf16[512,2048]{1,0:T(8,128)(2,1)S(1)}, bf16[512,2048]{1,0:T(8,128)(2,1)S(1)}, bf16[512,2048]{1,0:T(8,128)(2,1)}, bf16[512,2048]{1,0:T(8,128)(2,1)}) conditional(s32[]{:T(128)} %convert_element_type.1091, (s32[2816]{0:T(1024)S(1)}, bf16[1408,32,128]{2,1,0:T(8,128)(2,1)}) %tuple.99, ...), branch_computations={%region_26.27_spmd, %region_27.28_spmd} | conditional | bytes 90210416 | solution.py:1176
  182.8 10.0 branch_0_fun.1
  207.2 10.7 shard_map.334
  228.7 46.6 %shard_map.335 = (bf16[2048,512]{1,0:T(8,128)(2,1)S(1)}, f32[2048,512]{1,0:T(8,128)S(1)}) custom-call(s32[2]{0:T(128)S(1)} %bitcast.509, bf16[2048,1536]{1,0:T(8,128)(2,1)S(1)} %convolution_convert_fusion.query_ref.key_ref.value_ref, bf16[2048,1536]{1,0:T(8,128)(2,1)S(1)} %convolution_convert_fusion.query_ref.key_ref.value_ref, ...), custom_call_target="tpu_custom_call" | custom-call | flops 4294967296 | bytes 16777216 | tf_op jit(solution)/shard_map/pallas_call | solution.py:112
  278.1 11.5 fusion.561
  293.5 10.7 multiply_reduce_fusion.6
  308.0 9.2 all-to-all-done.5
  317.4 20.1 %shard_map.337 = (bf16[512,2048]{1,0:T(8,128)(2,1)S(1)}, bf16[512,2048]{1,0:T(8,128)(2,1)S(1)}, bf16[512,2048]{1,0:T(8,128)(2,1)S(1)}, bf16[512,2048]{1,0:T(8,12...) custom-call(s32[2816]{0:T(1024)S(1)} %reshape.1993.place_ref, ...), custom_call_target="tpu_custom_call" | custom-call | tf_op jit(solution)/shard_map/pallas_call | solution.py:573
  364.1 12.9 %shard_map.339 = (bf16[512,512]{1,0:T(8,128)(2,1)S(1)}, f32[512,512]{1,0:T(8,128)S(1)}) custom-call(s32[2]{0:T(128)S(1)} %bitcast.510, bf16[512,512]{1,0:T(8,128)(2,1)S(1)} %convolution_convert_fusion.29.query_ref, bf16[2048,1024]{1,0:T(8,128)(2,1)S(1)} %convolution_convert_fusion.2.key_ref.value_ref, ...), custom_call_target="tpu_custom_call" | custom-call | flops 1073741824 | bytes 10485760 | tf_op jit(solution)/shard_map/pallas_call | solution.py:112
  395.1 13.1 %shard_map.341 = (bf16[512,512]{1,0:T(8,128)(2,1)S(1)}, f32[512,512]{1,0:T(8,128)S(1)}) custom-call(s32[2]{0:T(128)S(1)} %bitcast.511, bf16[512,512]{1,0:T(8,128)(2,1)S(1)} %convolution_convert_fusion.28.query_ref, bf16[2048,1024]{1,0:T(8,128)(2,1)S(1)} %convolution_convert_fusion.1.key_ref.value_ref, ...), custom_call_target="tpu_custom_call" | custom-call | flops 1073741824 | bytes 10485760 | tf_op jit(solution)/shard_map/pallas_call | solution.py:112
  467.0 8.0 fusion.250
  484.8 9.9 all-to-all-done.8
  510.4 19.8 %shard_map.342 = (bf16[512,512]{1,0:T(8,128)(2,1)S(1)}, bf16[2048,512]{1,0:T(8,128)(2,1)S(1)}, bf16[2048,512]{1,0:T(8,128)(2,1)S(1)}) custom-call(s32[2]{0:T(128)S(1)} %bitcast.512, bf16[512,512]{1,0:T(8,128)(2,1)S(1)} %convolution_convert_fusion.28.query_ref, bf16[2048,1024]{1,0:T(8,128)(2,1)S(1)} %copy-done.7, bf16[2048,1024]{1,0:T(8,128)(2,1)S(1)} %copy-done.7, ...), custom_call_target="tpu_custom_call" | custom-call | flops 2684354560 | bytes 20971520 | tf_op jit(solution)/shard_map/pallas_call | solution.py:188
  557.2 19.8 %shard_map.344 = (bf16[512,512]{1,0:T(8,128)(2,1)S(1)}, bf16[2048,512]{1,0:T(8,128)(2,1)S(1)}, bf16[2048,512]{1,0:T(8,128)(2,1)S(1)}) custom-call(s32[2]{0:T(128)S(1)} %bitcast.513, bf16[512,512]{1,0:T(8,128)(2,1)S(1)} %convolution_convert_fusion.29.query_ref, bf16[2048,1024]{1,0:T(8,128)(2,1)S(1)} %copy-done.5, bf16[2048,1024]{1,0:T(8,128)(2,1)S(1)} %copy-done.5, ...), custom_call_target="tpu_custom_call" | custom-call | flops 2684354560 | bytes 20971520 | tf_op jit(solution)/shard_map/pallas_call | solution.py:188
  610.3 17.6 %fusion.161 = bf16[2048,2048]{1,0:T(8,128)(2,1)} fusion(f32[2048,2048]{1,0:T(8,128)} %fusion.561, bf16[512,2048]{1,0:T(8,128)(2,1)} %get-tuple-element.844, f32[2048,512]{1,0:T(8,128)S(1)} %add_add_fusion.2), kind=kOutput, calls=%fused_computation.250 | convolution fusion | flops 4379901952 | bytes 31457280 | tf_op jit(solution)/shard_map/dot_general | solution.py:52
  627.9 11.4 convolution_convert_fusion.11.refs_7_
  664.5 10.1 convolution_convert_fusion.14.refs_4_
  674.7 20.1 %shard_map.346 = (bf16[2176,32,128]{2,1,0:T(8,128)(2,1)}, bf16[640,32,128]{2,1,0:T(8,128)(2,1)S(1)}) custom-call(s32[2816]{0:T(1024)S(1)} %copy-done.174, bf16[512,2048]{1,0:T(8,128)(2,1)S(1)} %pad_maximum_fusion.3.refs_0_, bf16[512,2048]{1,0:T(8,128)(2,1)S(1)} %pad_maximum_fusion.4.refs_1_, bf16[512,2048]{1,0:T(8,128)(2,1)S(1)} %pad_maximum_fusion.5.refs_2_, ...), custom_call_target="tpu_custom_call" | custom-call | tf_op jit(solution)/shard_map/pallas_call | solution.py:654
  694.8 10.0 multiply_reduce_fusion.1
  707.7 9.0 fusion.188.total_ref
  734.9 34.8 %shard_map.347 = (bf16[2048,512]{1,0:T(8,128)(2,1)S(1)}, bf16[2048,512]{1,0:T(8,128)(2,1)S(1)}, bf16[2048,512]{1,0:T(8,128)(2,1)S(1)}) custom-call(s32[2]{0:T(128)S(1)} %bitcast.514, bf16[2048,1536]{1,0:T(8,128)(2,1)} %copy-done.1, bf16[2048,1536]{1,0:T(8,128)(2,1)} %copy-done.1, bf16[2048,1536]{1,0:T(8,128)(2,1)} %copy-done.1, f32[2048,512]{1,0:T(8,128)S(1)} %copy-done.13, ...), custom_call_target="tpu_custom_call" | custom-call | flops 5368709120 | bytes 16777216 | tf_op jit(solution)/shard_map/pallas_call | solution.py:188
  793.1 34.4 %shard_map.348 = (bf16[2048,512]{1,0:T(8,128)(2,1)S(1)}, bf16[2048,512]{1,0:T(8,128)(2,1)S(1)}, bf16[2048,512]{1,0:T(8,128)(2,1)S(1)}) custom-call(s32[2]{0:T(128)S(1)} %bitcast.515, bf16[2048,1536]{1,0:T(8,128)(2,1)} %copy-done.1, bf16[2048,1536]{1,0:T(8,128)(2,1)} %copy-done.1, ...), custom_call_target="tpu_custom_call", output_to_operand_aliasing={{0}: (6, {}), {1}: (7, {}), {2}: (8, {})} | custom-call | flops 5368709120 | bytes 16777216 | tf_op jit(solution)/shard_map/pallas_call | solution.py:188
  858.1 21.1 %collective-permute-done.18 = bf16[88,32,128]{2,1,0:T(8,128)(2,1)} collective-permute-done((bf16[88,32,128]{2,1,0:T(8,128)(2,1)}, bf16[88,32,128]{2,1,0:T(8,128)(2,1)}, u32[]{:S(2)}, u32[]{:S(2)}) %collective-permute-start.18) | collective-permute-done | bytes 720928 | tf_op jit(solution)/shard_map/ppermute | solution.py:705
  891.6 13.1 %collective-permute-done.21 = bf16[44,32,128]{2,1,0:T(8,128)(2,1)S(1)} collective-permute-done((bf16[44,32,128]{2,1,0:T(8,128)(2,1)S(1)}, bf16[44,32,128]{2,1,0:T(8,128)(2,1)S(1)}, u32[]{:S(2)}, u32[]{:S(2)}) %collective-permute-start.21) | collective-permute-done | bytes 360480 | tf_op jit(solution)/shard_map/ppermute | solution.py:705
  908.2 17.2 %shard_map.349 = bf16[4096,512]{1,0:T(8,128)(2,1)S(1)} custom-call(s32[4096]{0:T(1024)S(1)} %max.34.index_ref, f32[2560,512]{1,0:T(8,128)S(1)} %maximum_multiply_fusion.source_ref), custom_call_target="tpu_custom_call" | custom-call | tf_op jit(solution)/shard_map/pallas_call | solution.py:754
  1068.3 9.4 shard_map.352
  1168.8 27.7 %shard_map.353 = f32[64,64,256]{2,1,0:T(8,128)S(1)} custom-call(f32[64,64,256]{2,1,0:T(8,128)S(1)} %multiply_add_fusion.1.in_ref), custom_call_target="tpu_custom_call" | custom-call | tf_op jit(solution)/shard_map/pallas_call | solution.py:971
  1203.4 22.8 %fusion.564 = (bf16[4096,512]{1,0:T(8,128)(2,1)}, f32[4096,512]{1,0:T(8,128)}, f32[4096,512]{1,0:T(8,128)}, f32[4096,512]{1,0:T(8,128)}) fusion(f32[4096,512]{1,0:T(8,128)} %get-tuple-element.1689, f32[]{:T(128)S(6)} %min.3, bf16[4096,512]{1,0:T(8,128)(2,1)} %all-gather.14.cloned.1.call-done, f32[4096,512]{1,0:T(8,128)} %param.38, f32[4096,512]{1,0:T(8,128)} %param.39), kind=kLoop, calls=%fused_computation.1115 | loop fusion | flops 37748736 | bytes 58720260 | tf_op jit(solution)/shard_map/convert_element_type | solution.py:1398
  (1033 shorter events, 661.8 us)
Async XLA Ops:
  7.2 166.2 %all-gather.8.cloned.1.call-start = ((), (), s32[]{:S(2)}) async-start(), calls=%async_computation.13 | async-start | bytes 11894784 | tf_op jit(solution)/shard_map/all_gather | solution.py:1142
  41.6 24.5 %all-to-all-start.3 = ((s32[32,1,2688]{2,1,0:T(1,128)}), s32[32,1,2688]{2,1,0:T(1,128)S(1)}, u32[]{:S(2)}, u32[]{:S(2)}) async-start(s32[32,1,2688]{2,1,0:T(1,128)} %broadcast_in_dim.474), calls=%async_computation.3 | async-start | bytes 688128 | tf_op jit(solution)/shard_map/all_to_all | solution.py:803
  92.0 81.3 %all-to-all-start.4 = ((bf16[8,336,512]{2,1,0:T(8,128)(2,1)}), bf16[8,336,512]{2,1,0:T(8,128)(2,1)}, u32[]{:S(2)}, u32[]{:S(2)}) async-start(bf16[8,336,512]{2,1,0:T(8,128)(2,1)} %bitcast.58), calls=%async_computation.4 | async-start | bytes 5505024 | tf_op jit(solution)/shard_map/all_to_all | solution.py:883
  196.0 121.1 %all-gather.10.cloned.1.call-start = ((), (), s32[]{:S(2)}) async-start(), calls=%async_computation.14 | async-start | bytes 11894784 | tf_op jit(solution)/shard_map/all_gather | solution.py:1165
  289.7 27.5 %all-to-all-start.5 = ((bf16[8,112,512]{2,1,0:T(8,128)(2,1)}), bf16[8,112,512]{2,1,0:T(8,128)(2,1)S(1)}, u32[]{:S(2)}, u32[]{:S(2)}) async-start(bf16[8,112,512]{2,1,0:T(8,128)(2,1)} %bitcast.67), calls=%async_computation.5 | async-start | bytes 1835008 | tf_op jit(solution)/shard_map/all_to_all | solution.py:883
  422.9 19.5 %all-to-all-start.6 = ((bf16[8,64,512]{2,1,0:T(8,128)(2,1)}), bf16[8,64,512]{2,1,0:T(8,128)(2,1)}, u32[]{:S(2)}, u32[]{:S(2)}) async-start(bf16[8,64,512]{2,1,0:T(8,128)(2,1)} %broadcast_in_dim.494), calls=%async_computation.6 | async-start | bytes 1048576 | tf_op jit(solution)/shard_map/all_to_all | solution.py:803
  451.4 13.8 %all-to-all-start.7 = ((f32[32,3,512]{2,1,0:T(4,128)}), f32[32,3,512]{2,1,0:T(4,128)}, u32[]{:S(2)}, u32[]{:S(2)}) async-start(f32[32,3,512]{2,1,0:T(4,128)} %broadcast_in_dim.496), calls=%async_computation.7 | async-start | bytes 524288 | tf_op jit(solution)/shard_map/all_to_all | solution.py:803
  475.0 19.7 %all-to-all-start.8 = ((bf16[8,64,512]{2,1,0:T(8,128)(2,1)}), bf16[8,64,512]{2,1,0:T(8,128)(2,1)}, u32[]{:S(2)}, u32[]{:S(2)}) async-start(bf16[8,64,512]{2,1,0:T(8,128)(2,1)} %bitcast.608), calls=%async_computation.8 | async-start | bytes 1048576 | tf_op jit(solution)/shard_map/all_to_all | solution.py:1243
  479.3 228.3 %all-gather.12.cloned.1.call-start = ((), (), s32[]{:S(2)}) async-start(), calls=%async_computation.15 | async-start | bytes 2162688 | tf_op jit(solution)/shard_map/all_gather | solution.py:1210
  724.7 45.1 %collective-permute-start.13 = (bf16[1088,32,128]{2,1,0:T(8,128)(2,1)}, bf16[1088,32,128]{2,1,0:T(8,128)(2,1)}, u32[]{:S(2)}, u32[]{:S(2)}) collective-permute-start(bf16[1088,32,128]{2,1,0:T(8,128)(2,1)} %dynamic-slice_bitcast_fusion.13), channel_id=1, source_target_pairs={{0,1},{1,0},{2,3},{3,2},{4,5},{5,4},{6,7},{7,6},{8,9},{9,8},{10,11... | collective-permute-start | bytes 26738696 | tf_op jit(solution)/shard_map/ppermute | solution.py:705
  790.1 38.1 %collective-permute-start.15 = (bf16[176,32,128]{2,1,0:T(8,128)(2,1)}, bf16[176,32,128]{2,1,0:T(8,128)(2,1)S(1)}, u32[]{:S(2)}, u32[]{:S(2)}) collective-permute-start(bf16[176,32,128]{2,1,0:T(8,128)(2,1)} %dynamic-slice_bitcast_fusion.17), channel_id=1, source_target_pairs={{0,16},{1,17},{2,18},{3,19},{4,20},{5,21},{6,22},{7,23},{8,24},{9,... | collective-permute-start | bytes 4325384 | tf_op jit(solution)/shard_map/ppermute | solution.py:705
  790.9 41.4 %collective-permute-start.14 = (bf16[192,32,128]{2,1,0:T(8,128)(2,1)S(1)}, bf16[192,32,128]{2,1,0:T(8,128)(2,1)}, u32[]{:S(2)}, u32[]{:S(2)}) collective-permute-start(bf16[192,32,128]{2,1,0:T(8,128)(2,1)S(1)} %dynamic-slice_bitcast_fusion.15), channel_id=1, source_target_pairs={{0,8},{1,9},{2,10},{3,11},{4,12},{5,13},{6,14},{7,15},{8,0},{9,1},... | collective-permute-start | bytes 4718600 | tf_op jit(solution)/shard_map/ppermute | solution.py:705
  793.1 36.6 %collective-permute-start.16 = (bf16[176,32,128]{2,1,0:T(8,128)(2,1)}, bf16[176,32,128]{2,1,0:T(8,128)(2,1)}, u32[]{:S(2)}, u32[]{:S(2)}) collective-permute-start(bf16[176,32,128]{2,1,0:T(8,128)(2,1)} %dynamic-slice_bitcast_fusion.16), channel_id=1, source_target_pairs={{0,2},{1,3},{2,0},{3,1},{4,6},{5,7},{6,4},{7,5},{8,10},{9,11},{10,... | collective-permute-start | bytes 4325384 | tf_op jit(solution)/shard_map/ppermute | solution.py:705
  845.7 40.3 %collective-permute-start.17 = (bf16[96,32,128]{2,1,0:T(8,128)(2,1)}, bf16[96,32,128]{2,1,0:T(8,128)(2,1)}, u32[]{:S(2)}, u32[]{:S(2)}) collective-permute-start(bf16[96,32,128]{2,1,0:T(8,128)(2,1)} %dynamic-slice_bitcast_fusion.18), channel_id=1, source_target_pairs={{0,16},{1,17},{2,18},{3,19},{4,20},{5,21},{6,22},{7,23},{8,24},{9,... | collective-permute-start | bytes 2359304 | tf_op jit(solution)/shard_map/ppermute | solution.py:705
  847.9 31.3 %collective-permute-start.18 = (bf16[88,32,128]{2,1,0:T(8,128)(2,1)}, bf16[88,32,128]{2,1,0:T(8,128)(2,1)}, u32[]{:S(2)}, u32[]{:S(2)}) collective-permute-start(bf16[88,32,128]{2,1,0:T(8,128)(2,1)} %dynamic-slice_bitcast_fusion.20), channel_id=1, source_target_pairs={{0,2},{1,3},{2,0},{3,1},{4,6},{5,7},{6,4},{7,5},{8,10},{9,11},{10,... | collective-permute-start | bytes 2162696 | tf_op jit(solution)/shard_map/ppermute | solution.py:705
  850.8 33.8 %collective-permute-start.19 = (bf16[88,32,128]{2,1,0:T(8,128)(2,1)}, bf16[88,32,128]{2,1,0:T(8,128)(2,1)}, u32[]{:S(2)}, u32[]{:S(2)}) collective-permute-start(bf16[88,32,128]{2,1,0:T(8,128)(2,1)} %dynamic-slice_bitcast_fusion.19), channel_id=1, source_target_pairs={{0,4},{1,5},{2,6},{3,7},{4,0},{5,1},{6,2},{7,3},{8,12},{9,13},{10,... | collective-permute-start | bytes 2162696 | tf_op jit(solution)/shard_map/ppermute | solution.py:705
  855.9 69.7 %collective-permute-start.26 = (bf16[320,32,128]{2,1,0:T(8,128)(2,1)}, bf16[320,32,128]{2,1,0:T(8,128)(2,1)}, u32[]{:S(2)}, u32[]{:S(2)}) collective-permute-start(bf16[320,32,128]{2,1,0:T(8,128)(2,1)} %dynamic-slice_bitcast_fusion.14), channel_id=1, source_target_pairs={{0,1},{1,0},{2,3},{3,2},{4,5},{5,4},{6,7},{7,6},{8,9},{9,8},{10,11... | collective-permute-start | bytes 7864328 | tf_op jit(solution)/shard_map/ppermute | solution.py:705
  887.4 17.6 %collective-permute-start.20 = (bf16[48,32,128]{2,1,0:T(8,128)(2,1)S(1)}, bf16[48,32,128]{2,1,0:T(8,128)(2,1)S(1)}, u32[]{:S(2)}, u32[]{:S(2)}) collective-permute-start(bf16[48,32,128]{2,1,0:T(8,128)(2,1)S(1)} %dynamic-slice_bitcast_fusion.24), channel_id=1, source_target_pairs={{0,2},{1,3},{2,0},{3,1},{4,6},{5,7},{6,4},{7,5},{8,10},{9,11},{10,... | collective-permute-start | bytes 1179656 | tf_op jit(solution)/shard_map/ppermute | solution.py:705
  887.5 17.3 %collective-permute-start.21 = (bf16[44,32,128]{2,1,0:T(8,128)(2,1)S(1)}, bf16[44,32,128]{2,1,0:T(8,128)(2,1)S(1)}, u32[]{:S(2)}, u32[]{:S(2)}) collective-permute-start(bf16[44,32,128]{2,1,0:T(8,128)(2,1)S(1)} %dynamic-slice_bitcast_fusion.26), channel_id=1, source_target_pairs={{0,4},{1,5},{2,6},{3,7},{4,0},{5,1},{6,2},{7,3},{8,12},{9,13},{10,... | collective-permute-start | bytes 1081352 | tf_op jit(solution)/shard_map/ppermute | solution.py:705
  889.5 15.4 %collective-permute-start.22 = (bf16[44,32,128]{2,1,0:T(8,128)(2,1)S(1)}, bf16[44,32,128]{2,1,0:T(8,128)(2,1)S(1)}, u32[]{:S(2)}, u32[]{:S(2)}) collective-permute-start(bf16[44,32,128]{2,1,0:T(8,128)(2,1)S(1)} %dynamic-slice_bitcast_fusion.25), channel_id=1, source_target_pairs={{0,8},{1,9},{2,10},{3,11},{4,12},{5,13},{6,14},{7,15},{8,0},{9,1},... | collective-permute-start | bytes 1081352 | tf_op jit(solution)/shard_map/ppermute | solution.py:705
  905.2 20.3 %collective-permute-start.25 = (bf16[22,32,128]{2,1,0:T(8,128)(2,1)S(1)}, bf16[22,32,128]{2,1,0:T(8,128)(2,1)S(1)}, u32[]{:S(2)}, u32[]{:S(2)}) collective-permute-start(bf16[22,32,128]{2,1,0:T(8,128)(2,1)S(1)} %dynamic-slice_bitcast_fusion.31), channel_id=1, source_target_pairs={{0,16},{1,17},{2,18},{3,19},{4,20},{5,21},{6,22},{7,23},{8,24},{9,... | collective-permute-start | bytes 540680 | tf_op jit(solution)/shard_map/ppermute | solution.py:705
  906.0 19.5 %collective-permute-start.24 = (bf16[22,32,128]{2,1,0:T(8,128)(2,1)S(1)}, bf16[22,32,128]{2,1,0:T(8,128)(2,1)S(1)}, u32[]{:S(2)}, u32[]{:S(2)}) collective-permute-start(bf16[22,32,128]{2,1,0:T(8,128)(2,1)S(1)} %dynamic-slice_bitcast_fusion.32), channel_id=1, source_target_pairs={{0,8},{1,9},{2,10},{3,11},{4,12},{5,13},{6,14},{7,15},{8,0},{9,1},... | collective-permute-start | bytes 540680 | tf_op jit(solution)/shard_map/ppermute | solution.py:705
  907.3 22.5 %collective-permute-start.23 = (bf16[24,32,128]{2,1,0:T(8,128)(2,1)S(1)}, bf16[24,32,128]{2,1,0:T(8,128)(2,1)S(1)}, u32[]{:S(2)}, u32[]{:S(2)}) collective-permute-start(bf16[24,32,128]{2,1,0:T(8,128)(2,1)S(1)} %dynamic-slice_bitcast_fusion.30), channel_id=1, source_target_pairs={{0,4},{1,5},{2,6},{3,7},{4,0},{5,1},{6,2},{7,3},{8,12},{9,13},{10,... | collective-permute-start | bytes 589832 | tf_op jit(solution)/shard_map/ppermute | solution.py:705
  929.7 9.6 collective-permute-start.35
  931.1 10.7 collective-permute-start.31
  932.9 10.3 collective-permute-start.27
  939.5 10.2 collective-permute-start.36
  943.4 14.7 %collective-permute-start.28 = (bf16[32,32,128]{2,1,0:T(8,128)(2,1)S(1)}, bf16[32,32,128]{2,1,0:T(8,128)(2,1)S(1)}, u32[]{:S(2)}, u32[]{:S(2)}) collective-permute-start(bf16[32,32,128]{2,1,0:T(8,128)(2,1)S(1)} %dynamic-slice_bitcast_fusion.27), channel_id=1, source_target_pairs={{0,16},{1,17},{2,18},{3,19},{4,20},{5,21},{6,22},{7,23},{8,24},{9,... | collective-permute-start | bytes 786440 | tf_op jit(solution)/shard_map/ppermute | solution.py:705
  969.5 98.8 %all-to-all-start.9 = ((bf16[32,128,512]{2,1,0:T(8,128)(2,1)}), bf16[32,128,512]{2,1,0:T(8,128)(2,1)}, u32[]{:S(2)}, u32[]{:S(2)}) async-start(bf16[32,128,512]{2,1,0:T(8,128)(2,1)} %bitcast.505), calls=%async_computation.9 | async-start | bytes 8388608 | tf_op jit(solution)/shard_map/all_to_all | solution.py:915
  973.2 230.2 %all-gather.14.cloned.1.call-start = ((), (), s32[]{:S(2)}) async-start(), calls=%async_computation.16 | async-start | bytes 5242880 | tf_op jit(solution)/shard_map/all_gather | solution.py:1359
  1083.0 12.7 %all-to-all-start.10 = ((f32[32,1,256]{2,1,0:T(1,128)}), f32[32,1,256]{2,1,0:T(1,128)S(1)}, u32[]{:S(2)}, u32[]{:S(2)}) async-start(f32[32,1,256]{2,1,0:T(1,128)} %all_to_all.95), calls=%async_computation.10 | async-start | bytes 65536 | tf_op jit(solution)/shard_map/all_to_all | solution.py:1351
  1096.4 13.2 %all-to-all-start.11 = ((f32[32,3,128]{2,1,0:T(4,128)}), f32[32,3,128]{2,1,0:T(4,128)S(1)}, u32[]{:S(2)}, u32[]{:S(2)}) async-start(f32[32,3,128]{2,1,0:T(4,128)} %broadcast_in_dim.512), calls=%async_computation.11 | async-start | bytes 131072 | tf_op jit(solution)/shard_map/all_to_all | solution.py:803
  (267 other events, 2153.3 us)
Sparse Core Ops, SparseCore 0:
  20.6 108.9 all-gather.7
  200.3 90.2 all-gather.9
  484.3 56.0 all-gather.11
  1082.4 51.1 all-gather.13

commit v7 on v6

--- a/solution.py
+++ b/solution.py
@@ -101,8 +101,9 @@
             summit = jnp.max(scores, axis=1, keepdims=True)
             expo = jnp.exp(scores - summit)
             sums = jnp.sum(expo, axis=1, keepdims=True)
-            probs = (expo * (1.0 / sums)).astype(jnp.bfloat16)
-            total += jnp.dot(probs, values[head], preferred_element_type=jnp.float32)
+            total += jnp.dot(
+                expo.astype(jnp.bfloat16), values[head], preferred_element_type=jnp.float32
+            ) * (1.0 / sums)
             stats.append(summit + jnp.log(sums))
         out_ref[...] = total.astype(jnp.bfloat16)
         first = lax.broadcasted_iota(jnp.int32, (block, PAIR), 1) < HEAD_DIM
@@ -733,22 +734,23 @@
 
 
 def take_rows(source, index_at, kind):
-    count, width, block = (index_at.shape[0], source.shape[1], 128)
-    whole = -(-count // block) * block
+    count, width, unroll = (index_at.shape[0], source.shape[1], 32)
+    whole = -(-count // 128) * 128
+    block = max(size for size in range(128, 1025, 128) if whole % size == 0)
     index_at = jnp.pad(index_at, (0, whole - count))
 
     def kernel(index_ref, source_ref, out_ref, held_ref):
         first = pl.program_id(0) * block
 
-        def copy_eight(group, carry):
-            base = pl.multiple_of(group * 8, 8)
-            for row_no in range(8):
+        def copy_some(group, carry):
+            base = pl.multiple_of(group * unroll, unroll)
+            for row_no in range(unroll):
                 held_ref[pl.ds(base + row_no, 1), :] = source_ref[
                     pl.ds(index_ref[first + base + row_no], 1), :
                 ]
             return carry
 
-        lax.fori_loop(0, block // 8, copy_eight, 0)
+        lax.fori_loop(0, block // unroll, copy_some, 0)
         out_ref[...] = held_ref[...].astype(kind)
 
     taken = pl.pallas_call(

time: 1250 us -> 1220 us (0.976)
  Pallas kernels: 368 us -> 355 us
  transfers between devices with their start and end apart: 39 -> 39, of which waited for: 20 -> 20; matrix products, arithmetic and copies ran while one was open for 34% -> 35% of each run, Pallas kernels for 23% -> 22%
where the time goes in v7:
time: 1220 us
  Pallas kernels  355 us (29%)
  matrix products  256 us (21%)
  local copies, waits for them, and re-layouts  204 us (17%)
  waiting for transfers between devices  162 us (13%)
  other arithmetic  150 us (12%)
  starting transfers between devices  61.7 us (5%)
  between operations  25.2 us (2%)
    pallas_call x6, Pallas kernels, attend_backward(): pl.pallas_call(kernel, out_shape=(jax.ShapeDtypeStruct((MICRO * rows, D),...  123 us
    unnamed x547, local copies, waits for them, and re-layouts  114 us
    pallas_call x5, Pallas kernels, attend_forward(): pl.pallas_call(kernel, out_shape=(jax.ShapeDtypeStruct((MICRO * rows, D),...  76.8 us
    dot_general x19, matrix products, linear(): return jnp.dot(left_op, right_op, preferred_element_type=jnp.float32)  73.4 us
    dot_general x23, matrix products, outer_sum(): lax.dot_general(left_op, right_op, (((0,), (0,)), ((), ())), preferred_el...  68.2 us
    ppermute x26, waiting for transfers between devices, halve(): arrived = lax.ppermute(sent, ('dp', 'vocab'), pairs)  65.8 us
    dot_general x19, matrix products, linear_tr(): lax.dot_general(left_op, right_op, (((1,), (1,)), ((), ())), preferred_el...  59.2 us
    pallas_call x5, Pallas kernels, take_rows(): pl.pallas_call(kernel, out_shape=jax.ShapeDtypeStruct((whole, width), kin...  51.5 us
  transfers between devices with their start and end apart: 39, of which 20 were waited for; matrix products, arithmetic and copies ran while one was open for 35% of the time, Pallas kernels for 22%

profile of v7, /device:TPU:0, one launch (start us, length us, event | category | flops | bytes accessed | tf_op | source)
XLA Modules:
  0.0 1215.0 jit_solution(7350897518555144209)
XLA Ops:
  49.4 18.3 %all-to-all-done.3 = s32[32,1,2688]{2,1,0:T(1,128)S(1)} async-done(((s32[32,1,2688]{2,1,0:T(1,128)}), s32[32,1,2688]{2,1,0:T(1,128)S(1)}, u32[]{:S(2)}, u32[]{:S(2)}) %all-to-all-start.3) | async-done | bytes 344096 | tf_op jit(solution)/shard_map/all_to_all | solution.py:805
  72.6 14.9 %shard_map.332 = bf16[2688,512]{1,0:T(8,128)(2,1)} custom-call(s32[2688]{0:T(1024)S(1)} %max.32.index_ref, f32[4096,512]{1,0:T(8,128)} %source_ref.3), custom_call_target="tpu_custom_call" | custom-call | tf_op jit(solution)/shard_map/pallas_call | solution.py:756
  118.1 8.2 shard_map.333
  138.0 36.0 %all-to-all-done.4 = bf16[8,336,512]{2,1,0:T(8,128)(2,1)} async-done(((bf16[8,336,512]{2,1,0:T(8,128)(2,1)}), bf16[8,336,512]{2,1,0:T(8,128)(2,1)}, u32[]{:S(2)}, u32[]{:S(2)}) %all-to-all-start.4) | async-done | bytes 2752544 | tf_op jit(solution)/shard_map/all_to_all | solution.py:885
  174.0 13.2 %conditional.2 = (bf16[512,2048]{1,0:T(8,128)(2,1)}, bf16[512,2048]{1,0:T(8,128)(2,1)S(1)}, bf16[512,2048]{1,0:T(8,128)(2,1)S(1)}, bf16[512,2048]{1,0:T(8,128)(2,1)}, bf16[512,2048]{1,0:T(8,128)(2,1)}) conditional(s32[]{:T(128)} %convert_element_type.1091, (s32[2816]{0:T(1024)S(1)}, bf16[1408,32,128]{2,1,0:T(8,128)(2,1)}) %tuple.99, ...), branch_computations={%region_26.27_spmd, %region_27.28_spmd} | conditional | bytes 90210416 | solution.py:1178
  174.0 10.0 branch_0_fun.1
  198.3 9.6 shard_map.334
  218.9 40.1 %shard_map.335 = (bf16[2048,512]{1,0:T(8,128)(2,1)S(1)}, f32[2048,512]{1,0:T(8,128)S(1)}) custom-call(s32[2]{0:T(128)S(1)} %bitcast.509, bf16[2048,1536]{1,0:T(8,128)(2,1)S(1)} %convolution_convert_fusion.query_ref.key_ref.value_ref, bf16[2048,1536]{1,0:T(8,128)(2,1)S(1)} %convolution_convert_fusion.query_ref.key_ref.value_ref, ...), custom_call_target="tpu_custom_call" | custom-call | flops 4294967296 | bytes 16777216 | tf_op jit(solution)/shard_map/pallas_call | solution.py:113
  261.7 11.3 fusion.561
  277.0 11.1 multiply_reduce_fusion.6
  291.9 8.8 all-to-all-done.5
  301.0 20.1 %shard_map.337 = (bf16[512,2048]{1,0:T(8,128)(2,1)S(1)}, bf16[512,2048]{1,0:T(8,128)(2,1)S(1)}, bf16[512,2048]{1,0:T(8,128)(2,1)S(1)}, bf16[512,2048]{1,0:T(8,12...) custom-call(s32[2816]{0:T(1024)S(1)} %reshape.1993.place_ref, ...), custom_call_target="tpu_custom_call" | custom-call | tf_op jit(solution)/shard_map/pallas_call | solution.py:574
  348.4 11.2 shard_map.339
  378.9 11.6 shard_map.341
  449.5 8.0 fusion.250
  467.0 10.1 all-to-all-done.8
  493.0 19.8 %shard_map.342 = (bf16[512,512]{1,0:T(8,128)(2,1)S(1)}, bf16[2048,512]{1,0:T(8,128)(2,1)S(1)}, bf16[2048,512]{1,0:T(8,128)(2,1)S(1)}) custom-call(s32[2]{0:T(128)S(1)} %bitcast.512, bf16[512,512]{1,0:T(8,128)(2,1)S(1)} %convolution_convert_fusion.28.query_ref, bf16[2048,1024]{1,0:T(8,128)(2,1)S(1)} %copy-done.7, bf16[2048,1024]{1,0:T(8,128)(2,1)S(1)} %copy-done.7, ...), custom_call_target="tpu_custom_call" | custom-call | flops 2684354560 | bytes 20971520 | tf_op jit(solution)/shard_map/pallas_call | solution.py:189
  539.9 19.8 %shard_map.344 = (bf16[512,512]{1,0:T(8,128)(2,1)S(1)}, bf16[2048,512]{1,0:T(8,128)(2,1)S(1)}, bf16[2048,512]{1,0:T(8,128)(2,1)S(1)}) custom-call(s32[2]{0:T(128)S(1)} %bitcast.513, bf16[512,512]{1,0:T(8,128)(2,1)S(1)} %convolution_convert_fusion.29.query_ref, bf16[2048,1024]{1,0:T(8,128)(2,1)S(1)} %copy-done.5, bf16[2048,1024]{1,0:T(8,128)(2,1)S(1)} %copy-done.5, ...), custom_call_target="tpu_custom_call" | custom-call | flops 2684354560 | bytes 20971520 | tf_op jit(solution)/shard_map/pallas_call | solution.py:189
  592.9 17.6 %fusion.161 = bf16[2048,2048]{1,0:T(8,128)(2,1)} fusion(f32[2048,2048]{1,0:T(8,128)} %fusion.561, bf16[512,2048]{1,0:T(8,128)(2,1)} %get-tuple-element.844, f32[2048,512]{1,0:T(8,128)S(1)} %add_add_fusion.2), kind=kOutput, calls=%fused_computation.250 | convolution fusion | flops 4379901952 | bytes 31457280 | tf_op jit(solution)/shard_map/dot_general | solution.py:52
  610.4 11.4 convolution_convert_fusion.11.refs_7_
  647.1 10.1 convolution_convert_fusion.14.refs_4_
  657.3 20.1 %shard_map.346 = (bf16[2176,32,128]{2,1,0:T(8,128)(2,1)}, bf16[640,32,128]{2,1,0:T(8,128)(2,1)S(1)}) custom-call(s32[2816]{0:T(1024)S(1)} %copy-done.174, bf16[512,2048]{1,0:T(8,128)(2,1)S(1)} %pad_maximum_fusion.3.refs_0_, bf16[512,2048]{1,0:T(8,128)(2,1)S(1)} %pad_maximum_fusion.4.refs_1_, bf16[512,2048]{1,0:T(8,128)(2,1)S(1)} %pad_maximum_fusion.5.refs_2_, ...), custom_call_target="tpu_custom_call" | custom-call | tf_op jit(solution)/shard_map/pallas_call | solution.py:655
  677.4 10.0 multiply_reduce_fusion.1
  690.4 9.0 fusion.188.total_ref
  717.7 34.5 %shard_map.347 = (bf16[2048,512]{1,0:T(8,128)(2,1)S(1)}, bf16[2048,512]{1,0:T(8,128)(2,1)S(1)}, bf16[2048,512]{1,0:T(8,128)(2,1)S(1)}) custom-call(s32[2]{0:T(128)S(1)} %bitcast.514, bf16[2048,1536]{1,0:T(8,128)(2,1)} %copy-done.1, bf16[2048,1536]{1,0:T(8,128)(2,1)} %copy-done.1, bf16[2048,1536]{1,0:T(8,128)(2,1)} %copy-done.1, f32[2048,512]{1,0:T(8,128)S(1)} %copy-done.13, ...), custom_call_target="tpu_custom_call" | custom-call | flops 5368709120 | bytes 16777216 | tf_op jit(solution)/shard_map/pallas_call | solution.py:189
  775.6 34.4 %shard_map.348 = (bf16[2048,512]{1,0:T(8,128)(2,1)S(1)}, bf16[2048,512]{1,0:T(8,128)(2,1)S(1)}, bf16[2048,512]{1,0:T(8,128)(2,1)S(1)}) custom-call(s32[2]{0:T(128)S(1)} %bitcast.515, bf16[2048,1536]{1,0:T(8,128)(2,1)} %copy-done.1, bf16[2048,1536]{1,0:T(8,128)(2,1)} %copy-done.1, ...), custom_call_target="tpu_custom_call", output_to_operand_aliasing={{0}: (6, {}), {1}: (7, {}), {2}: (8, {})} | custom-call | flops 5368709120 | bytes 16777216 | tf_op jit(solution)/shard_map/pallas_call | solution.py:189
  840.7 21.1 %collective-permute-done.18 = bf16[88,32,128]{2,1,0:T(8,128)(2,1)} collective-permute-done((bf16[88,32,128]{2,1,0:T(8,128)(2,1)}, bf16[88,32,128]{2,1,0:T(8,128)(2,1)}, u32[]{:S(2)}, u32[]{:S(2)}) %collective-permute-start.18) | collective-permute-done | bytes 720928 | tf_op jit(solution)/shard_map/ppermute | solution.py:706
  874.3 13.1 %collective-permute-done.21 = bf16[44,32,128]{2,1,0:T(8,128)(2,1)S(1)} collective-permute-done((bf16[44,32,128]{2,1,0:T(8,128)(2,1)S(1)}, bf16[44,32,128]{2,1,0:T(8,128)(2,1)S(1)}, u32[]{:S(2)}, u32[]{:S(2)}) %collective-permute-start.21) | collective-permute-done | bytes 360480 | tf_op jit(solution)/shard_map/ppermute | solution.py:706
  890.8 15.6 %shard_map.349 = bf16[4096,512]{1,0:T(8,128)(2,1)S(1)} custom-call(s32[4096]{0:T(1024)S(1)} %max.34.index_ref, f32[2560,512]{1,0:T(8,128)S(1)} %maximum_multiply_fusion.source_ref), custom_call_target="tpu_custom_call" | custom-call | tf_op jit(solution)/shard_map/pallas_call | solution.py:756
  1049.3 9.4 shard_map.352
  1149.8 27.7 %shard_map.353 = f32[64,64,256]{2,1,0:T(8,128)S(1)} custom-call(f32[64,64,256]{2,1,0:T(8,128)S(1)} %multiply_add_fusion.1.in_ref), custom_call_target="tpu_custom_call" | custom-call | tf_op jit(solution)/shard_map/pallas_call | solution.py:973
  1184.3 22.8 %fusion.564 = (bf16[4096,512]{1,0:T(8,128)(2,1)}, f32[4096,512]{1,0:T(8,128)}, f32[4096,512]{1,0:T(8,128)}, f32[4096,512]{1,0:T(8,128)}) fusion(f32[4096,512]{1,0:T(8,128)} %get-tuple-element.1689, f32[]{:T(128)S(6)} %min.3, bf16[4096,512]{1,0:T(8,128)(2,1)} %all-gather.14.cloned.1.call-done, f32[4096,512]{1,0:T(8,128)} %param.38, f32[4096,512]{1,0:T(8,128)} %param.39), kind=kLoop, calls=%fused_computation.1115 | loop fusion | flops 37748736 | bytes 58720260 | tf_op jit(solution)/shard_map/convert_element_type | solution.py:1400
  (1033 shorter events, 664.0 us)
Async XLA Ops:
  7.2 166.8 %all-gather.8.cloned.1.call-start = ((), (), s32[]{:S(2)}) async-start(), calls=%async_computation.13 | async-start | bytes 11894784 | tf_op jit(solution)/shard_map/all_gather | solution.py:1144
  41.6 26.1 %all-to-all-start.3 = ((s32[32,1,2688]{2,1,0:T(1,128)}), s32[32,1,2688]{2,1,0:T(1,128)S(1)}, u32[]{:S(2)}, u32[]{:S(2)}) async-start(s32[32,1,2688]{2,1,0:T(1,128)} %broadcast_in_dim.474), calls=%async_computation.3 | async-start | bytes 688128 | tf_op jit(solution)/shard_map/all_to_all | solution.py:805
  92.0 82.0 %all-to-all-start.4 = ((bf16[8,336,512]{2,1,0:T(8,128)(2,1)}), bf16[8,336,512]{2,1,0:T(8,128)(2,1)}, u32[]{:S(2)}, u32[]{:S(2)}) async-start(bf16[8,336,512]{2,1,0:T(8,128)(2,1)} %bitcast.58), calls=%async_computation.4 | async-start | bytes 5505024 | tf_op jit(solution)/shard_map/all_to_all | solution.py:885
  187.2 113.5 %all-gather.10.cloned.1.call-start = ((), (), s32[]{:S(2)}) async-start(), calls=%async_computation.14 | async-start | bytes 11894784 | tf_op jit(solution)/shard_map/all_gather | solution.py:1167
  273.0 27.7 %all-to-all-start.5 = ((bf16[8,112,512]{2,1,0:T(8,128)(2,1)}), bf16[8,112,512]{2,1,0:T(8,128)(2,1)S(1)}, u32[]{:S(2)}, u32[]{:S(2)}) async-start(bf16[8,112,512]{2,1,0:T(8,128)(2,1)} %bitcast.67), calls=%async_computation.5 | async-start | bytes 1835008 | tf_op jit(solution)/shard_map/all_to_all | solution.py:885
  405.2 19.5 %all-to-all-start.6 = ((bf16[8,64,512]{2,1,0:T(8,128)(2,1)}), bf16[8,64,512]{2,1,0:T(8,128)(2,1)}, u32[]{:S(2)}, u32[]{:S(2)}) async-start(bf16[8,64,512]{2,1,0:T(8,128)(2,1)} %broadcast_in_dim.494), calls=%async_computation.6 | async-start | bytes 1048576 | tf_op jit(solution)/shard_map/all_to_all | solution.py:805
  433.7 14.0 %all-to-all-start.7 = ((f32[32,3,512]{2,1,0:T(4,128)}), f32[32,3,512]{2,1,0:T(4,128)}, u32[]{:S(2)}, u32[]{:S(2)}) async-start(f32[32,3,512]{2,1,0:T(4,128)} %broadcast_in_dim.496), calls=%async_computation.7 | async-start | bytes 524288 | tf_op jit(solution)/shard_map/all_to_all | solution.py:805
  457.5 19.7 %all-to-all-start.8 = ((bf16[8,64,512]{2,1,0:T(8,128)(2,1)}), bf16[8,64,512]{2,1,0:T(8,128)(2,1)}, u32[]{:S(2)}, u32[]{:S(2)}) async-start(bf16[8,64,512]{2,1,0:T(8,128)(2,1)} %bitcast.608), calls=%async_computation.8 | async-start | bytes 1048576 | tf_op jit(solution)/shard_map/all_to_all | solution.py:1245
  461.8 228.6 %all-gather.12.cloned.1.call-start = ((), (), s32[]{:S(2)}) async-start(), calls=%async_computation.15 | async-start | bytes 2162688 | tf_op jit(solution)/shard_map/all_gather | solution.py:1212
  707.4 44.8 %collective-permute-start.13 = (bf16[1088,32,128]{2,1,0:T(8,128)(2,1)}, bf16[1088,32,128]{2,1,0:T(8,128)(2,1)}, u32[]{:S(2)}, u32[]{:S(2)}) collective-permute-start(bf16[1088,32,128]{2,1,0:T(8,128)(2,1)} %dynamic-slice_bitcast_fusion.13), channel_id=1, source_target_pairs={{0,1},{1,0},{2,3},{3,2},{4,5},{5,4},{6,7},{7,6},{8,9},{9,8},{10,11... | collective-permute-start | bytes 26738696 | tf_op jit(solution)/shard_map/ppermute | solution.py:706
  772.7 38.3 %collective-permute-start.15 = (bf16[176,32,128]{2,1,0:T(8,128)(2,1)}, bf16[176,32,128]{2,1,0:T(8,128)(2,1)S(1)}, u32[]{:S(2)}, u32[]{:S(2)}) collective-permute-start(bf16[176,32,128]{2,1,0:T(8,128)(2,1)} %dynamic-slice_bitcast_fusion.17), channel_id=1, source_target_pairs={{0,16},{1,17},{2,18},{3,19},{4,20},{5,21},{6,22},{7,23},{8,24},{9,... | collective-permute-start | bytes 4325384 | tf_op jit(solution)/shard_map/ppermute | solution.py:706
  773.4 41.5 %collective-permute-start.14 = (bf16[192,32,128]{2,1,0:T(8,128)(2,1)S(1)}, bf16[192,32,128]{2,1,0:T(8,128)(2,1)}, u32[]{:S(2)}, u32[]{:S(2)}) collective-permute-start(bf16[192,32,128]{2,1,0:T(8,128)(2,1)S(1)} %dynamic-slice_bitcast_fusion.15), channel_id=1, source_target_pairs={{0,8},{1,9},{2,10},{3,11},{4,12},{5,13},{6,14},{7,15},{8,0},{9,1},... | collective-permute-start | bytes 4718600 | tf_op jit(solution)/shard_map/ppermute | solution.py:706
  775.6 36.6 %collective-permute-start.16 = (bf16[176,32,128]{2,1,0:T(8,128)(2,1)}, bf16[176,32,128]{2,1,0:T(8,128)(2,1)}, u32[]{:S(2)}, u32[]{:S(2)}) collective-permute-start(bf16[176,32,128]{2,1,0:T(8,128)(2,1)} %dynamic-slice_bitcast_fusion.16), channel_id=1, source_target_pairs={{0,2},{1,3},{2,0},{3,1},{4,6},{5,7},{6,4},{7,5},{8,10},{9,11},{10,... | collective-permute-start | bytes 4325384 | tf_op jit(solution)/shard_map/ppermute | solution.py:706
  828.3 40.3 %collective-permute-start.17 = (bf16[96,32,128]{2,1,0:T(8,128)(2,1)}, bf16[96,32,128]{2,1,0:T(8,128)(2,1)}, u32[]{:S(2)}, u32[]{:S(2)}) collective-permute-start(bf16[96,32,128]{2,1,0:T(8,128)(2,1)} %dynamic-slice_bitcast_fusion.18), channel_id=1, source_target_pairs={{0,16},{1,17},{2,18},{3,19},{4,20},{5,21},{6,22},{7,23},{8,24},{9,... | collective-permute-start | bytes 2359304 | tf_op jit(solution)/shard_map/ppermute | solution.py:706
  830.5 31.3 %collective-permute-start.18 = (bf16[88,32,128]{2,1,0:T(8,128)(2,1)}, bf16[88,32,128]{2,1,0:T(8,128)(2,1)}, u32[]{:S(2)}, u32[]{:S(2)}) collective-permute-start(bf16[88,32,128]{2,1,0:T(8,128)(2,1)} %dynamic-slice_bitcast_fusion.20), channel_id=1, source_target_pairs={{0,2},{1,3},{2,0},{3,1},{4,6},{5,7},{6,4},{7,5},{8,10},{9,11},{10,... | collective-permute-start | bytes 2162696 | tf_op jit(solution)/shard_map/ppermute | solution.py:706
  833.5 33.8 %collective-permute-start.19 = (bf16[88,32,128]{2,1,0:T(8,128)(2,1)}, bf16[88,32,128]{2,1,0:T(8,128)(2,1)}, u32[]{:S(2)}, u32[]{:S(2)}) collective-permute-start(bf16[88,32,128]{2,1,0:T(8,128)(2,1)} %dynamic-slice_bitcast_fusion.19), channel_id=1, source_target_pairs={{0,4},{1,5},{2,6},{3,7},{4,0},{5,1},{6,2},{7,3},{8,12},{9,13},{10,... | collective-permute-start | bytes 2162696 | tf_op jit(solution)/shard_map/ppermute | solution.py:706
  838.5 68.1 %collective-permute-start.26 = (bf16[320,32,128]{2,1,0:T(8,128)(2,1)}, bf16[320,32,128]{2,1,0:T(8,128)(2,1)}, u32[]{:S(2)}, u32[]{:S(2)}) collective-permute-start(bf16[320,32,128]{2,1,0:T(8,128)(2,1)} %dynamic-slice_bitcast_fusion.14), channel_id=1, source_target_pairs={{0,1},{1,0},{2,3},{3,2},{4,5},{5,4},{6,7},{7,6},{8,9},{9,8},{10,11... | collective-permute-start | bytes 7864328 | tf_op jit(solution)/shard_map/ppermute | solution.py:706
  870.0 17.6 %collective-permute-start.20 = (bf16[48,32,128]{2,1,0:T(8,128)(2,1)S(1)}, bf16[48,32,128]{2,1,0:T(8,128)(2,1)S(1)}, u32[]{:S(2)}, u32[]{:S(2)}) collective-permute-start(bf16[48,32,128]{2,1,0:T(8,128)(2,1)S(1)} %dynamic-slice_bitcast_fusion.24), channel_id=1, source_target_pairs={{0,2},{1,3},{2,0},{3,1},{4,6},{5,7},{6,4},{7,5},{8,10},{9,11},{10,... | collective-permute-start | bytes 1179656 | tf_op jit(solution)/shard_map/ppermute | solution.py:706
  870.1 17.3 %collective-permute-start.21 = (bf16[44,32,128]{2,1,0:T(8,128)(2,1)S(1)}, bf16[44,32,128]{2,1,0:T(8,128)(2,1)S(1)}, u32[]{:S(2)}, u32[]{:S(2)}) collective-permute-start(bf16[44,32,128]{2,1,0:T(8,128)(2,1)S(1)} %dynamic-slice_bitcast_fusion.26), channel_id=1, source_target_pairs={{0,4},{1,5},{2,6},{3,7},{4,0},{5,1},{6,2},{7,3},{8,12},{9,13},{10,... | collective-permute-start | bytes 1081352 | tf_op jit(solution)/shard_map/ppermute | solution.py:706
  872.1 15.4 %collective-permute-start.22 = (bf16[44,32,128]{2,1,0:T(8,128)(2,1)S(1)}, bf16[44,32,128]{2,1,0:T(8,128)(2,1)S(1)}, u32[]{:S(2)}, u32[]{:S(2)}) collective-permute-start(bf16[44,32,128]{2,1,0:T(8,128)(2,1)S(1)} %dynamic-slice_bitcast_fusion.25), channel_id=1, source_target_pairs={{0,8},{1,9},{2,10},{3,11},{4,12},{5,13},{6,14},{7,15},{8,0},{9,1},... | collective-permute-start | bytes 1081352 | tf_op jit(solution)/shard_map/ppermute | solution.py:706
  887.8 18.7 %collective-permute-start.25 = (bf16[22,32,128]{2,1,0:T(8,128)(2,1)S(1)}, bf16[22,32,128]{2,1,0:T(8,128)(2,1)S(1)}, u32[]{:S(2)}, u32[]{:S(2)}) collective-permute-start(bf16[22,32,128]{2,1,0:T(8,128)(2,1)S(1)} %dynamic-slice_bitcast_fusion.31), channel_id=1, source_target_pairs={{0,16},{1,17},{2,18},{3,19},{4,20},{5,21},{6,22},{7,23},{8,24},{9,... | collective-permute-start | bytes 540680 | tf_op jit(solution)/shard_map/ppermute | solution.py:706
  888.6 17.9 %collective-permute-start.24 = (bf16[22,32,128]{2,1,0:T(8,128)(2,1)S(1)}, bf16[22,32,128]{2,1,0:T(8,128)(2,1)S(1)}, u32[]{:S(2)}, u32[]{:S(2)}) collective-permute-start(bf16[22,32,128]{2,1,0:T(8,128)(2,1)S(1)} %dynamic-slice_bitcast_fusion.32), channel_id=1, source_target_pairs={{0,8},{1,9},{2,10},{3,11},{4,12},{5,13},{6,14},{7,15},{8,0},{9,1},... | collective-permute-start | bytes 540680 | tf_op jit(solution)/shard_map/ppermute | solution.py:706
  890.0 20.9 %collective-permute-start.23 = (bf16[24,32,128]{2,1,0:T(8,128)(2,1)S(1)}, bf16[24,32,128]{2,1,0:T(8,128)(2,1)S(1)}, u32[]{:S(2)}, u32[]{:S(2)}) collective-permute-start(bf16[24,32,128]{2,1,0:T(8,128)(2,1)S(1)} %dynamic-slice_bitcast_fusion.30), channel_id=1, source_target_pairs={{0,4},{1,5},{2,6},{3,7},{4,0},{5,1},{6,2},{7,3},{8,12},{9,13},{10,... | collective-permute-start | bytes 589832 | tf_op jit(solution)/shard_map/ppermute | solution.py:706
  910.8 9.6 collective-permute-start.35
  912.2 10.7 collective-permute-start.31
  913.9 10.3 collective-permute-start.27
  920.5 10.2 collective-permute-start.36
  924.4 14.8 %collective-permute-start.28 = (bf16[32,32,128]{2,1,0:T(8,128)(2,1)S(1)}, bf16[32,32,128]{2,1,0:T(8,128)(2,1)S(1)}, u32[]{:S(2)}, u32[]{:S(2)}) collective-permute-start(bf16[32,32,128]{2,1,0:T(8,128)(2,1)S(1)} %dynamic-slice_bitcast_fusion.27), channel_id=1, source_target_pairs={{0,16},{1,17},{2,18},{3,19},{4,20},{5,21},{6,22},{7,23},{8,24},{9,... | collective-permute-start | bytes 786440 | tf_op jit(solution)/shard_map/ppermute | solution.py:706
  950.5 98.8 %all-to-all-start.9 = ((bf16[32,128,512]{2,1,0:T(8,128)(2,1)}), bf16[32,128,512]{2,1,0:T(8,128)(2,1)}, u32[]{:S(2)}, u32[]{:S(2)}) async-start(bf16[32,128,512]{2,1,0:T(8,128)(2,1)} %bitcast.505), calls=%async_computation.9 | async-start | bytes 8388608 | tf_op jit(solution)/shard_map/all_to_all | solution.py:917
  954.2 230.1 %all-gather.14.cloned.1.call-start = ((), (), s32[]{:S(2)}) async-start(), calls=%async_computation.16 | async-start | bytes 5242880 | tf_op jit(solution)/shard_map/all_gather | solution.py:1361
  1063.8 12.5 %all-to-all-start.10 = ((f32[32,1,256]{2,1,0:T(1,128)}), f32[32,1,256]{2,1,0:T(1,128)S(1)}, u32[]{:S(2)}, u32[]{:S(2)}) async-start(f32[32,1,256]{2,1,0:T(1,128)} %all_to_all.95), calls=%async_computation.10 | async-start | bytes 65536 | tf_op jit(solution)/shard_map/all_to_all | solution.py:1353
  1077.0 13.6 %all-to-all-start.11 = ((f32[32,3,128]{2,1,0:T(4,128)}), f32[32,3,128]{2,1,0:T(4,128)S(1)}, u32[]{:S(2)}, u32[]{:S(2)}) async-start(f32[32,3,128]{2,1,0:T(4,128)} %broadcast_in_dim.512), calls=%async_computation.11 | async-start | bytes 131072 | tf_op jit(solution)/shard_map/all_to_all | solution.py:805
  (267 other events, 2076.4 us)
Sparse Core Ops, SparseCore 0:
  20.6 110.2 all-gather.7
  191.4 90.2 all-gather.9
  466.6 56.0 all-gather.11
  1063.3 50.8 all-gather.13
